TPU v7x, 128 devices: a whole 4x4x4 slice. The times are simulated.
128 devices in a mesh: dp: 8 (over y, core), row: 4 (over x), col: 4 (over z).
Axes of the slice: x: 4, y: 4, z: 4, core: 2. Of those that a mesh axis runs over, the one named last changes fastest.
Arguments:
- tokens: bfloat16 [16384, 2048], P(('dp', 'col'), 'row'), may hold values from -6 to 6
- positions: int32 [8, 2048], P('dp', 'row'), may hold values from 0 to 2047, each once within a row
- routes: int32 [16384, 4], P(('dp', 'col')), may hold values from 0 to 63, all different within a row; in each aligned block of 512 rows (0 to 511, 512 to 1023, ...) at most 36 rows name the same one
- attention_norm_gain: float32 [2048], P('row'), may hold values from 0.1 to 1.9
- experts_norm_gain: float32 [2048], P('row'), may hold values from 0.1 to 1.9
- w_qkv: bfloat16 [2048, 16, 384], P('row', 'col'), may hold values from -0.125 to 0.125
- q_gain: float32 [128], replicated, may hold values from 0.1 to 1.9
- k_gain: float32 [128], replicated, may hold values from 0.1 to 1.9
- w_out: bfloat16 [2048, 2048], P('col', 'row'), may hold values from -6 to 6
- w_router: bfloat16 [2048, 64], P('row'), may hold values from -0.0625 to 0.0625
- w_gate_up: bfloat16 [64, 2048, 2, 1024], P(('dp', 'col'), None, None, 'row'), may hold values from -0.125 to 0.125
- w_down: bfloat16 [64, 1024, 2048], P(('dp', 'col'), 'row'), may hold values from -0.75 to 0.75
- cotangent: bfloat16 [16384, 2048], P(('dp', 'col'), 'row'), may hold values from -6 to 6
Outputs:
- output: bfloat16 [16384, 2048], P(('dp', 'col'), 'row')
- grad_tokens: bfloat16 [16384, 2048], P(('dp', 'col'), 'row')
- grad_norm_attn: float32 [2048], P('row')
- grad_norm_moe: float32 [2048], P('row')
- grad_qkv: float32 [2048, 16, 384], P('row', 'col')
- grad_q_gain: float32 [128], replicated
- grad_k_gain: float32 [128], replicated
- grad_out: float32 [2048, 2048], P('col', 'row')
- grad_router: float32 [2048, 64], P('row')
- grad_gate_up: float32 [64, 2048, 2, 1024], P(('dp', 'col'), None, None, 'row')
- grad_down: float32 [64, 1024, 2048], P(('dp', 'col'), 'row')
Inputs may be any that keep to these rules, and one draw needn't show every extreme that they name: `routes`: each row names 4 different experts. In each aligned block of 512 rows no expert is named by more than 36 rows, and in some block one expert is named by exactly 36. `positions`: row d is a permutation of the 2048 places of sequence d.
All inputs are finite; a program needn't handle non-finite values.
Results may differ from a plain program's by a relative error of at most 0.03.
Values may be sent and summed in bfloat16 or wider, within the bound.
A program may use at most 256 MiB of HBM per device.

v0:
```python
from functools import partial

import jax
import jax.numpy as jnp
from jax import lax
from jax.sharding import PartitionSpec as P

MODEL_WIDTH = 2048
HEAD_DIM = 128
EXPERTS = 64
TOPK = 4
CAP = 36


EPS = 1e-06
THETA = 10000.0
EXACT = lax.Precision.HIGHEST


def rms_local(operand, gain_vec):
    return operand * lax.rsqrt(jnp.mean(operand * operand, axis=-1, keepdims=True) + EPS) * gain_vec


def rotate(operand, position):
    half_width = operand.shape[-1] // 2
    frequency = THETA ** (-2.0 * jnp.arange(half_width, dtype=jnp.float32) / operand.shape[-1])
    angles = position.astype(jnp.float32)[:, None] * frequency[None, :]
    cosine = jnp.cos(angles)[:, None, :]
    sine_part = jnp.sin(angles)[:, None, :]
    first_half = operand[..., :half_width]
    second_half = operand[..., half_width:]
    return jnp.concatenate(
        [
            first_half * cosine - second_half * sine_part,
            second_half * cosine + first_half * sine_part,
        ],
        axis=-1,
    )


def head_prep(position, q_raw, k_raw, gain_q, gain_k):
    return (rotate(rms_local(q_raw, gain_q), position), rotate(rms_local(k_raw, gain_k), position))


def swish_product(gate_up):
    half_width = gate_up.shape[-1] // 2
    gate_part = gate_up[..., :half_width]
    return gate_part / (1.0 + jnp.exp(-gate_part)) * gate_up[..., half_width:]


def row_grand_total(operand):
    return lax.psum(operand, "row")


def seq_collect(operand):
    return lax.all_gather(operand, "col", axis=0, tiled=True)


def seq_fold(term_fn, row_count):
    return lax.psum_scatter(
        term_fn(jnp.int32(0), row_count * lax.axis_size("col")),
        "col",
        scatter_dimension=0,
        tiled=True,
    )


def head_collect(operand):
    return lax.all_gather(operand, "row", axis=0, tiled=True)


def head_fold(term_fn, row_count):
    return lax.psum_scatter(
        term_fn(jnp.int32(0), row_count * lax.axis_size("row")),
        "row",
        scatter_dimension=0,
        tiled=True,
    )


def expert_swap(operand):
    return lax.all_to_all(operand, ("dp", "col"), split_axis=1, concat_axis=1, tiled=True)


def width_collect(operand):
    return lax.all_gather(operand, "row", axis=2, tiled=True)


def width_spread(operand):
    return lax.psum_scatter(
        operand.astype(jnp.bfloat16), "row", scatter_dimension=2, tiled=True
    ).astype(jnp.float32)


def contract_first(left_mat, right_mat):
    return lax.dot_general(
        left_mat, right_mat, (((0,), (0,)), ((), ())), preferred_element_type=jnp.float32
    )


def contract_last(left_mat, right_mat):
    return lax.dot_general(
        left_mat, right_mat, (((1,), (1,)), ((), ())), preferred_element_type=jnp.float32
    )


def shards(
    tokens,
    positions,
    routes,
    attention_norm_gain,
    experts_norm_gain,
    w_qkv,
    q_gain,
    k_gain,
    w_out,
    w_router,
    w_gate_up,
    w_down,
    cotangent,
):
    tok_rows, width_part = tokens.shape
    heads_here = w_qkv.shape[1]
    head_width = heads_here * HEAD_DIM
    query_rows = positions.shape[1]
    seq_len = query_rows * lax.axis_size("row")
    block_rows = min(512, query_rows)
    block_count = query_rows // block_rows
    score_scale = HEAD_DIM ** (-0.5)
    expert_here = w_gate_up.shape[0]
    ffn_part = w_gate_up.shape[3]
    peer_count = lax.axis_size(("dp", "col"))
    slot_rows = peer_count * CAP
    buffer_size = expert_here * slot_rows
    token_float_values = tokens.astype(jnp.float32)
    inverse_rms_attention = lax.rsqrt(
        row_grand_total(jnp.sum(token_float_values * token_float_values, axis=1)) / MODEL_WIDTH
        + EPS
    )
    unit_rows_attention = token_float_values * inverse_rms_attention[:, None]
    normalized_rows = (unit_rows_attention * attention_norm_gain).astype(jnp.bfloat16)
    normed_seq = seq_collect(normalized_rows)
    qkv_matrix = w_qkv.reshape(width_part, heads_here * 3 * HEAD_DIM)

    def qkv_term(first_row, row_count):
        return jnp.dot(normed_seq, qkv_matrix, preferred_element_type=jnp.float32)

    qkv_parts = head_fold(qkv_term, query_rows).reshape(query_rows, heads_here, 3, HEAD_DIM)
    (query_float, key_float), prep_back = jax.vjp(
        partial(head_prep, positions[0]), qkv_parts[:, :, 0], qkv_parts[:, :, 1], q_gain, k_gain
    )
    queries = query_float.astype(jnp.bfloat16)
    key_value = jnp.concatenate(
        [
            key_float.reshape(query_rows, head_width),
            qkv_parts[:, :, 2].reshape(query_rows, head_width),
        ],
        axis=1,
    ).astype(jnp.bfloat16)
    kv_seq = head_collect(key_value)
    keys_all = kv_seq[:, :head_width].reshape(seq_len, heads_here, HEAD_DIM)
    values_all = kv_seq[:, head_width:].reshape(seq_len, heads_here, HEAD_DIM)
    query_blocks = queries.reshape(block_count, block_rows, heads_here, HEAD_DIM)

    def forward_block(query_block):
        scores = (
            jnp.einsum("qhd,khd->hqk", query_block, keys_all, preferred_element_type=jnp.float32)
            * score_scale
        )
        largest = jnp.max(scores, axis=2, keepdims=True)
        exp_scores = jnp.exp(scores - largest)
        exp_total = jnp.sum(exp_scores, axis=2, keepdims=True)
        prob_weights = (exp_scores / exp_total).astype(jnp.bfloat16)
        attended = jnp.einsum(
            "hqk,khd->qhd", prob_weights, values_all, preferred_element_type=jnp.float32
        )
        return (attended, (largest + jnp.log(exp_total))[:, :, 0])

    attended, log_total = lax.map(forward_block, query_blocks)
    attended_low = attended.reshape(query_rows, head_width).astype(jnp.bfloat16)
    attended_seq = head_collect(attended_low)

    def out_term(first_row, row_count):
        return jnp.dot(attended_seq, w_out, preferred_element_type=jnp.float32)

    hidden_middle = token_float_values + seq_fold(out_term, tok_rows)
    inverse_rms_experts = lax.rsqrt(
        row_grand_total(jnp.sum(hidden_middle * hidden_middle, axis=1)) / MODEL_WIDTH + EPS
    )
    unit_rows_experts = hidden_middle * inverse_rms_experts[:, None]
    experts_input = (unit_rows_experts * experts_norm_gain).astype(jnp.bfloat16)
    logits = row_grand_total(jnp.dot(experts_input, w_router, preferred_element_type=jnp.float32))
    picker = (routes[:, :, None] == jnp.arange(EXPERTS, dtype=jnp.int32)[None, None, :]).astype(
        jnp.float32
    )
    chosen = jnp.einsum("tke,te->tk", picker, logits, precision=EXACT)
    shifted = jnp.exp(chosen - jnp.max(chosen, axis=1, keepdims=True))
    gate_probs = shifted / jnp.sum(shifted, axis=1, keepdims=True)
    flat_routes = routes.reshape(-1)
    onehot = (flat_routes[:, None] == jnp.arange(EXPERTS, dtype=jnp.int32)[None, :]).astype(
        jnp.int32
    )
    slot_rank = jnp.sum(jnp.cumsum(onehot, axis=0) * onehot, axis=1) - 1
    slot_index = (
        flat_routes % expert_here * peer_count + flat_routes // expert_here
    ) * CAP + slot_rank
    token_of = jnp.arange(flat_routes.shape[0], dtype=jnp.int32) // TOPK
    send_in = (
        jnp.zeros((buffer_size, width_part), jnp.bfloat16)
        .at[slot_index]
        .set(experts_input[token_of])
    )
    recv_in = expert_swap(send_in.reshape(expert_here, peer_count, CAP, width_part)).reshape(
        expert_here, slot_rows, width_part
    )
    expert_in = width_collect(recv_in)
    gate_up_w = w_gate_up.reshape(expert_here, MODEL_WIDTH, 2 * ffn_part)
    gate_up = jnp.einsum("erd,edf->erf", expert_in, gate_up_w, preferred_element_type=jnp.float32)
    act_float, swish_back = jax.vjp(swish_product, gate_up)
    act_low = act_float.astype(jnp.bfloat16)
    expert_out = width_spread(
        jnp.einsum("erf,efd->erd", act_low, w_down, preferred_element_type=jnp.float32)
    )
    out_low = expert_out.astype(jnp.bfloat16)
    back_out = expert_swap(out_low.reshape(expert_here, peer_count, CAP, width_part)).reshape(
        buffer_size, width_part
    )
    picked = back_out[slot_index].reshape(tok_rows, TOPK, width_part).astype(jnp.float32)
    output = (hidden_middle + jnp.sum(gate_probs[:, :, None] * picked, axis=1)).astype(jnp.bfloat16)
    cot_float = cotangent.astype(jnp.float32)
    slot_grad = (
        (gate_probs[:, :, None] * cot_float[:, None, :])
        .astype(jnp.bfloat16)
        .reshape(-1, width_part)
    )
    send_grad = jnp.zeros((buffer_size, width_part), jnp.bfloat16).at[slot_index].set(slot_grad)
    recv_grad = expert_swap(send_grad.reshape(expert_here, peer_count, CAP, width_part)).reshape(
        expert_here, slot_rows, width_part
    )
    gate_grad = row_grand_total(jnp.sum(picked * cot_float[:, None, :], axis=2))
    chosen_grad = gate_probs * (gate_grad - jnp.sum(gate_probs * gate_grad, axis=1, keepdims=True))
    logit_grad = jnp.einsum("tk,tke->te", chosen_grad, picker, precision=EXACT)
    router_in_grad = jnp.dot(logit_grad, w_router.astype(jnp.float32).T, precision=EXACT)
    router_part = jnp.dot(experts_input.astype(jnp.float32).T, logit_grad, precision=EXACT)
    grad_full = width_collect(recv_grad)
    act_grad = jnp.einsum("erd,efd->erf", grad_full, w_down, preferred_element_type=jnp.float32)
    grad_down = jnp.einsum("erf,erd->efd", act_low, grad_full, preferred_element_type=jnp.float32)
    gate_up_grad = swish_back(act_grad)[0].astype(jnp.bfloat16)
    grad_gate_up = jnp.einsum(
        "erd,erf->edf", expert_in, gate_up_grad, preferred_element_type=jnp.float32
    ).reshape(expert_here, MODEL_WIDTH, 2, ffn_part)
    in_grad = width_spread(
        jnp.einsum("erf,edf->erd", gate_up_grad, gate_up_w, preferred_element_type=jnp.float32)
    ).astype(jnp.bfloat16)
    back_grad = expert_swap(in_grad.reshape(expert_here, peer_count, CAP, width_part)).reshape(
        buffer_size, width_part
    )
    experts_input_grad = router_in_grad + jnp.sum(
        back_grad[slot_index].reshape(tok_rows, TOPK, width_part).astype(jnp.float32), axis=1
    )
    scaled_experts_rows = experts_input_grad * experts_norm_gain
    mean_square_experts = (
        row_grand_total(jnp.sum(scaled_experts_rows * unit_rows_experts, axis=1)) / MODEL_WIDTH
    )
    middle_grad = cot_float + inverse_rms_experts[:, None] * (
        scaled_experts_rows - unit_rows_experts * mean_square_experts[:, None]
    )
    experts_norm_partial = jnp.sum(experts_input_grad * unit_rows_experts, axis=0)
    middle_seq = seq_collect(middle_grad.astype(jnp.bfloat16))

    def attended_term(first_row, row_count):
        return contract_last(middle_seq, w_out)

    att_grad = head_fold(attended_term, query_rows).astype(jnp.bfloat16)
    out_part = contract_first(attended_seq, middle_seq)
    grad_blocks = att_grad.reshape(block_count, block_rows, heads_here, HEAD_DIM)

    def backward_block(running, pieces):
        query_block, grad_block, total_block = pieces
        scores = (
            jnp.einsum("qhd,khd->hqk", query_block, keys_all, preferred_element_type=jnp.float32)
            * score_scale
        )
        soft_full = jnp.exp(scores - total_block[:, :, None])
        prob_grad = jnp.einsum(
            "qhd,khd->hqk", grad_block, values_all, preferred_element_type=jnp.float32
        )
        score_grad = (
            soft_full * (prob_grad - jnp.sum(soft_full * prob_grad, axis=2, keepdims=True))
        ).astype(jnp.bfloat16)
        query_grad = (
            jnp.einsum("hqk,khd->qhd", score_grad, keys_all, preferred_element_type=jnp.float32)
            * score_scale
        )
        key_grad = (
            running[0]
            + jnp.einsum(
                "hqk,qhd->khd", score_grad, query_block, preferred_element_type=jnp.float32
            )
            * score_scale
        )
        value_grad = running[1] + jnp.einsum(
            "hqk,qhd->khd",
            soft_full.astype(jnp.bfloat16),
            grad_block,
            preferred_element_type=jnp.float32,
        )
        return ((key_grad, value_grad), query_grad)

    zero_keys = jnp.zeros((seq_len, heads_here, HEAD_DIM), jnp.float32)
    (key_sum, value_sum), query_grad = lax.scan(
        backward_block, (zero_keys, zero_keys), (query_blocks, grad_blocks, log_total)
    )
    key_value_grad = jnp.concatenate(
        [key_sum.reshape(seq_len, head_width), value_sum.reshape(seq_len, head_width)], axis=1
    )

    def key_value_term(first_row, row_count):
        return key_value_grad

    kv_mine = head_fold(key_value_term, query_rows)
    q_raw_grad, k_raw_grad, query_gain_partial, key_gain_partial = prep_back(
        (
            query_grad.reshape(query_rows, heads_here, HEAD_DIM),
            kv_mine[:, :head_width].reshape(query_rows, heads_here, HEAD_DIM),
        )
    )
    qkv_grad = jnp.stack(
        [q_raw_grad, k_raw_grad, kv_mine[:, head_width:].reshape(query_rows, heads_here, HEAD_DIM)],
        axis=2,
    )
    qkv_seq = head_collect(
        qkv_grad.reshape(query_rows, heads_here * 3 * HEAD_DIM).astype(jnp.bfloat16)
    )
    qkv_part = contract_first(normed_seq, qkv_seq)

    def normed_term(first_row, row_count):
        return contract_last(qkv_seq, qkv_matrix)

    normalized_rows_grad = seq_fold(normed_term, tok_rows)
    scaled_attention_rows = normalized_rows_grad * attention_norm_gain
    row_stats = row_grand_total(
        jnp.concatenate(
            [
                jnp.sum(scaled_attention_rows * unit_rows_attention, axis=1),
                query_gain_partial,
                key_gain_partial,
            ]
        )
    )
    mean_square_attention = row_stats[:tok_rows] / MODEL_WIDTH
    token_grad = middle_grad + inverse_rms_attention[:, None] * (
        scaled_attention_rows - unit_rows_attention * mean_square_attention[:, None]
    )
    attention_norm_partial = jnp.sum(normalized_rows_grad * unit_rows_attention, axis=0)
    qkv_total, out_total = (
        lax.psum(qkv_part.astype(jnp.bfloat16), "dp").astype(jnp.float32),
        lax.psum(out_part.astype(jnp.bfloat16), "dp").astype(jnp.float32),
    )
    router_total, attn_gain, moe_gain, head_gains = (
        lax.psum(router_part.astype(jnp.bfloat16), ("dp", "col")).astype(jnp.float32),
        lax.psum(attention_norm_partial.astype(jnp.bfloat16), ("dp", "col")).astype(jnp.float32),
        lax.psum(experts_norm_partial.astype(jnp.bfloat16), ("dp", "col")).astype(jnp.float32),
        lax.psum(row_stats[tok_rows:].astype(jnp.bfloat16), ("dp", "col")).astype(jnp.float32),
    )
    return (
        output,
        token_grad.astype(jnp.bfloat16),
        attn_gain,
        moe_gain,
        qkv_total.reshape(width_part, heads_here, 3 * HEAD_DIM),
        head_gains[:HEAD_DIM],
        head_gains[HEAD_DIM:],
        out_total,
        router_total,
        grad_gate_up,
        grad_down,
    )


def solution(mesh):
    placed = (
        P(("dp", "col"), "row"),
        P("dp", "row"),
        P(("dp", "col"), None),
        P("row"),
        P("row"),
        P("row", "col", None),
        P(),
        P(),
        P("col", "row"),
        P("row", None),
        P(("dp", "col"), None, None, "row"),
        P(("dp", "col"), "row", None),
        P(("dp", "col"), "row"),
    )
    return jax.shard_map(
        shards,
        mesh=mesh,
        in_specs=placed,
        out_specs=(
            P(("dp", "col"), "row"),
            P(("dp", "col"), "row"),
            P("row"),
            P("row"),
            P("row", "col", None),
            P(),
            P(),
            P("col", "row"),
            P("row", None),
            P(("dp", "col"), None, None, "row"),
            P(("dp", "col"), "row", None),
        ),
        check_vma=False,
    )
```

profile of v0, /device:TPU:1, one launch (start us, length us, event | category | flops | bytes accessed | tf_op | source)
XLA Modules:
  0.0 1541.1 jit_solution(9444752450067430582)
XLA Ops:
  23.4 30.6 %all-gather.8.cloned.1.call-done = bf16[2048,512]{1,0:T(8,128)(2,1)} async-done(((bf16[512,512]{1,0:T(8,128)(2,1)}), bf16[2048,512]{1,0:T(8,128)(2,1)}) %all-gather.8.cloned.1.call-update) | async-done | bytes 2097168 | tf_op jit(solution)/shard_map/all_gather | solution.py:56
  66.5 112.1 %reduce-scatter.8.cloned.1.call-done = f32[512,1536]{1,0:T(8,128)} async-done(((f32[2048,1536]{1,0:T(8,128)}), f32[512,1536]{1,0:T(8,128)}) %reduce-scatter.8.cloned.1.call-update) | async-done | bytes 3145744 | tf_op jit(solution)/shard_map/reduce_scatter | solution.py:73
  200.7 47.7 %all-gather.10.cloned.1.call-done = bf16[2048,1024]{0,1:T(8,128)(2,1)} async-done(((bf16[512,1024]{0,1:T(8,128)(2,1)}), bf16[2048,1024]{0,1:T(8,128)(2,1)}) %all-gather.10.cloned.1.call-update) | async-done | bytes 4194320 | tf_op jit(solution)/shard_map/all_gather | solution.py:69
  264.7 31.3 %all-gather.12.cloned.1.call-done = bf16[2048,512]{0,1:T(8,128)(2,1)} async-done(((bf16[512,512]{0,1:T(8,128)(2,1)}), bf16[2048,512]{0,1:T(8,128)(2,1)}) %all-gather.12.cloned.1.call-update) | async-done | bytes 2097168 | tf_op jit(solution)/shard_map/all_gather | solution.py:69
  302.5 18.1 %reduce-window.6 = s32[64,16,128]{2,1,0:T(8,128)S(1)} reduce-window(s32[64,16,128]{2,1,0:T(8,128)S(1)} %fusion.43, s32[]{:T(128)} %constant.110.clone.1), window={size=1x1x128 pad=0_0x0_0x127_0}, to_apply=%region_13.14 | reduce-window | flops 16646144 | bytes 1048580 | tf_op jit(solution)/shard_map/reduce-window
  322.1 26.2 %reduce-scatter.10.cloned.1.call-done = f32[512,512]{1,0:T(8,128)} async-done(((f32[2048,512]{1,0:T(8,128)}), f32[512,512]{1,0:T(8,128)}) %reduce-scatter.10.cloned.1.call-update) | async-done | bytes 1048592 | tf_op jit(solution)/shard_map/reduce_scatter | solution.py:60
  359.8 25.7 %scatter_custom_fusion = bf16[2304,512]{1,0:T(8,128)(2,1)} fusion(s32[2048]{0:T(1024)S(1)} %bitcast.168, bf16[512,512]{1,0:T(8,128)(2,1)} %multiply_convert_fusion.4, s32[2048]{0:T(1024)S(1)} %broadcast_clamp_fusion.1, bf16[]{:T(256)} %constant.109.clone.1), kind=kCustom, calls=%fused_computation.31 | custom fusion | bytes 2359808 | tf_op jit(solution)/shard_map/scatter | solution.py:211
  406.1 27.9 %all-to-all-done = bf16[2,32,36,512]{3,0,2,1:T(2,128)(2,1)} async-done(((bf16[2,32,36,512]{3,0,2,1:T(2,128)(2,1)}), bf16[2,32,36,512]{3,0,2,1:T(2,128)(2,1)}, u32[]{:S(2)}, u32[]{:S(2)}) %all-to-all-start) | async-done | bytes 2359328 | tf_op jit(solution)/shard_map/all_to_all | solution.py:82
  475.3 39.8 %all_to_all.20 = bf16[2,32,36,512]{3,0,2,1:T(2,128)(2,1)S(1)} all-to-all(bf16[2,32,36,512]{3,0,2,1:T(2,128)(2,1)S(1)} %copy.83), channel_id=1, replica_groups=mesh['dp'=8,'row'=4,'col'=4] {'dp','col'}, dimensions={1} | all-to-all | bytes 4718592 | tf_op jit(solution)/shard_map/all_to_all | solution.py:82
  524.7 16.7 %all-gather.14.cloned.1.call-done = bf16[2,1152,2048]{2,1,0:T(8,128)(2,1)} async-done(((bf16[2,1152,512]{2,1,0:T(8,128)(2,1)}), bf16[2,1152,2048]{2,1,0:T(8,128)(2,1)}) %all-gather.14.cloned.1.call-update) | async-done | bytes 9437200 | tf_op jit(solution)/shard_map/all_gather | solution.py:86
  551.7 85.0 %all-gather.16.cloned.1.call-done = bf16[2,1152,2048]{2,1,0:T(8,128)(2,1)} async-done(((bf16[2,1152,512]{2,1,0:T(8,128)(2,1)}), bf16[2,1152,2048]{2,1,0:T(8,128)(2,1)}) %all-gather.16.cloned.1.call-update) | async-done | bytes 9437200 | tf_op jit(solution)/shard_map/all_gather | solution.py:86
  663.3 83.4 %reduce-scatter.14.cloned.1.call-done = bf16[2,1152,512]{2,1,0:T(8,128)(2,1)} async-done(((bf16[2,1152,2048]{2,1,0:T(8,128)(2,1)}), bf16[2,1152,512]{2,1,0:T(8,128)(2,1)}) %reduce-scatter.14.cloned.1.call-update) | async-done | bytes 2359312 | tf_op jit(solution)/shard_map/reduce_scatter | solution.py:90
  746.7 14.1 copy.85
  768.6 69.2 %reduce-scatter.12.cloned.1.call-done = bf16[2,1152,512]{2,1,0:T(8,128)(2,1)} async-done(((bf16[2,1152,2048]{2,1,0:T(8,128)(2,1)}), bf16[2,1152,512]{2,1,0:T(8,128)(2,1)}) %reduce-scatter.12.cloned.1.call-update) | async-done | bytes 2359312 | tf_op jit(solution)/shard_map/reduce_scatter | solution.py:90
  837.8 14.1 copy.81
  917.6 14.9 psum.87
  952.3 34.1 %all-gather.18.cloned.1.call-done = bf16[2048,512]{1,0:T(8,128)(2,1)} async-done(((bf16[512,512]{1,0:T(8,128)(2,1)}), bf16[2048,512]{1,0:T(8,128)(2,1)}) %all-gather.18.cloned.1.call-update) | async-done | bytes 2097168 | tf_op jit(solution)/shard_map/all_gather | solution.py:56
  991.3 46.8 %reduce-scatter.16.cloned.1.call-done = f32[512,512]{1,0:T(8,128)} async-done(((f32[2048,512]{1,0:T(8,128)}), f32[512,512]{1,0:T(8,128)}) %reduce-scatter.16.cloned.1.call-update) | async-done | bytes 1048592 | tf_op jit(solution)/shard_map/reduce_scatter | solution.py:73
  1087.2 72.1 %reduce-scatter.18.cloned.1.call-done = f32[512,1024]{0,1:T(8,128)} async-done(((f32[2048,1024]{0,1:T(8,128)}), f32[512,1024]{0,1:T(8,128)}) %reduce-scatter.18.cloned.1.call-update) | async-done | bytes 2097168 | tf_op jit(solution)/shard_map/reduce_scatter | solution.py:73
  1182.2 59.0 %all-gather.20.cloned.1.call-done = bf16[2048,1536]{0,1:T(8,128)(2,1)} async-done(((bf16[512,1536]{0,1:T(8,128)(2,1)}), bf16[2048,1536]{0,1:T(8,128)(2,1)}) %all-gather.20.cloned.1.call-update) | async-done | bytes 6291472 | tf_op jit(solution)/shard_map/all_gather | solution.py:69
  1294.9 46.9 %all-reduce.14.cloned.1.call-done = bf16[512,64]{0,1:T(8,128)(2,1)} async-done(((bf16[512,64]{0,1:T(8,128)(2,1)}), bf16[512,64]{0,1:T(8,128)(2,1)}) %all-reduce.14.cloned.1.call-update) | async-done | bytes 65552 | tf_op jit(solution)/shard_map/psum | solution.py:361
  1343.3 63.8 %all-reduce.16.cloned.1.call-done = (bf16[512,4,384]{2,1,0:T(4,128)(2,1)}, bf16[512,512]{1,0:T(8,128)(2,1)}) async-done(((bf16[512,4,384]{2,1,0:T(4,128)(2,1)}, bf16[512,512]{1,0:T(8,128)(2,1)}), (bf16[512,4,384]{2,1,0:T(4,128)(2,1)}, bf16[512,512]{1,0:T(8,128)(2,1)})) %all-reduce.16.cloned.1.call-update) | async-done | bytes 2097168 | tf_op jit(solution)/shard_map/psum | solution.py:357
  1411.4 46.5 %reduce-scatter.20.cloned.1.call-done = f32[512,512]{1,0:T(8,128)} async-done(((f32[2048,512]{1,0:T(8,128)}), f32[512,512]{1,0:T(8,128)}) %reduce-scatter.20.cloned.1.call-update) | async-done | bytes 1048592 | tf_op jit(solution)/shard_map/reduce_scatter | solution.py:60
  1468.0 60.8 %all-reduce.6 = (bf16[256]{0:T(256)(128)(2,1)S(1)}, bf16[512]{0:T(512)(128)(2,1)S(1)}, bf16[512]{0:T(512)(128)(2,1)S(1)}) all-reduce(bf16[256]{0:T(256)(128)(2,1)S(1)} %slice.76, bf16[512]{0:T(512)(128)(2,1)S(1)} %get-tuple-element.97, bf16[512]{0:T(512)(128)(2,1)S(1)} %get-tuple-element.95), channel_id=1, replica_groups=mesh['dp'=8,'row'=4,'col'=4] {'dp','col'}, use_global_device_ids=true, to_apply=%region_42.43 | all-reduce | flops 1280 | bytes 5120 | tf_op jit(solution)/shard_map/psum | solution.py:364
  (289 shorter events, 439.3 us)
Async XLA Ops:
  7.2 629.5 %copy-start = (bf16[2,256,2048]{2,1,0:T(8,128)(2,1)S(1)}, bf16[2,256,2048]{2,1,0:T(8,128)(2,1)}, u32[]{:S(2)}) copy-start(bf16[2,256,2048]{2,1,0:T(8,128)(2,1)} %param.24) | copy-start | bytes 6291460
  7.2 46.8 %all-gather.8.cloned.1.call-start = ((), (), s32[]{:S(2)}) async-start(), calls=%async_computation.11 | async-start | bytes 2621440 | tf_op jit(solution)/shard_map/all_gather | solution.py:56
  20.5 158.0 %reduce-scatter.8.cloned.1.call-start = ((), (), s32[]{:S(2)}) async-start(), calls=%async_computation.12 | async-start | bytes 15728640 | tf_op jit(solution)/shard_map/reduce_scatter | solution.py:73
  64.0 184.4 %all-gather.10.cloned.1.call-start = ((), (), s32[]{:S(2)}) async-start(), calls=%async_computation.13 | async-start | bytes 5242880 | tf_op jit(solution)/shard_map/all_gather | solution.py:69
  66.5 127.7 %copy-start.27 = (f32[512,64]{1,0:T(8,128)}, f32[512,64]{1,0:T(8,128)S(1)}, u32[]{:S(2)}) copy-start(f32[512,64]{1,0:T(8,128)S(1)} %get-tuple-element.129) | copy-start | bytes 393220
  194.9 56.1 %copy-start.20 = (bf16[512,4,64]{2,0,1:T(8,128)(2,1)}, bf16[512,4,64]{2,0,1:T(8,128)(2,1)S(1)}, u32[]{:S(2)}) copy-start(bf16[512,4,64]{2,0,1:T(8,128)(2,1)S(1)} %get-tuple-element.117) | copy-start | bytes 786436
  194.9 56.1 %copy-start.22 = (bf16[512,4,64]{2,0,1:T(8,128)(2,1)}, bf16[512,4,64]{2,0,1:T(8,128)(2,1)S(1)}, u32[]{:S(2)}) copy-start(bf16[512,4,64]{2,0,1:T(8,128)(2,1)S(1)} %get-tuple-element.118) | copy-start | bytes 786436
  200.4 95.7 %all-gather.12.cloned.1.call-start = ((), (), s32[]{:S(2)}) async-start(), calls=%async_computation.14 | async-start | bytes 2621440 | tf_op jit(solution)/shard_map/all_gather | solution.py:69
  264.7 83.5 %reduce-scatter.10.cloned.1.call-start = ((), (), s32[]{:S(2)}) async-start(), calls=%async_computation.15 | async-start | bytes 5242880 | tf_op jit(solution)/shard_map/reduce_scatter | solution.py:60
  395.7 38.2 %all-to-all-start = ((bf16[2,32,36,512]{3,0,2,1:T(2,128)(2,1)}), bf16[2,32,36,512]{3,0,2,1:T(2,128)(2,1)}, u32[]{:S(2)}, u32[]{:S(2)}) async-start(bf16[2,32,36,512]{3,0,2,1:T(2,128)(2,1)} %copy.79), calls=%async_computation.2 | async-start | bytes 4718592 | tf_op jit(solution)/shard_map/all_to_all | solution.py:82
  403.9 42.6 %all-reduce.12.cloned.1.call-start = ((), (), s32[]{:S(2)}) async-start(), calls=%async_computation.16 | async-start | bytes 262144 | tf_op jit(solution)/shard_map/psum | solution.py:52
  406.0 135.4 %all-gather.14.cloned.1.call-start = ((), (), s32[]{:S(2)}) async-start(), calls=%async_computation.17 | async-start | bytes 11796480 | tf_op jit(solution)/shard_map/all_gather | solution.py:86
  437.5 199.2 %all-gather.16.cloned.1.call-start = ((), (), s32[]{:S(2)}) async-start(), calls=%async_computation.19 | async-start | bytes 11796480 | tf_op jit(solution)/shard_map/all_gather | solution.py:86
  516.8 229.9 %reduce-scatter.14.cloned.1.call-start = ((), (), s32[]{:S(2)}) async-start(), calls=%async_computation.20 | async-start | bytes 11796480 | tf_op jit(solution)/shard_map/reduce_scatter | solution.py:90
  656.5 181.2 %reduce-scatter.12.cloned.1.call-start = ((), (), s32[]{:S(2)}) async-start(), calls=%async_computation.18 | async-start | bytes 11796480 | tf_op jit(solution)/shard_map/reduce_scatter | solution.py:90
  760.8 91.1 %all-to-all-start.3 = ((bf16[2,32,36,512]{3,0,2,1:T(2,128)(2,1)}), bf16[2,32,36,512]{3,0,2,1:T(2,128)(2,1)}, u32[]{:S(2)}, u32[]{:S(2)}) async-start(bf16[2,32,36,512]{3,0,2,1:T(2,128)(2,1)} %bitcast.142), calls=%async_computation.7 | async-start | bytes 4718592 | tf_op jit(solution)/shard_map/all_to_all | solution.py:82
  851.9 37.9 %all-to-all-start.1 = ((bf16[2,32,36,512]{3,0,2,1:T(2,128)(2,1)}), bf16[2,32,36,512]{3,0,2,1:T(2,128)(2,1)}, u32[]{:S(2)}, u32[]{:S(2)}) async-start(bf16[2,32,36,512]{3,0,2,1:T(2,128)(2,1)} %bitcast.141), calls=%async_computation.4 | async-start | bytes 4718592 | tf_op jit(solution)/shard_map/all_to_all | solution.py:82
  859.8 126.6 %all-gather.18.cloned.1.call-start = ((), (), s32[]{:S(2)}) async-start(), calls=%async_computation.21 | async-start | bytes 2621440 | tf_op jit(solution)/shard_map/all_gather | solution.py:56
  952.0 86.1 %reduce-scatter.16.cloned.1.call-start = ((), (), s32[]{:S(2)}) async-start(), calls=%async_computation.22 | async-start | bytes 5242880 | tf_op jit(solution)/shard_map/reduce_scatter | solution.py:73
  991.3 168.1 %reduce-scatter.18.cloned.1.call-start = ((), (), s32[]{:S(2)}) async-start(), calls=%async_computation.23 | async-start | bytes 10485760 | tf_op jit(solution)/shard_map/reduce_scatter | solution.py:73
  1078.9 162.3 %all-gather.20.cloned.1.call-start = ((), (), s32[]{:S(2)}) async-start(), calls=%async_computation.24 | async-start | bytes 7864320 | tf_op jit(solution)/shard_map/all_gather | solution.py:69
  1175.8 165.9 %all-reduce.14.cloned.1.call-start = ((), (), s32[]{:S(2)}) async-start(), calls=%async_computation.26 | async-start | bytes 131072 | tf_op jit(solution)/shard_map/psum | solution.py:361
  1178.1 229.0 %all-reduce.16.cloned.1.call-start = ((), (), s32[]{:S(2)}) async-start(), calls=%async_computation.27 | async-start | bytes 4194304 | tf_op jit(solution)/shard_map/psum | solution.py:357
  1253.4 204.6 %reduce-scatter.20.cloned.1.call-start = ((), (), s32[]{:S(2)}) async-start(), calls=%async_computation.25 | async-start | bytes 5242880 | tf_op jit(solution)/shard_map/reduce_scatter | solution.py:60
  (55 other events, 518.1 us)
Sparse Core Ops, SparseCore 0:
  20.7 33.2 all-gather.7
  64.1 114.3 reduce-scatter.7
  200.5 47.8 all-gather.9
  264.8 31.1 all-gather.11
  301.1 47.1 reduce-scatter.9
  407.5 37.7 all-reduce.11
  447.0 94.4 all-gather.13
  543.7 92.9 all-gather.15
  656.7 90.0 reduce-scatter.13
  749.0 88.6 reduce-scatter.11
  952.1 34.1 all-gather.17
  991.4 46.6 reduce-scatter.15
  1079.0 80.2 reduce-scatter.17
  1175.9 65.2 all-gather.19
  1245.3 96.4 all-reduce.13
  1344.6 62.4 all-reduce.15
  1409.3 48.5 reduce-scatter.19
where the time goes:
time: 1550 us; the launch traced here: 1540 us
  waiting for transfers between devices  907 us (59%)
  local copies, waits for them, and re-layouts  199 us (13%)
  blocking collectives  149 us (10%)
  matrix products  141 us (9%)
  other arithmetic  102 us (7%)
  starting transfers between devices  26.8 us (2%)
    reduce_scatter x3, waiting for transfers between devices, head_fold(): lax.psum_scatter(term_fn(jnp.int32(0), row_count * lax.axis_size('row')),...  231 us
    reduce_scatter x2, waiting for transfers between devices, width_spread(): lax.psum_scatter(operand.astype(jnp.bfloat16), 'row', scatter_dimension=2...  153 us
    all_gather x3, waiting for transfers between devices, head_collect(): return lax.all_gather(operand, 'row', axis=0, tiled=True)  138 us
    all_gather x2, waiting for transfers between devices, width_collect(): return lax.all_gather(operand, 'row', axis=2, tiled=True)  102 us
    reduce_scatter x2, waiting for transfers between devices, seq_fold(): lax.psum_scatter(term_fn(jnp.int32(0), row_count * lax.axis_size('col')),...  72.7 us
    all_gather x2, waiting for transfers between devices, seq_collect(): return lax.all_gather(operand, 'col', axis=0, tiled=True)  64.7 us
    psum x1, waiting for transfers between devices, shards(): lax.psum(qkv_part.astype(jnp.bfloat16), 'dp').astype(jnp.float32)  63.8 us
    psum x1, blocking collectives, shards(): lax.psum(row_stats[tok_rows:].astype(jnp.bfloat16), ('dp', 'col'))  60.8 us
  transfers between devices with their start and end apart: 20, of which 18 were waited for; matrix products, arithmetic and copies ran while one was open for 14% of the time, Pallas kernels for 0%

commit v1 on v0

v1 whole, which is shorter than its diff:
```python
import jax
import jax.numpy as jnp
from jax import lax
from jax.experimental import pallas as pl
from jax.experimental.pallas import tpu as pltpu
from jax.sharding import PartitionSpec as P

WIDTH = 2048
HEAD = 128
EXPERTS = 64
CAP = 36
MAIN = 32
TAIL = CAP - MAIN
SEQ = 2048
EPS = 1e-06
THETA = 10000.0
EXACT = lax.Precision.HIGHEST
MESH = pl.DeviceIdType.MESH
SIZES = (4, 2, 4, 4)
BF = jnp.bfloat16
F32 = jnp.float32
ROWS = [(0, 0, d, 0) for d in (2, 1, 3)]
COLS = [(0, 0, 0, d) for d in (2, 1, 3)]
SIBLING = (0, 1, 0, 0)
PLANE = [(0, 0, i, (i + s) % 4) for s in range(4) for i in range(4) if (i, s) != (0, 0)]
CUBE = [
    (i, 0, (i + s) % 4, (i + t) % 4)
    for s in range(4)
    for t in range(4)
    for i in range(4)
    if (i, s, t) != (0, 0, 0)
]
SOURCES = [(i, 0, 0, (i + s) % 4) for s in range(4) for i in range(4) if (i, s) != (0, 0)]
SIDES = [(i, 0, (i + s) % 4, 0) for s in range(4) for i in range(4) if (i, s) != (0, 0)]
LINES = [(d, 0, 0, 0) for d in (2, 1, 3)]
OTHERS = [
    (a, k, 0, d) for a in range(4) for k in range(2) for d in range(4) if (a, k, d) != (0, 0, 0)
]


def shape(dims, dtype=BF):
    return jax.ShapeDtypeStruct(dims, dtype)


def here():
    group = lax.axis_index("dp")
    return (group // 2, group % 2, lax.axis_index("row"), lax.axis_index("col"))


def moved(place, offset):
    return tuple((p + o) % n for p, o, n in zip(place, offset, SIZES))


def back(place, offset):
    return tuple((p + n - o) % n for p, o, n in zip(place, offset, SIZES))


def device(place):
    return (place[0] * 2 + place[1], place[2], place[3])


def exchange(inputs, outputs, sends, kept, call_id, micros=30, work=None, work_in=(), work_out=(), work_scratch=()):
    offsets = sorted({s[0] for s in sends})
    n_in, n_out, n_send = len(inputs), len(outputs), len(sends)
    m_in, m_out = len(work_in), len(work_out)

    def kernel(*refs):
        ins, refs = refs[:n_in], refs[n_in:]
        worked, refs = refs[:m_in], refs[m_in:]
        outs, refs = refs[:n_out], refs[n_out:]
        made, refs = refs[:m_out], refs[m_out:]
        send_sem, recv_sem, kept_sem = refs[:3]
        special = {"work": worked, "scratch": refs[3:]}
        me = here()
        barrier = pltpu.get_barrier_semaphore()
        for offset in offsets:
            pl.semaphore_signal(
                barrier, inc=1, device_id=device(moved(me, offset)), device_id_type=MESH
            )
        local = []
        for index, (i, take, o, put) in enumerate(kept):
            local.append(
                pltpu.make_async_copy(take(ins[i], me), put(outs[o], me), kept_sem.at[index])
            )
            local[-1].start()
        pl.semaphore_wait(barrier, len(offsets))
        copies, arrived = [], set()

        def arrive(index):
            if index not in arrived:
                arrived.add(index)
                copies[index].wait_recv()

        def named(group, index):
            return special[index[0]][index[1]] if isinstance(index, tuple) else group[index]

        def start(index):
            offset, i, take, o, put = sends[index][:5]
            needs = sends[index][5] if len(sends[index]) > 5 else None
            for need in needs or ():
                if need >= 0:
                    arrive(need)
                elif need not in arrived:
                    arrived.add(need)
                    for copy in local:
                        copy.wait()
            peer = moved(me, offset)
            copies.append(
                pltpu.make_async_remote_copy(
                    src_ref=take(named(ins if needs is None else outs, i), me, peer),
                    dst_ref=put(named(outs, o), me, peer),
                    send_sem=send_sem.at[index],
                    recv_sem=recv_sem.at[index],
                    device_id=device(peer),
                    device_id_type=MESH,
                )
            )
            copies[-1].start()

        for index in range(n_send):
            start(index)
        if work is not None:
            work(arrive, *worked, *made, *refs[3:])
        for index in range(n_send):
            arrive(index)
        for copy in copies:
            copy.wait_send()
        if -1 not in arrived:
            for copy in local:
                copy.wait()

    return pl.pallas_call(
        kernel,
        out_shape=list(outputs) + list(work_out),
        in_specs=[pl.BlockSpec(memory_space=pl.ANY)] * n_in
        + [pl.BlockSpec(memory_space=pltpu.VMEM)] * m_in,
        out_specs=[pl.BlockSpec(memory_space=pl.ANY)] * n_out
        + [pl.BlockSpec(memory_space=pltpu.VMEM)] * m_out,
        scratch_shapes=[
            pltpu.SemaphoreType.DMA((n_send,)),
            pltpu.SemaphoreType.DMA((n_send,)),
            pltpu.SemaphoreType.DMA((max(1, len(kept)),)),
            *work_scratch,
        ],
        compiler_params=pltpu.CompilerParams(
            collective_id=call_id,
            has_side_effects=True,
            vmem_limit_bytes=(8 if work is None else 56) * 2**20,
        ),
        cost_estimate=pl.CostEstimate(
            flops=0, bytes_accessed=micros * 3_500_000, transcendentals=0
        ),
    )(*inputs, *work_in)


def rows(start, size):
    return pl.ds(pl.multiple_of(start, size), size)


def gather_inputs(tokens, w_qkv, w_out, small_int, small_float):
    outputs = [
        shape((512, WIDTH)),
        shape((4, 512, 1536)),
        shape((4, 4, HEAD, 512)),
        shape((4, 4, HEAD), jnp.int32),
        shape((4, 4, HEAD), F32),
    ]
    sends = []

    def eighth(size):
        me = here()
        return rows((me[1] * 4 + me[0]) * size, size)

    def half(size):
        return rows(here()[1] * size, size)

    def add(group, take, o, put=None, i=None, needs=None):
        numbers = []
        for offset in group:
            numbers.append(len(sends))
            if needs is None:
                sends.append((offset, i, take, o, put))
            else:
                view = lambda ref, me, p: take(ref, me)
                sends.append((offset, o, view, o, view, needs))
        return numbers

    first = add(
        ROWS,
        lambda s, me, p: s.at[eighth(64), rows(p[2] * 384, 384)],
        1,
        lambda o, me, p: o.at[me[2], eighth(64), rows(me[3] * 384, 384)],
        1,
    )
    add(ROWS, lambda s, me, p: s, 0, lambda o, me, p: o.at[:, rows(me[2] * 512, 512)], 0)
    add(ROWS, lambda s, me, p: s, 3, lambda o, me, p: o.at[me[2]], 3)
    add(ROWS, lambda s, me, p: s, 4, lambda o, me, p: o.at[me[2]], 4)
    low, high = pl.ds(0, 2), pl.ds(2, 2)
    out_z = add(COLS, lambda o, me: o.at[low, me[3], eighth(16)], 2, needs=[-1])
    out_y = add(LINES, lambda o, me: o.at[high, me[3], eighth(16)], 2, needs=[-1])
    by_z = add(
        COLS, lambda o, me: o.at[low, eighth(64), rows(me[3] * 384, 384)], 1, needs=first
    )
    by_y = add(
        LINES, lambda o, me: o.at[high, eighth(64), rows(me[3] * 384, 384)], 1, needs=first
    )
    out_zy = add(LINES, lambda o, me: o.at[low, :, eighth(16)], 2, needs=out_z)
    out_yz = add(COLS, lambda o, me: o.at[high, me[3], half(64)], 2, needs=out_y)
    by_zy = add(LINES, lambda o, me: o.at[low, eighth(64)], 1, needs=by_z)
    by_yz = add(
        COLS, lambda o, me: o.at[high, half(256), rows(me[3] * 384, 384)], 1, needs=by_y
    )
    pair = [SIBLING]
    add(pair, lambda o, me: o.at[low, :, half(64)], 2, needs=out_zy)
    add(pair, lambda o, me: o.at[high, :, half(64)], 2, needs=out_yz)
    add(pair, lambda o, me: o.at[low, half(256)], 1, needs=by_zy)
    add(pair, lambda o, me: o.at[high, half(256)], 1, needs=by_yz)
    kept = [
        (0, lambda s, me: s, 0, lambda o, me: o.at[:, rows(me[2] * 512, 512)]),
        (
            1,
            lambda s, me: s.at[eighth(64), rows(me[2] * 384, 384)],
            1,
            lambda o, me: o.at[me[2], eighth(64), rows(me[3] * 384, 384)],
        ),
        (2, lambda s, me: s.at[:, eighth(16)], 2, lambda o, me: o.at[:, me[3], eighth(16)]),
        (3, lambda s, me: s, 3, lambda o, me: o.at[me[2]]),
        (4, lambda s, me: s, 4, lambda o, me: o.at[me[2]]),
    ]
    return exchange(
        [tokens, w_qkv.reshape(512, 1536), w_out.reshape(4, HEAD, 512), small_int, small_float],
        outputs,
        sends,
        kept,
        0,
    )


def to_heads(qkv):
    take = lambda s, me, p: s.at[:, rows(p[3] * 384, 384)]
    put = lambda o, me, p: o.at[rows(me[3] * 512, 512)]
    return exchange(
        [qkv],
        [shape((SEQ, 384))],
        [(offset, 0, take, 0, put) for offset in COLS],
        [(0, lambda s, me: take(s, me, me), 0, lambda o, me: put(o, me, me))],
        1,
    )[0]


def from_heads(grads, qkv_part):
    take = lambda s, me, p: s.at[rows(p[3] * 512, 512)]
    put = lambda o, me, p: o.at[:, rows(me[3] * 384, 384)]
    return exchange(
        [grads, qkv_part],
        [shape((512, 1536)), shape((4, 256, 384))],
        [(offset, 0, take, 0, put) for offset in COLS]
        + [(SIBLING, 1, lambda s, me, p: s.at[:, rows(p[1] * 256, 256)], 1, lambda o, me, p: o)],
        [(0, lambda s, me: take(s, me, me), 0, lambda o, me: put(o, me, me))],
        2,
    )


def gather_attended(attended):
    take = lambda s, me, p: s.at[rows(p[3] * 512, 512)]
    put = lambda o, me, p: o.at[:, rows((me[2] * 4 + me[3]) * HEAD, HEAD)]
    return exchange(
        [attended],
        [shape((512, WIDTH))],
        [(offset, 0, take, 0, put) for offset in PLANE],
        [(0, lambda s, me: take(s, me, me), 0, lambda o, me: put(o, me, me))],
        3,
    )[0]


def spread_attended_grad(partial, out_part, small_part):
    take = lambda s, me, p: s.at[:, rows((p[2] * 4 + p[3]) * HEAD, HEAD)]
    put = lambda o, me, p: o.at[me[2], rows(me[3] * 512, 512)]
    return exchange(
        [partial, out_part, small_part],
        [shape((4, SEQ, HEAD)), shape((16, 64, 512)), shape(small_part.shape, F32)],
        [(offset, 0, take, 0, put) for offset in PLANE]
        + [
            (SIBLING, 1, lambda s, me, p: s.at[:, rows(p[1] * 64, 64)], 1, lambda o, me, p: o),
            (SIBLING, 2, lambda s, me, p: s, 2, lambda o, me, p: o),
        ],
        [(0, lambda s, me: take(s, me, me), 0, lambda o, me: put(o, me, me))],
        4,
    )


def row_stack(operand, call_id):
    take = lambda s, me, p: s
    put = lambda o, me, p: o.at[me[2]]
    return exchange(
        [operand],
        [shape((4,) + operand.shape, operand.dtype)],
        [(offset, 0, take, 0, put) for offset in ROWS],
        [(0, lambda s, me: s, 0, lambda o, me: put(o, me, me))],
        call_id,
    )[0]


def spread_features(partial, stats, qkv_half, out_half, small):
    take = lambda s, me, p: s.at[:, rows(p[2] * 512, 512)]
    put = lambda o, me, p: o.at[me[2]]
    whole = lambda s, me, p: s
    take_qkv = lambda s, me, p: s.at[p[2], rows(p[0] * 64, 64)]
    put_qkv = lambda o, me, p: o.at[me[0], me[2]]
    take_out = lambda s, me, p: s.at[p[0] * 4 + p[3]]
    put_out = lambda o, me, p: o.at[me[0] * 4 + me[3]]
    keep = lambda i, take, put: (i, lambda s, me: take(s, me, me), i, lambda o, me: put(o, me, me))
    return exchange(
        [partial, stats, qkv_half, out_half, small],
        [
            shape((4, 512, 512)),
            shape((4,) + stats.shape, F32),
            shape((4, 4, 64, 384)),
            shape((16, 64, 512)),
            shape((16,) + small.shape[1:], F32),
        ],
        [(offset, 0, take, 0, put) for offset in ROWS]
        + [(offset, 1, whole, 1, put) for offset in ROWS]
        + [(offset, 2, take_qkv, 2, put_qkv) for offset in SIDES]
        + [(offset, 3, take_out, 3, put_out) for offset in SOURCES]
        + [(offset, 4, take_out, 4, put_out) for offset in SOURCES],
        [
            keep(0, take, put),
            keep(1, whole, put),
            keep(2, take_qkv, put_qkv),
            keep(3, take_out, put_out),
            keep(4, take_out, put_out),
        ],
        5,
    )


def expert_at(place):
    return place[0] * 16 + (place[2] // 2) * 8 + place[3] * 2 + place[2] % 2


def to_experts(main, tail, call_id, **work):
    take = lambda s, me, p: s.at[expert_at(p)]
    put_main = lambda o, me, p: o.at[me[0] * 4 + me[3], :, rows(me[2] * 512, 512)]
    put_tail = lambda o, me, p: o.at[me[0] * 4 + me[3], me[2]]
    sends = []
    for offset in CUBE:
        sends.append((offset, 0, take, 0, put_main))
        sends.append((offset, 1, take, 1, put_tail))
    return exchange(
        [main, tail],
        [shape((16, MAIN, WIDTH)), shape((16, 4) + tail.shape[1:])],
        sends,
        [
            (0, lambda s, me: take(s, me, me), 0, lambda o, me: put_main(o, me, me)),
            (1, lambda s, me: take(s, me, me), 1, lambda o, me: put_tail(o, me, me)),
        ],
        call_id,
        **work,
    )


def from_experts(main, tail, call_id, first_sends=(), **work):
    take_main = lambda s, me, p: s.at[p[0] * 4 + p[3], :, rows(p[2] * 512, 512)]
    take_tail = lambda s, me, p: s.at[p[0] * 4 + p[3], p[2]]
    put = lambda o, me, p: o.at[expert_at(me)]
    sends = list(first_sends)
    for offset in CUBE:
        sends.append((offset, 0, take_main, 0, put))
        sends.append((offset, 1, take_tail, 1, put))
    return exchange(
        [main, tail],
        [shape((EXPERTS, MAIN, 512)), shape((EXPERTS,) + tail.shape[2:])],
        sends,
        [
            (0, lambda s, me: take_main(s, me, me), 0, lambda o, me: put(o, me, me)),
            (1, lambda s, me: take_tail(s, me, me), 1, lambda o, me: put(o, me, me)),
        ],
        call_id,
        **work,
    )


def collect_sums(qkv_piece, out_piece, small_piece, late):
    put_qkv = lambda o, me, p: o.at[me[1], me[0]]
    put_out = lambda o, me, p: o.at[me[0], me[1]]
    put_small = lambda o, me, p: o.at[me[0] * 4 + me[3]]
    put_late = lambda o, me, p: o.at[(me[0] * 2 + me[1]) * 4 + me[3]]
    whole = lambda s, me, p: s
    sends = []
    for offset in LINES:
        sends.append((offset, 0, whole, 0, put_qkv))
        sends.append((offset, 1, whole, 1, put_out))
    sends.append((SIBLING, 0, whole, 0, put_qkv))
    sends.append((SIBLING, 1, whole, 1, put_out))
    sends += [(offset, 2, whole, 2, put_small) for offset in SOURCES]
    sends += [(offset, 3, whole, 3, put_late) for offset in OTHERS]
    for index, offset in enumerate(LINES):
        for o, view in ((0, put_qkv), (1, put_out)):
            brought = lambda ref, me, p, view=view, offset=offset: view(ref, back(me, offset), p)
            sends.append((SIBLING, o, brought, o, brought, [2 * index + o]))
    return exchange(
        [qkv_piece, out_piece, small_piece, late],
        [
            shape((2, 4, 64, 1536)),
            shape((4, 2, 64, 512)),
            shape((16,) + small_piece.shape, F32),
            shape((32,) + late.shape, F32),
        ],
        sends,
        [
            (0, lambda s, me: s, 0, lambda o, me: put_qkv(o, me, me)),
            (1, lambda s, me: s, 1, lambda o, me: put_out(o, me, me)),
            (2, lambda s, me: s, 2, lambda o, me: put_small(o, me, me)),
            (3, lambda s, me: s, 3, lambda o, me: put_late(o, me, me)),
        ],
        12,
    )


BLOCK = 256
SCALE = HEAD ** (-0.5)
LAST = (((1,), (1,)), ((), ()))
FIRST = (((0,), (0,)), ((), ()))


def swapped(operand):
    return pltpu.roll(operand, HEAD // 2, 1)


def attend_kernel(arrive, qkv_ref, cos_ref, sin_ref, gain_ref, out_ref, query_ref, key_ref, lse_ref):
    def prepare(step, carry):
        span = pl.ds(pl.multiple_of(step * BLOCK, BLOCK), BLOCK)
        for part, target in ((0, query_ref), (1, key_ref)):
            raw = qkv_ref[span, part * HEAD : (part + 1) * HEAD].astype(F32)
            scaled = (
                raw
                * lax.rsqrt(jnp.mean(raw * raw, axis=1, keepdims=True) + EPS)
                * gain_ref[part : part + 1, :]
            )
            target[span, :] = (scaled * cos_ref[span, :] + swapped(scaled) * sin_ref[span, :]).astype(
                BF
            )
        return carry

    lax.fori_loop(0, SEQ // BLOCK, prepare, 0)

    def block(step, carry):
        span = pl.ds(pl.multiple_of(step * BLOCK, BLOCK), BLOCK)
        scores = (
            lax.dot_general(query_ref[span, :], key_ref[...], LAST, preferred_element_type=F32)
            * SCALE
        )
        largest = jnp.max(scores, axis=1, keepdims=True)
        weights = jnp.exp(scores - largest)
        total = jnp.sum(weights, axis=1, keepdims=True)
        mixed = jnp.dot(
            weights.astype(BF), qkv_ref[:, 2 * HEAD :], preferred_element_type=F32
        )
        out_ref[span, :] = (mixed / total).astype(BF)
        lse_ref[span, :] = largest + jnp.log(total)
        return carry

    lax.fori_loop(0, SEQ // BLOCK, block, 0)


def attend(qkv, cosine, sine, gains, main, tail):
    return to_experts(
        main,
        tail,
        6,
        work=attend_kernel,
        work_in=[qkv, cosine, sine, gains],
        work_out=[
            shape((SEQ, HEAD)),
            shape((SEQ, HEAD)),
            shape((SEQ, HEAD)),
            shape((SEQ, 1), F32),
        ],
    )


def attend_back_kernel(
    arrive,
    qkv_ref,
    query_ref,
    key_ref,
    lse_ref,
    parts_ref,
    cos_ref,
    sin_ref,
    gain_ref,
    normed_ref,
    before_ref,
    behind_ref,
    across_ref,
    beyond_ref,
    grad_ref,
    gain_grad_ref,
    weight_grad_ref,
    query_grad,
    key_grad,
    value_grad,
):
    key_grad[...] = jnp.zeros_like(key_grad)
    value_grad[...] = jnp.zeros_like(value_grad)

    def block(step, carry):
        span = pl.ds(pl.multiple_of(step * BLOCK, BLOCK), BLOCK)
        query = query_ref[span, :]
        out_grad = parts_ref[0, span, :].astype(F32)
        for part in range(1, 4):
            out_grad = out_grad + parts_ref[part, span, :].astype(F32)
        out_grad = out_grad.astype(BF)
        scores = (
            lax.dot_general(query, key_ref[...], LAST, preferred_element_type=F32) * SCALE
        )
        soft = jnp.exp(scores - lse_ref[span, :])
        prob_grad = lax.dot_general(
            out_grad, qkv_ref[:, 2 * HEAD :], LAST, preferred_element_type=F32
        )
        inner = jnp.sum(soft * prob_grad, axis=1, keepdims=True)
        score_grad = (soft * (prob_grad - inner)).astype(BF)
        query_grad[span, :] = (
            jnp.dot(score_grad, key_ref[...], preferred_element_type=F32) * SCALE
        )
        key_grad[...] += lax.dot_general(score_grad, query, FIRST, preferred_element_type=F32)
        value_grad[...] += lax.dot_general(
            soft.astype(BF), out_grad, FIRST, preferred_element_type=F32
        )
        return carry

    lax.fori_loop(0, SEQ // BLOCK, block, 0)
    gain_grad_ref[...] = jnp.zeros_like(gain_grad_ref)

    def finish(step, carry):
        span = pl.ds(pl.multiple_of(step * BLOCK, BLOCK), BLOCK)
        for part, source, factor in ((0, query_grad, 1.0), (1, key_grad, SCALE)):
            turned = source[span, :] * factor
            grad = turned * cos_ref[span, :] + swapped(turned * sin_ref[span, :])
            raw = qkv_ref[span, part * HEAD : (part + 1) * HEAD].astype(F32)
            inverse = lax.rsqrt(jnp.mean(raw * raw, axis=1, keepdims=True) + EPS)
            unit = raw * inverse
            gain_grad_ref[part : part + 1, :] += jnp.sum(grad * unit, axis=0, keepdims=True)
            scaled = grad * gain_ref[part : part + 1, :]
            raw_grad = inverse * (scaled - unit * jnp.mean(scaled * unit, axis=1, keepdims=True))
            grad_ref[span, part * HEAD : (part + 1) * HEAD] = raw_grad.astype(BF)
        grad_ref[span, 2 * HEAD :] = value_grad[span, :].astype(BF)
        return carry

    lax.fori_loop(0, SEQ // BLOCK, finish, 0)
    col = lax.axis_index("col")

    def project(step, carry):
        span = pl.ds(pl.multiple_of(step * BLOCK, BLOCK), BLOCK)
        total = jnp.zeros((BLOCK, 3 * HEAD), F32)
        for ref, ahead, skip in (
            (normed_ref, 0, 0),
            (before_ref, 3, 0),
            (behind_ref, 1, 0),
            (across_ref, 2, 0),
            (beyond_ref, 2, 256),
        ):
            size = ref.shape[0]
            first = pl.multiple_of(lax.rem(col + ahead, 4) * 512 + skip, 256)
            total += lax.dot_general(
                ref[:, span], grad_ref[pl.ds(first, size), :], FIRST, preferred_element_type=F32
            )
        weight_grad_ref[span, :] = total.astype(BF)
        return carry

    lax.fori_loop(0, WIDTH // BLOCK, project, 0)


def attend_back(operands, main, tail):
    return from_experts(
        main,
        tail,
        13,
        work=attend_back_kernel,
        work_in=operands,
        work_out=[shape((SEQ, 3 * HEAD)), shape((8, HEAD), F32), shape((WIDTH, 3 * HEAD))],
        work_scratch=[pltpu.VMEM((SEQ, HEAD), F32)] * 3,
    )


SLOTS = 16 * CAP


def expert_kernel(*refs):
    in_main, in_tail, cot_main, cot_tail, gate_ref = refs[:5]
    weights, refs = refs[5:13], refs[13:]
    x_ref, slot_grad_ref, out_main, out_tail, back_main, back_tail = refs[:6]
    act_ref, grad_ref, gate_grad_ref, inner_ref = refs[6:10]
    cot_ref, up_ref, down_ref, out_sum, back_sum, row_sem, weight_sem = refs[10:]
    whole, first, last = pl.ds(0, SLOTS), pl.ds(0, 16 * MAIN), pl.ds(16 * MAIN, 16 * TAIL)
    loads = [
        pltpu.make_async_copy(source, target.at[span], row_sem.at[index])
        for index, (source, target, span) in enumerate(
            (
                (in_main, x_ref, first),
                (in_tail, x_ref, last),
                (cot_main, cot_ref, first),
                (cot_tail, cot_ref, last),
            )
        )
    ]
    for load in loads:
        load.start()
    weight_loads = []
    for slot in range(4):
        for part, target in ((0, up_ref), (4, down_ref)):
            weight_loads.append(
                pltpu.make_async_copy(
                    weights[part + slot], target.at[slot], weight_sem.at[part + slot]
                )
            )
            weight_loads[-1].start()
    for load in loads:
        load.wait()
    slot_grad_ref[...] = (gate_ref[...] * cot_ref[...].astype(F32)).astype(BF)
    for slot in range(4):
        weight_loads[2 * slot].wait()
        weight_loads[2 * slot + 1].wait()
        gate_up = jnp.dot(x_ref[...], up_ref[slot], preferred_element_type=F32)
        gate_part, up_part = gate_up[:, :256], gate_up[:, 256:]
        sigmoid = 1.0 / (1.0 + jnp.exp(-gate_part))
        silu = gate_part * sigmoid
        act = (silu * up_part).astype(BF)
        act_ref[slot] = act
        act_grad = lax.dot_general(
            slot_grad_ref[...], down_ref[slot], LAST, preferred_element_type=F32
        )
        slope = sigmoid * (1.0 + gate_part * (1.0 - sigmoid))
        grad_ref[slot, :, :256] = (act_grad * up_part * slope).astype(BF)
        grad_ref[slot, :, 256:] = (act_grad * silu).astype(BF)
        out = jnp.dot(act, down_ref[slot], preferred_element_type=F32)
        out_sum[...] = out if slot == 0 else out_sum[...] + out
        in_grad = lax.dot_general(
            grad_ref[slot], up_ref[slot], LAST, preferred_element_type=F32
        )
        back_sum[...] = in_grad if slot == 0 else back_sum[...] + in_grad
    out = out_sum[...].astype(BF)
    out_main[...] = out[: 16 * MAIN]
    out_tail[...] = out[16 * MAIN :]
    gate_grad_ref[...] = jnp.sum(
        cot_ref[...].astype(F32) * out.astype(F32), axis=1, keepdims=True
    )
    inner_ref[...] = jnp.sum(back_sum[...] * x_ref[...].astype(F32), axis=1, keepdims=True)
    in_grad = back_sum[...].astype(BF)
    back_main[...] = in_grad[: 16 * MAIN]
    back_tail[...] = in_grad[16 * MAIN :]


def run_expert(in_main, in_tail, cot_main, cot_tail, gate, weights):
    main, tail = shape((16 * MAIN, WIDTH)), shape((16 * TAIL, WIDTH))
    return pl.pallas_call(
        expert_kernel,
        out_shape=[
            shape((SLOTS, WIDTH)),
            shape((SLOTS, WIDTH)),
            main,
            tail,
            main,
            tail,
            shape((4, SLOTS, 256)),
            shape((4, SLOTS, 512)),
            shape((SLOTS, 1), F32),
            shape((SLOTS, 1), F32),
        ],
        in_specs=[pl.BlockSpec(memory_space=pl.ANY)] * 4
        + [pl.BlockSpec(memory_space=pltpu.VMEM)]
        + [pl.BlockSpec(memory_space=pl.ANY)] * 8,
        out_specs=[pl.BlockSpec(memory_space=pltpu.VMEM)] * 10,
        scratch_shapes=[
            pltpu.VMEM((SLOTS, WIDTH), BF),
            pltpu.VMEM((4, WIDTH, 512), BF),
            pltpu.VMEM((4, 256, WIDTH), BF),
            pltpu.VMEM((SLOTS, WIDTH), F32),
            pltpu.VMEM((SLOTS, WIDTH), F32),
            pltpu.SemaphoreType.DMA((4,)),
            pltpu.SemaphoreType.DMA((8,)),
        ],
        compiler_params=pltpu.CompilerParams(vmem_limit_bytes=60 * 2**20),
        cost_estimate=pl.CostEstimate(
            flops=2 * SLOTS * WIDTH * 1024 * 6,
            bytes_accessed=100_000_000,
            transcendentals=SLOTS * 1024,
        ),
    )(in_main, in_tail, cot_main, cot_tail, gate, *weights)


def weight_grads_kernel(
    arrive, x_ref, slot_grad_ref, grad_ref, act_ref, up_grad, down_grad, *theirs
):
    their_x, their_slot_grad, their_grad, their_act = theirs

    def own_up(step, carry):
        span = pl.ds(pl.multiple_of(step * 512, 512), 512)
        for slot in range(2):
            up_grad[slot, span, :] = lax.dot_general(
                x_ref[:, span], grad_ref[slot], FIRST, preferred_element_type=F32
            )
        return carry

    def own_down(step, carry):
        span = pl.ds(pl.multiple_of(step * 512, 512), 512)
        for slot in range(2):
            down_grad[slot, :, span] = lax.dot_general(
                act_ref[slot], slot_grad_ref[:, span], FIRST, preferred_element_type=F32
            )
        return carry

    def their_up(step, carry):
        span = pl.ds(pl.multiple_of(step * 512, 512), 512)
        for slot in range(2):
            up_grad[slot, span, :] += lax.dot_general(
                their_x[:, span], their_grad[slot], FIRST, preferred_element_type=F32
            )
        return carry

    def their_down(step, carry):
        span = pl.ds(pl.multiple_of(step * 512, 512), 512)
        for slot in range(2):
            down_grad[slot, :, span] += lax.dot_general(
                their_act[slot], their_slot_grad[:, span], FIRST, preferred_element_type=F32
            )
        return carry

    lax.fori_loop(0, 4, own_up, 0)
    lax.fori_loop(0, 4, own_down, 0)
    for index in range(4):
        arrive(index)
    lax.fori_loop(0, 4, their_up, 0)
    lax.fori_loop(0, 4, their_down, 0)


def return_rows(main, tail, x, slot_grad, grads, acts):
    whole = lambda s, me, p: s
    other = lambda s, me, p: s.at[pl.ds(2, 2)]
    return from_experts(
        main,
        tail,
        9,
        first_sends=[
            (SIBLING, ("work", 0), whole, ("scratch", 0), whole),
            (SIBLING, ("work", 1), whole, ("scratch", 1), whole),
            (SIBLING, ("work", 2), other, ("scratch", 2), whole),
            (SIBLING, ("work", 3), other, ("scratch", 3), whole),
        ],
        work=weight_grads_kernel,
        work_in=[x, slot_grad, grads, acts],
        work_out=[shape((2, WIDTH, 512), F32), shape((2, 256, WIDTH), F32)],
        work_scratch=[
            pltpu.VMEM((SLOTS, WIDTH), BF),
            pltpu.VMEM((SLOTS, WIDTH), BF),
            pltpu.VMEM((2, SLOTS, 512), BF),
            pltpu.VMEM((2, SLOTS, 256), BF),
        ],
    )


def dot(left, right):
    return jnp.dot(left, right, preferred_element_type=F32)


def dot_last(left, right):
    return lax.dot_general(left, right, LAST, preferred_element_type=F32)


def dot_first(left, right):
    return lax.dot_general(left, right, FIRST, preferred_element_type=F32)


def pieces(value):
    high = value.astype(BF)
    rest = value - high.astype(F32)
    middle = rest.astype(BF)
    low = (rest - middle.astype(F32)).astype(BF)
    return [high, middle, low]


def aux_rows(values):
    stacked = jnp.stack([piece for value in values for piece in pieces(value)], axis=1)
    return jnp.pad(stacked, ((0, 0), (0, 16 - stacked.shape[1]), (0, HEAD - CAP)))


def aux_value(rows_of, index):
    return jnp.sum(rows_of[:, 3 * index : 3 * index + 3, :CAP].astype(F32), axis=1)


def pack_tail(tail):
    return (
        tail.reshape(EXPERTS, TAIL, 4, HEAD).transpose(0, 2, 1, 3).reshape(EXPERTS, 16, HEAD)
    )


def unpack_tail(tail):
    return (
        tail.reshape(EXPERTS, 4, TAIL, HEAD).transpose(0, 2, 1, 3).reshape(EXPERTS * TAIL, 512)
    )


def join_tail(tail):
    return tail.reshape(16, 4, 4, TAIL, HEAD).transpose(0, 3, 1, 2, 4).reshape(16 * TAIL, WIDTH)


def split_tail(tail):
    return (
        tail.reshape(16, TAIL, 4, 4, HEAD).transpose(0, 2, 3, 1, 4).reshape(16, 4, 16, HEAD)
    )


def join_values(values):
    return jnp.concatenate([values[:, :MAIN].reshape(-1), values[:, MAIN:].reshape(-1)])


def split_values(values):
    return jnp.concatenate(
        [values[: 16 * MAIN].reshape(16, MAIN), values[16 * MAIN :].reshape(16, TAIL)], axis=1
    )


FIRST_HOP = [
    ((2 * y + k) * 4 + x, (2 * y + 1 - x % 2) * 4 + 2 * k + x // 2)
    for y in range(4)
    for k in range(2)
    for x in range(4)
]
SECOND_HOP = [
    ((2 * y + k) * 4 + x, (2 * y + x % 2) * 4 + 2 * k + 1 - x // 2)
    for y in range(4)
    for k in range(2)
    for x in range(4)
]
PAIR = [(d, d ^ 1) for d in range(8)]


def hop(operand, pairs):
    return lax.ppermute(operand, ("dp", "row"), pairs)


def hop_col(operand, by):
    return lax.ppermute(operand, "col", [(c, (c + by) % 4) for c in range(4)])


def after(*operands):
    return lax.optimization_barrier(operands)


def inverse_pairs(pairs):
    return [(b, a) for a, b in pairs]


def shards(
    tokens,
    positions,
    routes,
    attention_norm_gain,
    experts_norm_gain,
    w_qkv,
    q_gain,
    k_gain,
    w_out,
    w_router,
    w_gate_up,
    w_down,
    cotangent,
):
    row = lax.axis_index("row")
    upper = row // 2
    token_rows, w_group, w_all, position_rows, gain_rows = gather_inputs(
        tokens,
        w_qkv,
        w_out,
        positions.reshape(4, HEAD),
        attention_norm_gain.reshape(4, HEAD),
    )
    w_group = w_group.reshape(WIDTH, 1536)
    w_all = w_all.reshape(WIDTH, 512)
    gain_full = gain_rows.reshape(WIDTH)

    w_gate_up, w_down, token_rows = after(w_gate_up, w_down, token_rows)
    gate_up_w = w_gate_up.reshape(2, WIDTH, 512)
    own = lambda w, which: lax.dynamic_index_in_dim(w, which, 0, keepdims=False)
    gate_up_1 = hop(own(gate_up_w, upper), FIRST_HOP)
    gate_up_2 = hop(own(gate_up_w, 1 - upper), SECOND_HOP)
    down_1 = hop(own(w_down, upper), FIRST_HOP)
    down_2 = hop(own(w_down, 1 - upper), SECOND_HOP)
    sibling = lambda w: lax.ppermute(w, "dp", PAIR)
    up_ws = [gate_up_1, gate_up_2, sibling(gate_up_1), sibling(gate_up_2)]
    down_ws = [down_1, down_2, sibling(down_1), sibling(down_2)]

    frequency = THETA ** (-2.0 * jnp.arange(HEAD // 2, dtype=F32) / HEAD)
    angles = position_rows.reshape(SEQ).astype(F32)[:, None] * frequency[None, :]
    cosine = jnp.concatenate([jnp.cos(angles)] * 2, axis=1)
    sine = jnp.concatenate([-jnp.sin(angles), jnp.sin(angles)], axis=1)
    gains = jnp.concatenate([q_gain[None], k_gain[None], jnp.zeros((6, HEAD), F32)], axis=0)

    experts = jnp.arange(EXPERTS, dtype=jnp.int32)
    named = jnp.any(routes[:, :, None] == experts[None, None, :], axis=1)
    place = jnp.arange(512, dtype=jnp.int32)
    earlier = (place[None, :] < place[:, None]).astype(BF)
    rank = dot(earlier, named.astype(BF))
    rank = jnp.where(named, rank, -1.0).T
    main_pick = (
        (rank[:, None, :] == jnp.arange(MAIN, dtype=F32)[None, :, None])
        .astype(BF)
        .reshape(EXPERTS * MAIN, 512)
    )
    tail_pick = (
        (rank[:, None, :] == jnp.arange(MAIN, CAP, dtype=F32)[None, :, None])
        .astype(BF)
        .reshape(EXPERTS * TAIL, 512)
    )
    all_pick = jnp.concatenate(
        [main_pick.reshape(EXPERTS, MAIN, 512), tail_pick.reshape(EXPERTS, TAIL, 512)], axis=1
    )

    def pick_rows(operand):
        return (
            dot(main_pick, operand).astype(BF).reshape(EXPERTS, MAIN, 512),
            pack_tail(dot(tail_pick, operand).astype(BF)),
        )

    def place_rows(main, tail):
        return dot_first(main_pick, main.reshape(EXPERTS * MAIN, 512)) + dot_first(
            tail_pick, unpack_tail(tail)
        )

    token_full = token_rows.astype(F32)
    inverse_attention = lax.rsqrt(jnp.mean(token_full * token_full, axis=1) + EPS)
    normed_exact = token_full * inverse_attention[:, None] * gain_full[None, :]
    normed = normed_exact.astype(BF)
    qkv = to_heads(dot(normed, w_group).astype(BF))
    cot_main, cot_tail, attended, query, key, lse = attend(
        qkv, cosine, sine, gains, *pick_rows(cotangent)
    )
    attended_rows = gather_attended(attended)

    token_float = tokens.astype(F32)
    hidden = token_float + dot(attended_rows, w_all)
    scaled_hidden = hidden * experts_norm_gain
    partial_stats = jnp.concatenate(
        [
            lax.dot_general(
                w_router.astype(F32),
                scaled_hidden,
                (((0,), (1,)), ((), ())),
                precision=EXACT,
                preferred_element_type=F32,
            ),
            jnp.sum(hidden * hidden, axis=1)[None],
            jnp.zeros((7, 512), F32),
        ],
        axis=0,
    )
    stats = jnp.sum(row_stack(partial_stats, 7), axis=0)
    inverse_experts = lax.rsqrt(stats[EXPERTS] / WIDTH + EPS)
    logits = stats[:EXPERTS] * inverse_experts[None, :]
    unit_experts = hidden * inverse_experts[:, None]
    experts_input = (unit_experts * experts_norm_gain).astype(BF)
    named_t = rank >= 0
    largest = jnp.max(jnp.where(named_t, logits, -jnp.inf), axis=0, keepdims=True)
    shifted = jnp.where(named_t, jnp.exp(jnp.where(named_t, logits - largest, 0.0)), 0.0)
    gates = shifted / jnp.sum(shifted, axis=0, keepdims=True)
    slot_gates = jnp.sum(all_pick.astype(F32) * gates[:, None, :], axis=2)

    send_main, send_tail = pick_rows(experts_input)
    in_main, in_tail = to_experts(
        send_main, jnp.concatenate([send_tail, aux_rows([slot_gates])], axis=1), 8
    )
    in_main, in_tail, normed = after(in_main, in_tail, normed)
    before, behind = hop_col(normed, 1), hop_col(normed, 3)
    gate_of = join_values(aux_value(in_tail[:, 0, 16:], 0))[:, None]
    (
        slot_in,
        slot_grad,
        out_main,
        out_tail,
        back_main,
        back_tail,
        acts,
        gate_up_grads,
        slot_gate_grad,
        slot_inner,
    ) = run_expert(
        in_main.reshape(16 * MAIN, WIDTH),
        join_tail(in_tail[:, :, :16]),
        cot_main.reshape(16 * MAIN, WIDTH),
        join_tail(cot_tail),
        gate_of,
        up_ws + down_ws,
    )
    aux = jnp.broadcast_to(
        aux_rows([split_values(slot_gate_grad[:, 0]), split_values(slot_inner[:, 0])])[:, None],
        (16, 4, 16, HEAD),
    )
    back_main, back_tail, up_grads, down_grads = return_rows(
        back_main.reshape(16, MAIN, WIDTH),
        jnp.concatenate([split_tail(back_tail), aux], axis=2),
        slot_in,
        slot_grad,
        gate_up_grads,
        acts,
    )
    first_back, second_back = inverse_pairs(FIRST_HOP), inverse_pairs(SECOND_HOP)
    up_grads, down_grads = up_grads.astype(BF), down_grads.astype(BF)
    up_1, up_2 = hop(up_grads[0], first_back), hop(up_grads[1], second_back)
    down_1, down_2 = hop(down_grads[0], first_back), hop(down_grads[1], second_back)

    back_tail, before, behind = after(back_tail, before, behind)
    across, beyond = hop_col(before[:256], 1), hop_col(behind[256:], 3)
    back_aux = back_tail[:, 16:]
    picked = all_pick.astype(F32)
    gate_grad = jnp.sum(picked * aux_value(back_aux, 0)[:, :, None], axis=1)
    inner = jnp.sum(picked * aux_value(back_aux, 1)[:, :, None], axis=(0, 1))
    logit_grad = gates * (gate_grad - jnp.sum(gates * gate_grad, axis=0, keepdims=True))
    experts_input_grad = place_rows(back_main, back_tail[:, :16]) + lax.dot_general(
        logit_grad,
        w_router.astype(F32),
        (((0,), (1,)), ((), ())),
        precision=EXACT,
        preferred_element_type=F32,
    )
    mean_experts = (inner + jnp.sum(logit_grad * logits, axis=0)) / WIDTH
    cot_float = cotangent.astype(F32)
    middle_grad = cot_float + inverse_experts[:, None] * (
        experts_input_grad * experts_norm_gain - unit_experts * mean_experts[:, None]
    )
    router_part = lax.dot_general(
        logit_grad,
        experts_input.astype(F32),
        (((1,), (0,)), ((), ())),
        precision=EXACT,
        preferred_element_type=F32,
    )
    experts_gain_part = jnp.sum(experts_input_grad * unit_experts, axis=0)
    attended_grad = middle_grad.astype(BF)
    out_part = dot_first(attended_rows, attended_grad).astype(BF).reshape(16, HEAD, 512)
    small_part = jnp.concatenate(
        [
            router_part.reshape(256, HEAD),
            experts_gain_part.reshape(4, HEAD),
            jnp.zeros((124, HEAD), F32),
        ],
        axis=0,
    )
    core = lax.axis_index("dp") % 2
    grad_parts, out_other, small_other = spread_attended_grad(
        dot_last(attended_grad, w_all).astype(BF), out_part, small_part
    )
    out_half = (
        lax.dynamic_slice_in_dim(out_part, core * 64, 64, 1).astype(F32)
        + out_other.astype(F32)
    ).astype(BF)
    small = (small_part + small_other).reshape(16, 24, HEAD)
    out_main, out_tail, qkv_grad, head_gain_part, qkv_part = attend_back(
        [qkv, query, key, lse, grad_parts, cosine, sine, gains]
        + [normed, before, behind, across, beyond],
        out_main.reshape(16, MAIN, WIDTH),
        split_tail(out_tail),
    )
    qkv_part = qkv_part.reshape(4, 512, 384)
    qkv_grad, qkv_other = from_heads(qkv_grad, qkv_part)
    qkv_half = (
        lax.dynamic_slice_in_dim(qkv_part, core * 256, 256, 1).astype(F32)
        + qkv_other.astype(F32)
    ).astype(BF)
    normed_grad_part = dot_last(qkv_grad, w_group)
    stat_part = jnp.sum(normed_grad_part * normed_exact, axis=1)
    normed_grad, row_stats, qkv_pieces, out_pieces, small_pieces = spread_features(
        normed_grad_part.astype(BF),
        jnp.concatenate([stat_part.reshape(4, HEAD), head_gain_part[:4]], axis=0),
        qkv_half,
        out_half,
        small,
    )
    normed_grad = jnp.sum(normed_grad.astype(F32), axis=0)
    row_stats = jnp.sum(row_stats, axis=0)
    mean_attention = row_stats[:4].reshape(512) / WIDTH
    unit_attention = token_float * inverse_attention[:, None]
    token_grad = middle_grad + inverse_attention[:, None] * (
        normed_grad * attention_norm_gain - unit_attention * mean_attention[:, None]
    )
    attention_gain_part = jnp.sum(normed_grad * unit_attention, axis=0)

    qkv_piece = (
        jnp.sum(qkv_pieces.astype(F32), axis=0).transpose(1, 0, 2).reshape(64, 1536).astype(BF)
    )
    out_piece = jnp.sum(out_pieces.astype(F32), axis=0).astype(BF)
    qkv_piece, up_1, up_2, down_1, down_2 = after(qkv_piece, up_1, up_2, down_1, down_2)
    is_lower = upper == 0
    grad_gate_up = jnp.stack(
        [jnp.where(is_lower, up_1, up_2), jnp.where(is_lower, up_2, up_1)]
    ).astype(F32)
    grad_down = jnp.stack(
        [jnp.where(is_lower, down_1, down_2), jnp.where(is_lower, down_2, down_1)]
    ).astype(F32)
    qkv_total, out_total, small_total, late = collect_sums(
        qkv_piece,
        out_piece,
        jnp.sum(small_pieces, axis=0),
        jnp.concatenate([attention_gain_part.reshape(4, HEAD), row_stats[4:]], axis=0),
    )
    small_total = small_total.reshape(384, HEAD)
    late = jnp.sum(late, axis=0)
    weight = all_pick.astype(F32) * gates[:, None, :]
    weight_high = weight.astype(BF)
    weight_low = (weight - weight_high.astype(F32)).astype(BF)
    out_tail_rows = unpack_tail(out_tail)
    output = hidden
    for part in (weight_high, weight_low):
        output = (
            output
            + dot_first(
                part[:, :MAIN].reshape(EXPERTS * MAIN, 512),
                out_main.reshape(EXPERTS * MAIN, 512),
            )
            + dot_first(part[:, MAIN:].reshape(EXPERTS * TAIL, 512), out_tail_rows)
        )
    output = output.astype(BF)

    return (
        output,
        token_grad.astype(BF),
        late[:4].reshape(512),
        small_total[256:260].reshape(512),
        qkv_total.astype(F32).reshape(512, 4, 384),
        late[4],
        late[5],
        out_total.astype(F32).reshape(512, 512),
        small_total[:256].reshape(EXPERTS, 512).T,
        grad_gate_up.reshape(2, WIDTH, 2, 256),
        grad_down,
    )


def solution(mesh):
    tokens_like = P(("dp", "col"), "row")
    up_like = P(("dp", "col"), None, None, "row")
    down_like = P(("dp", "col"), "row", None)
    return jax.shard_map(
        shards,
        mesh=mesh,
        in_specs=(
            tokens_like,
            P("dp", "row"),
            P(("dp", "col"), None),
            P("row"),
            P("row"),
            P("row", "col", None),
            P(),
            P(),
            P("col", "row"),
            P("row", None),
            up_like,
            down_like,
            tokens_like,
        ),
        out_specs=(
            tokens_like,
            tokens_like,
            P("row"),
            P("row"),
            P("row", "col", None),
            P(),
            P(),
            P("col", "row"),
            P("row", None),
            up_like,
            down_like,
        ),
        check_vma=False,
    )
```

time: 1550 us -> 682 us (0.44)
  waiting for transfers between devices: 907 us -> 0.04 us
  Pallas kernels: 0 us -> 461 us
  blocking collectives: 149 us -> 0 us
  local copies, waits for them, and re-layouts: 199 us -> 93.3 us
  matrix products: 141 us -> 46.6 us
  other arithmetic: 102 us -> 50.1 us
    pallas_call x0 -> x13, Pallas kernels: none -> 461 us  [the longest x12 435 us: exchange(): pl.pallas_call(kernel, out_shape=list(outputs) + list(work_out), in_specs...]
    reduce_scatter x7 -> x0, waiting for transfers between devices: 456 us -> none  [the longest x3 231 us: head_fold(): lax.psum_scatter(term_fn(jnp.int32(0), row_count * lax.axis_size('row')),...]
    all_gather x7 -> x0, waiting for transfers between devices: 304 us -> none  [the longest x3 138 us: head_collect(): return lax.all_gather(operand, 'row', axis=0, tiled=True)]
    psum x3 -> x0, waiting for transfers between devices: 111 us -> none  [the longest x1 63.8 us: shards(): lax.psum(qkv_part.astype(jnp.bfloat16), 'dp').astype(jnp.float32)]
    psum x6 -> x0, blocking collectives: 109 us -> none  [the longest x1 60.8 us: shards(): lax.psum(row_stats[tok_rows:].astype(jnp.bfloat16), ('dp', 'col'))]
    dot_general x23 -> x19, matrix products: 141 us -> 46.6 us  [the longest x7 19.8 us: dot_first(): return lax.dot_general(left, right, FIRST, preferred_element_type=F32)]
    all_to_all x1 -> x0, blocking collectives: 39.8 us -> none  [expert_swap(): lax.all_to_all(operand, ('dp', 'col'), split_axis=1, concat_axis=1, tiled...]
    all_to_all x3 -> x0, waiting for transfers between devices: 35.7 us -> none  [expert_swap(): lax.all_to_all(operand, ('dp', 'col'), split_axis=1, concat_axis=1, tiled...]
  transfers between devices with their start and end apart: 20 -> 16, of which waited for: 18 -> 0; matrix products, arithmetic and copies ran while one was open for 14% -> 17% of each run, Pallas kernels for 0% -> 58%
where the time goes in v1:
time: 682 us; the launch traced here: 673 us
  Pallas kernels  461 us (68%)
  local copies, waits for them, and re-layouts  93.3 us (14%)
  other arithmetic  50.1 us (7%)
  matrix products  46.6 us (7%)
  starting transfers between devices  19.6 us (3%)
    pallas_call x12, Pallas kernels, exchange(): pl.pallas_call(kernel, out_shape=list(outputs) + list(work_out), in_specs...  435 us
    pallas_call x1, Pallas kernels, run_expert(): pl.pallas_call(expert_kernel, out_shape=[shape((SLOTS, WIDTH)), shape((SL...  25.9 us
    dot_general x7, matrix products, dot_first(): return lax.dot_general(left, right, FIRST, preferred_element_type=F32)  19.8 us
    unnamed x122, local copies, waits for them, and re-layouts  19.1 us
    dot_general x7, matrix products, dot(): return jnp.dot(left, right, preferred_element_type=F32)  14.8 us
  transfers between devices with their start and end apart: 16, of which 0 were waited for; matrix products, arithmetic and copies ran while one was open for 17% of the time, Pallas kernels for 58%

profile of v1, /device:TPU:1, one launch (start us, length us, event | category | flops | bytes accessed | tf_op | source)
XLA Modules:
  0.0 672.5 jit_solution(10907742834807351552)
XLA Ops:
  2.5 46.6 %shard_map.212 = (bf16[512,2048]{1,0:T(8,128)(2,1)S(1)}, bf16[4,512,1536]{2,1,0:T(8,128)(2,1)S(1)}, bf16[4,4,128,512]{3,2,1,0:T(8,128)(2,1)S(1)}, s32[4,4,128]{2,1,0:T(4,128)S(1)}, f32[4,4,128]{2,1,0:T(4,128)S(1)}) custom-call(bf16[512,512]{1,0:T(8,128)(2,1)S(1)} %copy-done.8, bf16[512,1536]{1,0:T(8,128)(2,1)S(1)} %bitcast.164, ...), custom_call_target="tpu_custom_call" | custom-call | bytes 105000000 | tf_op jit(solution)/shard_map/pallas_call | solution.py:132
  57.7 7.6 %reshape.572 = bf16[2,2048,512]{2,1,0:T(8,128)(2,1)} reshape(bf16[2,2048,2,256]{3,2,1,0:T(2,128)(2,1)} %param.23) | data formatting | bytes 8388608 | tf_op jit(solution)/shard_map/reshape | solution.py:884
  65.3 4.5 dynamic-slice_bitcast_fusion
  87.5 5.0 convolution_convert_fusion.3.refs_0_
  92.5 20.9 %shard_map.213.refs_2_ = bf16[2048,384]{1,0:T(8,128)(2,1)S(1)} custom-call(bf16[512,1536]{1,0:T(8,128)(2,1)S(1)} %convolution_convert_fusion.3.refs_0_), custom_call_target="tpu_custom_call" | custom-call | bytes 105000000 | tf_op jit(solution)/shard_map/pallas_call | solution.py:132
  120.9 38.9 %shard_map.214 = (bf16[16,32,2048]{2,1,0:T(8,128)(2,1)}, bf16[16,4,16,128]{3,2,1,0:T(8,128)(2,1)}, bf16[2048,128]{1,0:T(8,128)(2,1)}, bf16[2048,128]{1,0:T(8,128...) custom-call(bf16[64,32,512]{2,1,0:T(8,128)(2,1)} %bitcast.191, bf16[64,16,128]{2,1,0:T(8,128)(2,1)} %bitcast.195, ...), custom_call_target="tpu_custom_call" | custom-call | bytes 105000000 | tf_op jit(solution)/shard_map/pallas_call | solution.py:132
  160.8 29.2 %shard_map.215 = bf16[512,2048]{1,0:T(8,128)(2,1)S(1)} custom-call(bf16[2048,128]{1,0:T(8,128)(2,1)S(1)} %copy-done.12), custom_call_target="tpu_custom_call" | custom-call | bytes 105000000 | tf_op jit(solution)/shard_map/pallas_call | solution.py:132
  192.5 8.5 %shard_map.216 = f32[4,72,512]{2,1,0:T(8,128)S(1)} custom-call(f32[72,512]{1,0:T(8,128)S(1)} %maximum_maximum_fusion.1.refs_0_), custom_call_target="tpu_custom_call" | custom-call | bytes 105000000 | tf_op jit(solution)/shard_map/pallas_call | solution.py:132
  220.9 40.0 %shard_map.217 = (bf16[16,32,2048]{2,1,0:T(8,128)(2,1)S(1)}, bf16[16,4,32,128]{3,2,1,0:T(8,128)(2,1)S(1)}) custom-call(bf16[64,32,512]{2,1,0:T(8,128)(2,1)S(1)} %bitcast.169, bf16[64,32,128]{2,1,0:T(8,128)(2,1)S(1)} %fusion.51.refs_1_), custom_call_target="tpu_custom_call" | custom-call | bytes 105000000 | tf_op jit(solution)/shard_map/pallas_call | solution.py:132
  280.3 25.9 %shard_map.218 = (bf16[576,2048]{1,0:T(8,128)(2,1)}, bf16[576,2048]{1,0:T(8,128)(2,1)}, bf16[512,2048]{1,0:T(8,128)(2,1)}, bf16[64,2048]{1,0:T(8,128)(2,1)}, bf1...) custom-call(bf16[512,2048]{1,0:T(8,128)(2,1)} %bitcast.185, ...), custom_call_target="tpu_custom_call" | custom-call | flops 14495514624 | bytes 100000000 | tf_op jit(solution)/shard_map/pallas_call | solution.py:657
  313.2 48.7 %shard_map.219 = (bf16[64,32,512]{2,1,0:T(8,128)(2,1)}, bf16[64,32,128]{2,1,0:T(8,128)(2,1)}, f32[2,2048,512]{2,1,0:T(8,128)}, f32[2,256,2048]{2,1,0:T(8,128)}) custom-call(bf16[16,32,2048]{2,1,0:T(8,128)(2,1)} %bitcast.192, bf16[16,4,32,128]{3,2,1,0:T(8,128)(2,1)} %pad_maximum_fusion.2.refs_1_, bf16[576,2048]{1,0:T(8,128)(2,1)} %get-tuple-element.95.refs_2_, ...), custom_call_target="tpu_custom_call" | custom-call | bytes 105000000 | tf_op jit(solution)/shard_map/pallas_call | solution.py:132
  365.8 5.4 fusion.23
  391.8 4.5 collective-permute-start.15
  401.6 63.7 %shard_map.220 = (bf16[4,2048,128]{2,1,0:T(8,128)(2,1)S(1)}, bf16[16,64,512]{2,1,0:T(8,128)(2,1)S(1)}, f32[384,128]{1,0:T(8,128)S(1)}) custom-call(bf16[512,2048]{1,0:T(8,128)(2,1)S(1)} %convolution_convert_fusion.1.refs_0_, bf16[16,128,512]{2,1,0:T(8,128)(2,1)S(1)} %bitcast.165, f32[384,128]{1,0:T(8,128)S(1)} %maximum_maximum_fusion.refs_2_), custom_call_target="tpu_custom_call" | custom-call | bytes 105000000 | tf_op jit(solution)/shard_map/pallas_call | solution.py:132
  471.9 53.8 %shard_map.221 = (bf16[64,32,512]{2,1,0:T(8,128)(2,1)}, bf16[64,16,128]{2,1,0:T(8,128)(2,1)}, bf16[2048,384]{1,0:T(8,128)(2,1)}, f32[8,128]{1,0:T(8,128)}, bf16[2048,384]{1,0:T(8,128)(2,1)}) custom-call(bf16[16,32,2048]{2,1,0:T(8,128)(2,1)} %bitcast.190, bf16[16,4,16,128]{3,2,1,0:T(8,128)(2,1)} %bitcast.194, bf16[2048,384]{1,0:T(8,128)(2,1)} %copy-done.2, ...), custom_call_target="tpu_custom_call" | custom-call | bytes 105000000 | tf_op jit(solution)/shard_map/pallas_call | solution.py:132
  530.9 20.7 %shard_map.222 = (bf16[512,1536]{1,0:T(8,128)(2,1)S(1)}, bf16[4,256,384]{2,1,0:T(8,128)(2,1)S(1)}) custom-call(bf16[2048,384]{1,0:T(8,128)(2,1)S(1)} %copy-done.9, bf16[4,512,384]{2,1,0:T(8,128)(2,1)S(1)} %bitcast.167), custom_call_target="tpu_custom_call" | custom-call | bytes 105000000 | tf_op jit(solution)/shard_map/pallas_call | solution.py:132
  551.6 6.8 %fusion.10 = (f32[512]{0:T(512)S(1)}, bf16[512,2048]{1,0:T(8,128)(2,1)S(1)}) fusion(bf16[512,2048]{1,0:T(8,128)(2,1)S(1)} %get-tuple-element.72, f32[2048]{0:T(1024)S(1)} %bitcast.176, f32[512]{0:T(512)S(1)} %add_rsqrt_fusion, bf16[512,1536]{1,0:T(8,128)(2,1)S(1)} %get-tuple-element.110, bf16[2048,1536]{1,0:T(8,128)(2,1)} %bitcast.179), kind=kOutput, calls=%fused_computation.16 | convolution fusion | flops 3227516416 | bytes 12070912 | tf_op jit(solution)/shard_map/dot_general | solution.py:768
  558.6 39.2 %shard_map.223 = (bf16[4,512,512]{2,1,0:T(8,128)(2,1)S(1)}, f32[4,8,128]{2,1,0:T(8,128)S(1)}, bf16[4,4,64,384]{3,2,1,0:T(8,128)(2,1)S(1)}, bf16[16,64,512]{2,1,0:T(8,128)(2,1)S(1)}, f32[16,24,128]{2,1,0:T(8,128)S(1)}) custom-call(bf16[512,2048]{1,0:T(8,128)(2,1)S(1)} %get-tuple-element.144.refs_0_, f32[8,128]{1,0:T(8,128)S(1)} %pad_maximum_fusion.7.refs_1_, ...), custom_call_target="tpu_custom_call" | custom-call | bytes 105000000 | tf_op jit(solution)/shard_map/pallas_call | solution.py:132
  608.6 4.8 fusion.35
  617.6 24.7 %shard_map.224 = (bf16[2,4,64,1536]{3,2,1,0:T(8,128)(2,1)S(1)}, bf16[4,2,64,512]{3,2,1,0:T(8,128)(2,1)S(1)}, f32[16,24,128]{2,1,0:T(8,128)S(1)}, f32[32,8,128]{2,1,0:T(8,128)S(1)}) custom-call(bf16[64,1536]{1,0:T(8,128)(2,1)S(1)} %bitcast.171, bf16[64,512]{1,0:T(8,128)(2,1)S(1)} %reduce_sum.215.refs_1_, f32[24,128]{1,0:T(8,128)S(1)} %reduce_sum.216.refs_2_, ...), custom_call_target="tpu_custom_call" | custom-call | bytes 105000000 | tf_op jit(solution)/shard_map/pallas_call | solution.py:132
  644.0 4.5 broadcast_select_fusion.1
  648.5 4.0 stack.35
  652.5 4.0 stack.36
  665.8 6.4 maximum_convert_fusion
  (297 shorter events, 152.3 us)
Async XLA Ops:
  0.6 190.8 %copy-start = (bf16[512,64]{0,1:T(8,128)(2,1)S(1)}, bf16[512,64]{0,1:T(8,128)(2,1)}, u32[]{:S(2)}) copy-start(bf16[512,64]{0,1:T(8,128)(2,1)} %param.22) | copy-start | bytes 196612
  56.3 156.9 %collective-permute-start.5 = (bf16[256,2048]{1,0:T(8,128)(2,1)}, bf16[256,2048]{1,0:T(8,128)(2,1)}, u32[]{:S(2)}, u32[]{:S(2)}) collective-permute-start(bf16[256,2048]{1,0:T(8,128)(2,1)} %get-tuple-element.153), channel_id=1, source_target_pairs={{0,4},{4,20},{8,0},{12,16},{16,12},{20,28},{24,8},{28,24},{32,36},... | collective-permute-start | bytes 3145736 | tf_op jit(solution)/shard_map/ppermute | solution.py:840
  57.7 155.9 %collective-permute-start.4 = (bf16[256,2048]{1,0:T(8,128)(2,1)}, bf16[256,2048]{1,0:T(8,128)(2,1)}, u32[]{:S(2)}, u32[]{:S(2)}) collective-permute-start(bf16[256,2048]{1,0:T(8,128)(2,1)} %get-tuple-element.154), channel_id=1, source_target_pairs={{0,16},{4,0},{8,20},{12,4},{16,24},{20,8},{24,28},{28,12},{32,48},... | collective-permute-start | bytes 3145736 | tf_op jit(solution)/shard_map/ppermute | solution.py:840
  65.3 7.6 %copy-start.52 = (s32[512,4]{0,1:T(4,128)S(1)}, s32[512,4]{0,1:T(4,128)}, u32[]{:S(2)}) copy-start(s32[512,4]{0,1:T(4,128)} %param.15) | copy-start | bytes 24580
  69.8 136.4 %collective-permute-start.1 = (bf16[2048,512]{1,0:T(8,128)(2,1)}, bf16[2048,512]{1,0:T(8,128)(2,1)}, u32[]{:S(2)}, u32[]{:S(2)}) collective-permute-start(bf16[2048,512]{1,0:T(8,128)(2,1)} %get-tuple-element.145), channel_id=1, source_target_pairs={{0,4},{4,20},{8,0},{12,16},{16,12},{20,28},{24,8},{28,24},{32,36},... | collective-permute-start | bytes 6291464 | tf_op jit(solution)/shard_map/ppermute | solution.py:840
  71.8 136.8 %collective-permute-start = (bf16[2048,512]{1,0:T(8,128)(2,1)}, bf16[2048,512]{1,0:T(8,128)(2,1)}, u32[]{:S(2)}, u32[]{:S(2)}) collective-permute-start(bf16[2048,512]{1,0:T(8,128)(2,1)} %get-tuple-element.146), channel_id=1, source_target_pairs={{0,16},{4,0},{8,20},{12,4},{16,24},{20,8},{24,28},{28,12},{32,48},... | collective-permute-start | bytes 6291464 | tf_op jit(solution)/shard_map/ppermute | solution.py:840
  160.8 29.2 %copy-start.18 = (bf16[4,4,128,512]{3,2,1,0:T(8,128)(2,1)S(1)}, bf16[4,4,128,512]{3,2,1,0:T(8,128)(2,1)}, u32[]{:S(2)}) copy-start(bf16[4,4,128,512]{3,2,1,0:T(8,128)(2,1)} %copy-done.17) | copy-start | bytes 6291460
  206.2 74.1 %collective-permute-start.3 = (bf16[2048,512]{1,0:T(8,128)(2,1)}, bf16[2048,512]{1,0:T(8,128)(2,1)}, u32[]{:S(2)}, u32[]{:S(2)}) collective-permute-start(bf16[2048,512]{1,0:T(8,128)(2,1)} %collective-permute-done.1.refs_6_), channel_id=1, source_target_pairs={{0,16},{16,0},{32,48},{48,32},{64,80},{80,64},{96,112},{112,96},{1... | collective-permute-start | bytes 6291464 | tf_op jit(solution)/shard_map/ppermute | solution.py:890
  208.6 71.7 %collective-permute-start.2 = (bf16[2048,512]{1,0:T(8,128)(2,1)}, bf16[2048,512]{1,0:T(8,128)(2,1)}, u32[]{:S(2)}, u32[]{:S(2)}) collective-permute-start(bf16[2048,512]{1,0:T(8,128)(2,1)} %collective-permute-done.refs_5_), channel_id=1, source_target_pairs={{0,16},{16,0},{32,48},{48,32},{64,80},{80,64},{96,112},{112,96},{1... | collective-permute-start | bytes 6291464 | tf_op jit(solution)/shard_map/ppermute | solution.py:890
  212.2 8.7 %copy-start.29 = (bf16[512,512]{1,0:T(8,128)(2,1)}, bf16[512,512]{1,0:T(8,128)(2,1)S(1)}, u32[]{:S(2)}) copy-start(bf16[512,512]{1,0:T(8,128)(2,1)S(1)} %multiply_convert_fusion) | copy-start | bytes 1572868
  213.2 66.3 %collective-permute-start.7 = (bf16[256,2048]{1,0:T(8,128)(2,1)}, bf16[256,2048]{1,0:T(8,128)(2,1)}, u32[]{:S(2)}, u32[]{:S(2)}) collective-permute-start(bf16[256,2048]{1,0:T(8,128)(2,1)} %collective-permute-done.5.refs_10_), channel_id=1, source_target_pairs={{0,16},{16,0},{32,48},{48,32},{64,80},{80,64},{96,112},{112,96},{1... | collective-permute-start | bytes 3145736 | tf_op jit(solution)/shard_map/ppermute | solution.py:890
  213.6 66.7 %collective-permute-start.6 = (bf16[256,2048]{1,0:T(8,128)(2,1)}, bf16[256,2048]{1,0:T(8,128)(2,1)}, u32[]{:S(2)}, u32[]{:S(2)}) collective-permute-start(bf16[256,2048]{1,0:T(8,128)(2,1)} %collective-permute-done.4.refs_9_), channel_id=1, source_target_pairs={{0,16},{16,0},{32,48},{48,32},{64,80},{80,64},{96,112},{112,96},{1... | collective-permute-start | bytes 3145736 | tf_op jit(solution)/shard_map/ppermute | solution.py:890
  262.2 99.7 %collective-permute-start.9 = (bf16[512,2048]{1,0:T(8,128)(2,1)}, bf16[512,2048]{1,0:T(8,128)(2,1)}, u32[]{:S(2)}, u32[]{:S(2)}) collective-permute-start(bf16[512,2048]{1,0:T(8,128)(2,1)} %fusion.9.refs_10_), channel_id=1, source_target_pairs={{0,3},{1,0},{2,1},{3,2},{4,7},{5,4},{6,5},{7,6},{8,11},{9,8},{10,9... | collective-permute-start | bytes 6291464 | tf_op jit(solution)/shard_map/ppermute | solution.py:844
  279.6 82.4 %collective-permute-start.8 = (bf16[512,2048]{1,0:T(8,128)(2,1)}, bf16[512,2048]{1,0:T(8,128)(2,1)}, u32[]{:S(2)}, u32[]{:S(2)}) collective-permute-start(bf16[512,2048]{1,0:T(8,128)(2,1)} %fusion.9.refs_10_), channel_id=1, source_target_pairs={{0,1},{1,2},{2,3},{3,0},{4,5},{5,6},{6,7},{7,4},{8,9},{9,10},{10,1... | collective-permute-start | bytes 6291464 | tf_op jit(solution)/shard_map/ppermute | solution.py:844
  313.2 51.6 %copy-start.50 = (bf16[64,2048]{1,0:T(8,128)(2,1)S(1)}, bf16[64,2048]{1,0:T(8,128)(2,1)}, u32[]{:S(2)}) copy-start(bf16[64,2048]{1,0:T(8,128)(2,1)} %get-tuple-element.87) | copy-start | bytes 786436
  383.0 17.4 %copy-start.32 = (f32[512,512]{1,0:T(8,128)}, f32[512,512]{1,0:T(8,128)S(1)}, u32[]{:S(2)}) copy-start(f32[512,512]{1,0:T(8,128)S(1)} %get-tuple-element.148) | copy-start | bytes 3145732
  383.0 14.3 %slice-start.2 = ((s8[8388608]{0:T(1024)(128)(4,1)}), s8[4194304]{0:T(1024)(128)(4,1)S(1)}, s32[]{:S(2)}) async-start(s8[8388608]{0:T(1024)(128)(4,1)} %bitcast.186), calls=%async_computation.2 | async-start | bytes 8388608
  385.9 11.3 %slice-start.3 = ((s8[8388608]{0:T(1024)(128)(4,1)}), s8[4194304]{0:T(1024)(128)(4,1)S(1)}, s32[]{:S(2)}) async-start(s8[8388608]{0:T(1024)(128)(4,1)} %bitcast.186), calls=%async_computation.3 | async-start | bytes 8388608
  388.5 78.7 %collective-permute-start.11 = (bf16[256,2048]{1,0:T(8,128)(2,1)}, bf16[256,2048]{1,0:T(8,128)(2,1)S(1)}, u32[]{:S(2)}, u32[]{:S(2)}) collective-permute-start(bf16[256,2048]{1,0:T(8,128)(2,1)} %slice.119), channel_id=1, source_target_pairs={{0,3},{1,0},{2,1},{3,2},{4,7},{5,4},{6,5},{7,6},{8,11},{9,8},{10,9... | collective-permute-start | bytes 3145736 | tf_op jit(solution)/shard_map/ppermute | solution.py:844
  388.6 82.3 %collective-permute-start.10 = (bf16[256,2048]{1,0:T(8,128)(2,1)S(1)}, bf16[256,2048]{1,0:T(8,128)(2,1)S(1)}, u32[]{:S(2)}, u32[]{:S(2)}) collective-permute-start(bf16[256,2048]{1,0:T(8,128)(2,1)S(1)} %slice.118), channel_id=1, source_target_pairs={{0,1},{1,2},{2,3},{3,0},{4,5},{5,6},{6,7},{7,4},{8,9},{9,10},{10,1... | collective-permute-start | bytes 3145736 | tf_op jit(solution)/shard_map/ppermute | solution.py:844
  391.8 225.8 %collective-permute-start.15 = (bf16[256,2048]{1,0:T(8,128)(2,1)}, bf16[256,2048]{1,0:T(8,128)(2,1)}, u32[]{:S(2)}, u32[]{:S(2)}) collective-permute-start(bf16[256,2048]{1,0:T(8,128)(2,1)} %get-tuple-element.151), channel_id=1, source_target_pairs={{4,0},{20,4},{0,8},{16,12},{12,16},{28,20},{8,24},{24,28},{36,32},... | collective-permute-start | bytes 3145736 | tf_op jit(solution)/shard_map/ppermute | solution.py:840
  396.3 221.3 %collective-permute-start.14 = (bf16[256,2048]{1,0:T(8,128)(2,1)}, bf16[256,2048]{1,0:T(8,128)(2,1)}, u32[]{:S(2)}, u32[]{:S(2)}) collective-permute-start(bf16[256,2048]{1,0:T(8,128)(2,1)} %get-tuple-element.152), channel_id=1, source_target_pairs={{16,0},{0,4},{20,8},{4,12},{24,16},{8,20},{28,24},{12,28},{48,32},... | collective-permute-start | bytes 3145736 | tf_op jit(solution)/shard_map/ppermute | solution.py:840
  400.2 217.4 %collective-permute-start.13 = (bf16[2048,512]{1,0:T(8,128)(2,1)}, bf16[2048,512]{1,0:T(8,128)(2,1)}, u32[]{:S(2)}, u32[]{:S(2)}) collective-permute-start(bf16[2048,512]{1,0:T(8,128)(2,1)} %get-tuple-element.141), channel_id=1, source_target_pairs={{4,0},{20,4},{0,8},{16,12},{12,16},{28,20},{8,24},{24,28},{36,32},... | collective-permute-start | bytes 6291464 | tf_op jit(solution)/shard_map/ppermute | solution.py:840
  467.2 150.4 %collective-permute-start.12 = (bf16[2048,512]{1,0:T(8,128)(2,1)}, bf16[2048,512]{1,0:T(8,128)(2,1)}, u32[]{:S(2)}, u32[]{:S(2)}) collective-permute-start(bf16[2048,512]{1,0:T(8,128)(2,1)} %get-tuple-element.142), channel_id=1, source_target_pairs={{16,0},{0,4},{20,8},{4,12},{24,16},{8,20},{28,24},{12,28},{48,32},... | collective-permute-start | bytes 6291464 | tf_op jit(solution)/shard_map/ppermute | solution.py:840
  (52 other events, 168.1 us)

commit v2 on v1

v2 whole, which is shorter than its diff:
```python
import jax
import jax.numpy as jnp
from jax import lax
from jax.experimental import pallas as pl
from jax.experimental.pallas import tpu as pltpu
from jax.sharding import PartitionSpec as P

WIDTH = 2048
HEAD = 128
EXPERTS = 64
CAP = 36
MAIN = 32
TAIL = 8
USED = CAP - MAIN
SEQ = 2048
EPS = 1e-06
THETA = 10000.0
EXACT = lax.Precision.HIGHEST
MESH = pl.DeviceIdType.MESH
SIZES = (4, 2, 4, 4)
BF = jnp.bfloat16
F32 = jnp.float32
ROWS = [(0, 0, d, 0) for d in (2, 1, 3)]
COLS = [(0, 0, 0, d) for d in (2, 1, 3)]
SIBLING = (0, 1, 0, 0)
PLANE = [(0, 0, i, (i + s) % 4) for s in range(4) for i in range(4) if (i, s) != (0, 0)]
CUBE = [
    (i, 0, (i + s) % 4, (i + t) % 4)
    for s in range(4)
    for t in range(4)
    for i in range(4)
    if (i, s, t) != (0, 0, 0)
]
SOURCES = [(i, 0, 0, (i + s) % 4) for s in range(4) for i in range(4) if (i, s) != (0, 0)]
LINES = [(d, 0, 0, 0) for d in (2, 1, 3)]
OTHERS = [
    (a, k, 0, d) for a in range(4) for k in range(2) for d in range(4) if (a, k, d) != (0, 0, 0)
]


def shape(dims, dtype=BF):
    return jax.ShapeDtypeStruct(dims, dtype)


def here():
    group = lax.axis_index("dp")
    return (group // 2, group % 2, lax.axis_index("row"), lax.axis_index("col"))


class Hop:
    def __init__(self, to, origin):
        self.to, self.origin = to, origin


ONE_WAY = Hop(
    lambda p: (p[0], 1 - p[2] % 2, 2 * p[1] + p[2] // 2, p[3]),
    lambda p: (p[0], p[2] // 2, 2 * (p[2] % 2) + 1 - p[1], p[3]),
)
OTHER_WAY = Hop(
    lambda p: (p[0], p[2] % 2, 2 * p[1] + 1 - p[2] // 2, p[3]),
    lambda p: (p[0], p[2] // 2, 2 * (1 - p[2] % 2) + p[1], p[3]),
)


class Links:
    def __init__(self, send, arrive):
        self.send, self.arrive = send, arrive


def moved(place, offset):
    if isinstance(offset, Hop):
        return offset.to(place)
    return tuple((p + o) % n for p, o, n in zip(place, offset, SIZES))


def device(place):
    return (place[0] * 2 + place[1], place[2], place[3])


def exchange(
    inputs,
    outputs,
    sends,
    kept,
    call_id,
    micros=30,
    work=None,
    work_in=(),
    work_out=(),
    work_scratch=(),
    stages=(),
    deferred=(),
):
    offsets = sorted({s[0] for s in sends if not isinstance(s[0], Hop)})
    hops = {id(s[0]): s[0] for s in sends if isinstance(s[0], Hop)}.values()
    n_in, n_out, n_send = len(inputs), len(outputs), len(sends)
    m_in, m_out = len(work_in), len(work_out)

    def kernel(*refs):
        ins, refs = refs[:n_in], refs[n_in:]
        worked, refs = refs[:m_in], refs[m_in:]
        outs, refs = refs[:n_out], refs[n_out:]
        made, refs = refs[:m_out], refs[m_out:]
        send_sem, recv_sem, kept_sem = refs[:3]
        staged, refs = refs[3 : 3 + len(kept)], refs[3 + len(kept) :]
        special = {"work": worked, "made": made, "scratch": refs}
        me = here()
        barrier = pltpu.get_barrier_semaphore()
        greeted = [moved(me, offset) for offset in offsets]
        for way in hops:
            greeted += [way.to(me), way.origin(me)]
        for peer in greeted:
            pl.semaphore_signal(barrier, inc=1, device_id=device(peer), device_id_type=MESH)
        local = []
        for index, (i, take, o, put, _) in enumerate(kept):
            source, target = take(ins[i], me), put(outs[o], me)
            local.append(
                (
                    pltpu.make_async_copy(source, staged[index], kept_sem.at[index, 0]),
                    pltpu.make_async_copy(staged[index], target, kept_sem.at[index, 1]),
                )
            )
            local[-1][0].start()
        pl.semaphore_wait(barrier, len(greeted))
        copies, arrived = {}, set()

        def arrive(index):
            if index not in arrived:
                arrived.add(index)
                copies[index].wait_recv()

        def named(group, index):
            return special[index[0]][index[1]] if isinstance(index, tuple) else group[index]

        def start(index):
            offset, i, take, o, put = sends[index][:5]
            needs = sends[index][5] if len(sends[index]) > 5 else None
            for need in needs or ():
                if need >= 0:
                    arrive(need)
                elif need not in arrived:
                    arrived.add(need)
                    local[-need - 1][1].wait()
            peer = moved(me, offset)
            copies[index] = pltpu.make_async_remote_copy(
                src_ref=take(named(ins if needs is None else outs, i), me, peer),
                dst_ref=put(named(outs, o), me, peer),
                send_sem=send_sem.at[index],
                recv_sem=recv_sem.at[index],
                device_id=device(peer),
                device_id_type=MESH,
            )
            copies[index].start()

        links = Links(start, arrive)
        parts = work(links, *worked, *made, *refs) if stages else ()
        first = [i for i in range(n_send) if len(sends[i]) < 6 and i not in deferred]
        for index in first:
            start(index)
        for load, store in local:
            load.wait()
            store.start()
        for index in range(n_send):
            if index in first or index in deferred:
                continue
            for part, at in zip(parts, stages):
                if at == index:
                    part()
            start(index)
        if work is not None and not stages:
            work(links, *worked, *made, *refs)
        for index in range(n_send):
            arrive(index)
        for copy in copies.values():
            copy.wait_send()
        for index, copy in enumerate(local):
            if -index - 1 not in arrived:
                copy[1].wait()

    return pl.pallas_call(
        kernel,
        out_shape=list(outputs) + list(work_out),
        in_specs=[pl.BlockSpec(memory_space=pl.ANY)] * n_in
        + [pl.BlockSpec(memory_space=pltpu.VMEM)] * m_in,
        out_specs=[pl.BlockSpec(memory_space=pl.ANY)] * n_out
        + [pl.BlockSpec(memory_space=pltpu.VMEM)] * m_out,
        scratch_shapes=[
            pltpu.SemaphoreType.DMA((n_send,)),
            pltpu.SemaphoreType.DMA((n_send,)),
            pltpu.SemaphoreType.DMA((max(1, len(kept)), 2)),
            *[pltpu.VMEM(k[4], inputs[k[0]].dtype) for k in kept],
            *work_scratch,
        ],
        compiler_params=pltpu.CompilerParams(
            collective_id=call_id,
            has_side_effects=True,
            vmem_limit_bytes=(8 if work is None else 56) * 2**20,
        ),
        cost_estimate=pl.CostEstimate(
            flops=0, bytes_accessed=micros * 3_500_000, transcendentals=0
        ),
    )(*inputs, *work_in)


def rows(start, size):
    return pl.ds(pl.multiple_of(start, size), size)


def eighth(size):
    me = here()
    return rows((me[1] * 4 + me[0]) * size, size)


def half(size):
    return rows(here()[1] * size, size)


class Sends(list):
    def add(self, group, take, o, put=None, i=None, needs=None):
        first = len(self)
        for offset in group:
            if needs is None:
                self.append((offset, i, take, o, put))
            else:
                view = lambda ref, me, p: take(ref, me)
                self.append((offset, o, view, o, view, needs))
        return list(range(first, len(self)))


def early_kernel(links, up_ref, rank_ref, cot_ref, up_1, up_2, main_ref, tail_ref):
    upper = lax.axis_index("row") // 2

    def unpack(which, target):
        def part(step, carry):
            span = pl.ds(pl.multiple_of(step * 256, 256), 256)
            target[span, :256] = up_ref[which, span, 0, :]
            target[span, 256:] = up_ref[which, span, 1, :]
            return carry

        return lambda: lax.fori_loop(0, WIDTH // 256, part, 0)

    def pick():
        def part(step, carry):
            ranks = rank_ref[pl.ds(pl.multiple_of(step * 8, 8), 8), :]
            slots = lax.broadcasted_iota(jnp.int32, (8, MAIN + TAIL, 512), 1).astype(F32)
            chosen = (ranks[:, None, :] == slots).astype(F32).reshape(8 * (MAIN + TAIL), 512)
            rows_of = jnp.dot(chosen.astype(BF), cot_ref[...], preferred_element_type=F32)
            rows_of = rows_of.reshape(8, MAIN + TAIL, 512)
            group = pl.ds(pl.multiple_of(step * 8, 8), 8)
            main_ref[group] = rows_of[:, :MAIN].astype(BF)
            tail_ref[group] = rows_of[:, MAIN:].astype(BF)
            return carry

        lax.fori_loop(0, EXPERTS // 8, part, 0)

    return [unpack(upper, up_1), unpack(1 - upper, up_2), pick]


def gather_inputs(tokens, w_qkv, w_out, w_down, small_int, small_float, early):
    outputs = [
        shape((512, WIDTH)),
        shape((4, 512, 1536)),
        shape((4, 4, HEAD), jnp.int32),
        shape((4, 4, HEAD), F32),
        shape((4, 4, HEAD, 512)),
        shape((256, WIDTH)),
        shape((256, WIDTH)),
    ]
    sends = Sends()
    own_cols = lambda me: rows(me[3] * 384, 384)
    low, high = pl.ds(0, 2), pl.ds(2, 2)
    first = sends.add(
        ROWS,
        lambda s, me, p: s.at[eighth(64), rows(p[2] * 384, 384)],
        1,
        lambda o, me, p: o.at[me[2], eighth(64), own_cols(me)],
        1,
    )
    sends.add(ROWS, lambda s, me, p: s, 0, lambda o, me, p: o.at[:, rows(me[2] * 512, 512)], 0)
    sends.add(ROWS, lambda s, me, p: s, 2, lambda o, me, p: o.at[me[2]], 2)
    sends.add(ROWS, lambda s, me, p: s, 3, lambda o, me, p: o.at[me[2]], 3)
    sends.append((ONE_WAY, 5, lambda s, me, p: s.at[me[2] // 2], 5, lambda o, me, p: o))
    sends.append((OTHER_WAY, 5, lambda s, me, p: s.at[1 - me[2] // 2], 6, lambda o, me, p: o))
    out_z = sends.add(COLS, lambda o, me: o.at[low, me[3], eighth(16)], 4, needs=[-2])
    out_y = sends.add(LINES, lambda o, me: o.at[high, me[3], eighth(16)], 4, needs=[-2])
    stages = [len(sends)]
    by_z = sends.add(
        COLS, lambda o, me: o.at[low, eighth(64), own_cols(me)], 1, needs=[-1] + first
    )
    by_y = sends.add(LINES, lambda o, me: o.at[high, eighth(64), own_cols(me)], 1, needs=first)
    sends.add(LINES, lambda o, me: o.at[low, eighth(64), own_cols(me)], 1, needs=first)
    sends.add(COLS, lambda o, me: o.at[high, eighth(64), own_cols(me)], 1, needs=first)
    stages.append(len(sends))
    last_z, last_y = {0: [len(sends) - 6 + i for i in range(3)]}, {0: list(range(len(sends) - 3, len(sends)))}
    for d in (1, 3, 2):
        came = by_z[[offset[3] for offset in COLS].index(d)]
        cols = lambda me, d=d: rows((me[3] + 4 - d) % 4 * 384, 384)
        last_z[d] = sends.add(
            LINES,
            lambda o, me, cols=cols: o.at[low, eighth(64), cols(me)],
            1,
            needs=[came],
        )
        came = by_y[[offset[0] for offset in LINES].index(d)]
        span = lambda me, d=d: rows((me[1] * 4 + (me[0] + 4 - d) % 4) * 64, 64)
        last_y[d] = sends.add(
            COLS,
            lambda o, me, span=span: o.at[high, span(me), own_cols(me)],
            1,
            needs=[came],
        )
    out_zy = sends.add(LINES, lambda o, me: o.at[low, :, eighth(16)], 4, needs=out_z)
    out_yz = sends.add(COLS, lambda o, me: o.at[high, me[3], half(64)], 4, needs=out_y)
    stages.append(len(sends))
    pair = [SIBLING]
    sends.add(pair, lambda o, me: o.at[low, eighth(64)], 1, needs=by_z)
    sends.add(pair, lambda o, me: o.at[high, half(256), own_cols(me)], 1, needs=by_y)
    for d in (1, 3, 2):
        line = [offset[0] for offset in LINES].index(d)
        span = lambda me, d=d: rows((me[1] * 4 + (me[0] + 4 - d) % 4) * 64, 64)
        sends.add(
            pair,
            lambda o, me, span=span: o.at[low, span(me)],
            1,
            needs=[numbers[line] for numbers in last_z.values()],
        )
        col = [offset[3] for offset in COLS].index(d)
        cols = lambda me, d=d: rows((me[3] + 4 - d) % 4 * 384, 384)
        sends.add(
            pair,
            lambda o, me, cols=cols: o.at[high, half(256), cols(me)],
            1,
            needs=[numbers[col] for numbers in last_y.values()],
        )
    sends.add(pair, lambda o, me: o.at[low, :, half(64)], 4, needs=out_zy)
    sends.add(pair, lambda o, me: o.at[high, :, half(64)], 4, needs=out_yz)
    kept = [
        (
            1,
            lambda s, me: s.at[eighth(64), rows(me[2] * 384, 384)],
            1,
            lambda o, me: o.at[me[2], eighth(64), own_cols(me)],
            (64, 384),
        ),
        (
            4,
            lambda s, me: s.at[:, eighth(16)],
            4,
            lambda o, me: o.at[:, me[3], eighth(16)],
            (4, 16, 512),
        ),
        (0, lambda s, me: s, 0, lambda o, me: o.at[:, rows(me[2] * 512, 512)], (512, 512)),
        (2, lambda s, me: s, 2, lambda o, me: o.at[me[2]], (4, HEAD)),
        (3, lambda s, me: s, 3, lambda o, me: o.at[me[2]], (4, HEAD)),
    ]
    return exchange(
        [
            tokens,
            w_qkv.reshape(512, 1536),
            small_int,
            small_float,
            w_out.reshape(4, HEAD, 512),
            w_down,
        ],
        outputs,
        sends,
        kept,
        0,
        work=early_kernel,
        work_in=early,
        work_out=[
            shape((WIDTH, 512)),
            shape((WIDTH, 512)),
            shape((EXPERTS, MAIN, 512)),
            shape((EXPERTS, TAIL, 512)),
        ],
        stages=stages,
    )


def to_heads(qkv):
    take = lambda s, me, p: s.at[:, rows(p[3] * 384, 384)]
    put = lambda o, me, p: o.at[rows(me[3] * 512, 512)]
    return exchange(
        [qkv],
        [shape((SEQ, 384))],
        [(offset, 0, take, 0, put) for offset in COLS],
        [(0, lambda s, me: take(s, me, me), 0, lambda o, me: put(o, me, me), (512, 384))],
        1,
    )[0]


def combine_kernel(links, hidden_ref, main_pick, tail_pick, main_ref, tail_ref, out_ref):
    total = hidden_ref[...]
    total = total + lax.dot_general(
        main_pick[...], main_ref[...], FIRST, preferred_element_type=F32
    )
    total = total + lax.dot_general(
        tail_pick[...], tail_ref[...], FIRST, preferred_element_type=F32
    )
    out_ref[...] = total.astype(BF)


def from_heads(grads, combine):
    take = lambda s, me, p: s.at[rows(p[3] * 512, 512)]
    put = lambda o, me, p: o.at[:, rows(me[3] * 384, 384)]
    return exchange(
        [grads],
        [shape((512, 1536))],
        [(offset, 0, take, 0, put) for offset in COLS],
        [(0, lambda s, me: take(s, me, me), 0, lambda o, me: put(o, me, me), (512, 384))],
        2,
        micros=300,
        work=combine_kernel,
        work_in=combine,
        work_out=[shape((512, 512))],
    )


def gather_attended(attended):
    take = lambda s, me, p: s.at[rows(p[3] * 512, 512)]
    put = lambda o, me, p: o.at[:, rows((me[2] * 4 + me[3]) * HEAD, HEAD)]
    return exchange(
        [attended],
        [shape((512, WIDTH))],
        [(offset, 0, take, 0, put) for offset in PLANE],
        [(0, lambda s, me: take(s, me, me), 0, lambda o, me: put(o, me, me), (512, HEAD))],
        3,
    )[0]


def spread_attended_grad(partial, out_part, small_part):
    take = lambda s, me, p: s.at[:, rows((p[2] * 4 + p[3]) * HEAD, HEAD)]
    put = lambda o, me, p: o.at[me[2], rows(me[3] * 512, 512)]
    return exchange(
        [partial, out_part, small_part],
        [shape((4, SEQ, HEAD)), shape((16, 64, 512)), shape(small_part.shape, F32)],
        [(offset, 0, take, 0, put) for offset in PLANE]
        + [
            (SIBLING, 1, lambda s, me, p: s.at[:, rows(p[1] * 64, 64)], 1, lambda o, me, p: o),
            (SIBLING, 2, lambda s, me, p: s, 2, lambda o, me, p: o),
        ],
        [(0, lambda s, me: take(s, me, me), 0, lambda o, me: put(o, me, me), (512, HEAD))],
        4,
    )


def row_stack(operand, call_id):
    take = lambda s, me, p: s
    put = lambda o, me, p: o.at[me[2]]
    return exchange(
        [operand],
        [shape((4,) + operand.shape, operand.dtype)],
        [(offset, 0, take, 0, put) for offset in ROWS],
        [(0, lambda s, me: s, 0, lambda o, me: put(o, me, me), operand.shape)],
        call_id,
    )[0]


def sum_weights_kernel(
    links, first, normed_ref, grad_ref, piece_ref, their_half, came, half, spread
):
    core, y = lax.axis_index("dp") % 2, lax.axis_index("dp") // 2

    def product(start):
        return lax.dot_general(
            normed_ref[:, rows(start, 256)], grad_ref[...], FIRST, preferred_element_type=F32
        )

    for r in range(4):
        their_half[r] = product(r * 512 + (1 - core) * 256).astype(BF)
        links.send(first + r)
    for r in range(4):
        mine = product(r * 512 + core * 256)
        links.arrive(first + r)
        half[r] = (mine + came[r].astype(F32)).astype(BF)
        for line in range(3):
            links.send(first + 4 + 3 * r + line)
        spread[y, r] = half[r, rows(y * 64, 64), :]
    for r in range(4):
        for line in range(3):
            links.arrive(first + 4 + 3 * r + line)
        total = spread[0, r].astype(F32)
        for source in range(1, 4):
            total = total + spread[source, r].astype(F32)
        piece_ref[r] = total.astype(BF)


def spread_features(partial, stats, out_half, small, normed, grads):
    take = lambda s, me, p: s.at[:, rows(p[2] * 512, 512)]
    put = lambda o, me, p: o.at[me[2]]
    whole = lambda s, me, p: s
    take_out = lambda s, me, p: s.at[p[0] * 4 + p[3]]
    put_out = lambda o, me, p: o.at[me[0] * 4 + me[3]]
    keep = lambda i, take, put, dims: (
        i,
        lambda s, me: take(s, me, me),
        i,
        lambda o, me: put(o, me, me),
        dims,
    )
    sends = (
        [(offset, 0, take, 0, put) for offset in ROWS]
        + [(offset, 1, whole, 1, put) for offset in ROWS]
        + [(offset, 2, take_out, 2, put_out) for offset in SOURCES]
        + [(offset, 3, take_out, 3, put_out) for offset in SOURCES]
    )
    first = len(sends)
    for r in range(4):
        view = lambda ref, me, p, r=r: ref.at[r]
        sends.append((SIBLING, ("scratch", 0), view, ("scratch", 1), view))
    for r in range(4):
        for offset in LINES:
            sends.append(
                (
                    offset,
                    ("scratch", 2),
                    lambda s, me, p, r=r: s.at[r, rows(p[0] * 64, 64)],
                    ("scratch", 3),
                    lambda o, me, p, r=r: o.at[me[0], r],
                )
            )
    return exchange(
        [partial, stats, out_half, small],
        [
            shape((4, 512, 512)),
            shape((4,) + stats.shape, F32),
            shape((16, 64, 512)),
            shape((16,) + small.shape[1:], F32),
        ],
        sends,
        [
            keep(0, take, put, (512, 512)),
            keep(1, whole, put, stats.shape),
            keep(2, take_out, put_out, (64, 512)),
            keep(3, take_out, put_out, small.shape[1:]),
        ],
        5,
        work=lambda links, *refs: sum_weights_kernel(links, first, *refs),
        work_in=[normed, grads],
        work_out=[shape((4, 64, 1536))],
        work_scratch=[pltpu.VMEM((4, 256, 1536), BF)] * 3 + [pltpu.VMEM((4, 4, 64, 1536), BF)],
        deferred=range(first, len(sends)),
    )


def expert_at(place):
    return place[0] * 16 + (place[2] // 2) * 8 + place[3] * 2 + place[2] % 2


def to_experts(main, tail, call_id, **work):
    take = lambda s, me, p: s.at[expert_at(p)]
    put_main = lambda o, me, p: o.at[me[0] * 4 + me[3], :, rows(me[2] * 512, 512)]
    put_tail = lambda o, me, p: o.at[me[0] * 4 + me[3], :, rows(me[2] * 512, 512)]
    sends = []
    for offset in CUBE:
        sends.append((offset, 0, take, 0, put_main))
        sends.append((offset, 1, take, 1, put_tail))
    return exchange(
        [main, tail],
        [shape((16, MAIN, WIDTH)), shape((16, TAIL, WIDTH))],
        sends,
        [
            (0, lambda s, me: take(s, me, me), 0, lambda o, me: put_main(o, me, me), (MAIN, 512)),
            (1, lambda s, me: take(s, me, me), 1, lambda o, me: put_tail(o, me, me), (TAIL, 512)),
        ],
        call_id,
        **work,
    )


def from_experts(main, tail, call_id, first_sends=(), **work):
    take_main = lambda s, me, p: s.at[p[0] * 4 + p[3], :, rows(p[2] * 512, 512)]
    take_tail = lambda s, me, p: s.at[p[0] * 4 + p[3], :, rows(p[2] * 512, 512)]
    put = lambda o, me, p: o.at[expert_at(me)]
    sends = list(first_sends)
    for offset in CUBE:
        sends.append((offset, 0, take_main, 0, put))
        sends.append((offset, 1, take_tail, 1, put))
    return exchange(
        [main, tail],
        [shape((EXPERTS, MAIN, 512)), shape((EXPERTS, TAIL, 512))],
        sends,
        [
            (0, lambda s, me: take_main(s, me, me), 0, lambda o, me: put(o, me, me), (MAIN, 512)),
            (1, lambda s, me: take_tail(s, me, me), 1, lambda o, me: put(o, me, me), (TAIL, 512)),
        ],
        call_id,
        **work,
    )


def collect_sums(qkv_piece, out_piece, small_piece, late):
    put_qkv = lambda o, me, p: o.at[me[1], me[0]]
    put_out = lambda o, me, p: o.at[me[0], me[1]]
    put_small = lambda o, me, p: o.at[me[0] * 4 + me[3]]
    put_late = lambda o, me, p: o.at[(me[0] * 2 + me[1]) * 4 + me[3]]
    whole = lambda s, me, p: s
    sends = Sends()
    heads = sends.add(
        PLANE,
        lambda s, me, p: s.at[p[2], :, rows(p[3] * 384, 384)],
        ("scratch", 0),
        lambda o, me, p: o.at[me[3], me[2]],
        ("work", 0),
    )
    out_sent = sends.add(LINES, whole, 0, put_out, 0)
    sends.add([SIBLING], whole, 0, put_out, 0)
    sends.add(SOURCES, whole, 1, put_small, 1)
    sends.add(OTHERS, whole, 2, put_late, 2)
    later = len(sends)
    qkv_sent = sends.add(LINES, whole, ("made", 0), put_qkv, ("scratch", 1))
    sends.add([SIBLING], whole, ("made", 0), put_qkv, ("scratch", 1))
    relays = []
    for index in (1, 2, 0):
        origin = lambda me, d=LINES[index][0]: (me[0] + 4 - d) % 4
        view = lambda ref, me, p, origin=origin: ref.at[origin(me), me[1]]
        relays.append((out_sent[index], len(sends)))
        sends.append((SIBLING, 0, view, 0, view, [out_sent[index]]))
    for index in (1, 2, 0):
        origin = lambda me, d=LINES[index][0]: (me[0] + 4 - d) % 4
        view = lambda ref, me, p, origin=origin: ref.at[me[1], origin(me)]
        relays.append((qkv_sent[index], len(sends)))
        sends.append((SIBLING, ("made", 0), view, ("made", 0), view, [qkv_sent[index]]))

    def work(links, piece_ref, total_ref, spread, mine):
        group, row, col = lax.axis_index("dp"), lax.axis_index("row"), lax.axis_index("col")
        spread[col, row] = piece_ref[row, :, rows(col * 384, 384)]
        for number in heads:
            links.arrive(number)
        for head in range(4):
            total = spread[0, head].astype(F32)
            for source in range(1, 4):
                total = total + spread[source, head].astype(F32)
            mine[:, head * 384 : (head + 1) * 384] = total.astype(BF)
        for number in range(later, later + 4):
            links.send(number)
        total_ref[group % 2, group // 2] = mine[...]
        for came, number in relays:
            links.arrive(came)
            links.send(number)

    return exchange(
        [out_piece, small_piece, late],
        [
            shape((4, 2, 64, 512)),
            shape((16,) + small_piece.shape, F32),
            shape((32,) + late.shape, F32),
        ],
        sends,
        [
            (0, lambda s, me: s, 0, lambda o, me: put_out(o, me, me), (64, 512)),
            (1, lambda s, me: s, 1, lambda o, me: put_small(o, me, me), small_piece.shape),
            (2, lambda s, me: s, 2, lambda o, me: put_late(o, me, me), late.shape),
        ],
        12,
        work=work,
        work_in=[qkv_piece],
        work_out=[shape((2, 4, 64, 1536))],
        work_scratch=[pltpu.VMEM((4, 4, 64, 384), BF), pltpu.VMEM((64, 1536), BF)],
        deferred=range(later, len(sends)),
    )


BLOCK = 256
SCALE = HEAD ** (-0.5)
LAST = (((1,), (1,)), ((), ()))
FIRST = (((0,), (0,)), ((), ()))


def swapped(operand):
    return pltpu.roll(operand, HEAD // 2, 1)


def attend_kernel(
    links,
    qkv_ref,
    position_ref,
    frequency_ref,
    gain_ref,
    out_ref,
    query_ref,
    key_ref,
    lse_ref,
    cos_ref,
    sin_ref,
):
    def prepare(step, carry):
        span = pl.ds(pl.multiple_of(step * BLOCK, BLOCK), BLOCK)
        angles = position_ref[span, :] * frequency_ref[0:1, :]
        cos_ref[span, :] = jnp.cos(angles)
        sin_ref[span, :] = jnp.sin(angles) * frequency_ref[1:2, :]
        for part, target in ((0, query_ref), (1, key_ref)):
            raw = qkv_ref[span, part * HEAD : (part + 1) * HEAD].astype(F32)
            scaled = (
                raw
                * lax.rsqrt(jnp.mean(raw * raw, axis=1, keepdims=True) + EPS)
                * gain_ref[part : part + 1, :]
            )
            target[span, :] = (scaled * cos_ref[span, :] + swapped(scaled) * sin_ref[span, :]).astype(
                BF
            )
        return carry

    lax.fori_loop(0, SEQ // BLOCK, prepare, 0)

    def block(step, carry):
        span = pl.ds(pl.multiple_of(step * BLOCK, BLOCK), BLOCK)
        scores = (
            lax.dot_general(query_ref[span, :], key_ref[...], LAST, preferred_element_type=F32)
            * SCALE
        )
        largest = jnp.max(scores, axis=1, keepdims=True)
        weights = jnp.exp(scores - largest)
        total = jnp.sum(weights, axis=1, keepdims=True)
        mixed = jnp.dot(
            weights.astype(BF), qkv_ref[:, 2 * HEAD :], preferred_element_type=F32
        )
        out_ref[span, :] = (mixed / total).astype(BF)
        lse_ref[span, :] = largest + jnp.log(total)
        return carry

    lax.fori_loop(0, SEQ // BLOCK, block, 0)


def attend(qkv, position, frequency, gains, main, tail):
    return to_experts(
        main,
        tail,
        6,
        work=attend_kernel,
        work_in=[qkv, position, frequency, gains],
        work_out=[
            shape((SEQ, HEAD)),
            shape((SEQ, HEAD)),
            shape((SEQ, HEAD)),
            shape((SEQ, 1), F32),
            shape((SEQ, HEAD), F32),
            shape((SEQ, HEAD), F32),
        ],
    )


def attend_back_kernel(
    links,
    qkv_ref,
    query_ref,
    key_ref,
    lse_ref,
    parts_ref,
    cos_ref,
    sin_ref,
    gain_ref,
    grad_ref,
    gain_grad_ref,
    query_grad,
    key_grad,
    value_grad,
):
    key_grad[...] = jnp.zeros_like(key_grad)
    value_grad[...] = jnp.zeros_like(value_grad)

    def block(step, carry):
        span = pl.ds(pl.multiple_of(step * BLOCK, BLOCK), BLOCK)
        query = query_ref[span, :]
        out_grad = parts_ref[0, span, :].astype(F32)
        for part in range(1, 4):
            out_grad = out_grad + parts_ref[part, span, :].astype(F32)
        out_grad = out_grad.astype(BF)
        scores = (
            lax.dot_general(query, key_ref[...], LAST, preferred_element_type=F32) * SCALE
        )
        soft = jnp.exp(scores - lse_ref[span, :])
        prob_grad = lax.dot_general(
            out_grad, qkv_ref[:, 2 * HEAD :], LAST, preferred_element_type=F32
        )
        inner = jnp.sum(soft * prob_grad, axis=1, keepdims=True)
        score_grad = (soft * (prob_grad - inner)).astype(BF)
        query_grad[span, :] = (
            jnp.dot(score_grad, key_ref[...], preferred_element_type=F32) * SCALE
        )
        key_grad[...] += lax.dot_general(score_grad, query, FIRST, preferred_element_type=F32)
        value_grad[...] += lax.dot_general(
            soft.astype(BF), out_grad, FIRST, preferred_element_type=F32
        )
        return carry

    lax.fori_loop(0, SEQ // BLOCK, block, 0)
    gain_grad_ref[...] = jnp.zeros_like(gain_grad_ref)

    def finish(step, carry):
        span = pl.ds(pl.multiple_of(step * BLOCK, BLOCK), BLOCK)
        for part, source, factor in ((0, query_grad, 1.0), (1, key_grad, SCALE)):
            turned = source[span, :] * factor
            grad = turned * cos_ref[span, :] + swapped(turned * sin_ref[span, :])
            raw = qkv_ref[span, part * HEAD : (part + 1) * HEAD].astype(F32)
            inverse = lax.rsqrt(jnp.mean(raw * raw, axis=1, keepdims=True) + EPS)
            unit = raw * inverse
            gain_grad_ref[part : part + 1, :] += jnp.sum(grad * unit, axis=0, keepdims=True)
            scaled = grad * gain_ref[part : part + 1, :]
            raw_grad = inverse * (scaled - unit * jnp.mean(scaled * unit, axis=1, keepdims=True))
            grad_ref[span, part * HEAD : (part + 1) * HEAD] = raw_grad.astype(BF)
        grad_ref[span, 2 * HEAD :] = value_grad[span, :].astype(BF)
        return carry

    lax.fori_loop(0, SEQ // BLOCK, finish, 0)

def attend_back(operands, main, tail):
    return from_experts(
        main,
        tail,
        13,
        work=attend_back_kernel,
        work_in=operands,
        work_out=[shape((SEQ, 3 * HEAD)), shape((8, HEAD), F32)],
        work_scratch=[pltpu.VMEM((SEQ, HEAD), F32)] * 3,
    )


SLOTS = 16 * (MAIN + TAIL)


def expert_kernel(*refs):
    in_main, in_tail, cot_main, cot_tail, gate_ref = refs[:5]
    weights, refs = refs[5:13], refs[13:]
    x_ref, slot_grad_ref, out_main, out_tail, back_main, back_tail = refs[:6]
    act_ref, grad_ref, gate_grad_ref, inner_ref = refs[6:10]
    cot_ref, up_ref, down_ref, out_sum, back_sum, row_sem, weight_sem = refs[10:]
    whole, first, last = pl.ds(0, SLOTS), pl.ds(0, 16 * MAIN), pl.ds(16 * MAIN, 16 * TAIL)
    loads = [
        pltpu.make_async_copy(source, target.at[span], row_sem.at[index])
        for index, (source, target, span) in enumerate(
            (
                (in_main, x_ref, first),
                (in_tail, x_ref, last),
                (cot_main, cot_ref, first),
                (cot_tail, cot_ref, last),
            )
        )
    ]
    for load in loads:
        load.start()
    weight_loads = []
    for slot in range(4):
        for part, target in ((0, up_ref), (4, down_ref)):
            weight_loads.append(
                pltpu.make_async_copy(
                    weights[part + slot], target.at[slot], weight_sem.at[part + slot]
                )
            )
            weight_loads[-1].start()
    for load in loads:
        load.wait()
    slot_grad_ref[...] = (gate_ref[...] * cot_ref[...].astype(F32)).astype(BF)
    for slot in range(4):
        weight_loads[2 * slot].wait()
        weight_loads[2 * slot + 1].wait()
        gate_up = jnp.dot(x_ref[...], up_ref[slot], preferred_element_type=F32)
        gate_part, up_part = gate_up[:, :256], gate_up[:, 256:]
        sigmoid = 1.0 / (1.0 + jnp.exp(-gate_part))
        silu = gate_part * sigmoid
        act = (silu * up_part).astype(BF)
        act_ref[slot] = act
        act_grad = lax.dot_general(
            slot_grad_ref[...], down_ref[slot], LAST, preferred_element_type=F32
        )
        slope = sigmoid * (1.0 + gate_part * (1.0 - sigmoid))
        grad_ref[slot, :, :256] = (act_grad * up_part * slope).astype(BF)
        grad_ref[slot, :, 256:] = (act_grad * silu).astype(BF)
        out = jnp.dot(act, down_ref[slot], preferred_element_type=F32)
        out_sum[...] = out if slot == 0 else out_sum[...] + out
        in_grad = lax.dot_general(
            grad_ref[slot], up_ref[slot], LAST, preferred_element_type=F32
        )
        back_sum[...] = in_grad if slot == 0 else back_sum[...] + in_grad
    out = out_sum[...].astype(BF)
    gated = (gate_ref[...] * out_sum[...]).astype(BF)
    out_main[...] = gated[: 16 * MAIN]
    out_tail[...] = gated[16 * MAIN :]
    gate_grad_ref[...] = jnp.sum(
        cot_ref[...].astype(F32) * out.astype(F32), axis=1, keepdims=True
    )
    inner_ref[...] = jnp.sum(back_sum[...] * x_ref[...].astype(F32), axis=1, keepdims=True)
    in_grad = back_sum[...].astype(BF)
    back_main[...] = in_grad[: 16 * MAIN]
    back_tail[...] = in_grad[16 * MAIN :]


def run_expert(in_main, in_tail, cot_main, cot_tail, gate, weights):
    main, tail = shape((16 * MAIN, WIDTH)), shape((16 * TAIL, WIDTH))
    return pl.pallas_call(
        expert_kernel,
        out_shape=[
            shape((SLOTS, WIDTH)),
            shape((SLOTS, WIDTH)),
            main,
            tail,
            main,
            tail,
            shape((4, SLOTS, 256)),
            shape((4, SLOTS, 512)),
            shape((SLOTS, 1), F32),
            shape((SLOTS, 1), F32),
        ],
        in_specs=[pl.BlockSpec(memory_space=pl.ANY)] * 4
        + [pl.BlockSpec(memory_space=pltpu.VMEM)]
        + [pl.BlockSpec(memory_space=pl.ANY)] * 8,
        out_specs=[pl.BlockSpec(memory_space=pltpu.VMEM)] * 10,
        scratch_shapes=[
            pltpu.VMEM((SLOTS, WIDTH), BF),
            pltpu.VMEM((4, WIDTH, 512), BF),
            pltpu.VMEM((4, 256, WIDTH), BF),
            pltpu.VMEM((SLOTS, WIDTH), F32),
            pltpu.VMEM((SLOTS, WIDTH), F32),
            pltpu.SemaphoreType.DMA((4,)),
            pltpu.SemaphoreType.DMA((8,)),
        ],
        compiler_params=pltpu.CompilerParams(vmem_limit_bytes=60 * 2**20),
        cost_estimate=pl.CostEstimate(
            flops=2 * SLOTS * WIDTH * 1024 * 6,
            bytes_accessed=100_000_000,
            transcendentals=SLOTS * 1024,
        ),
    )(in_main, in_tail, cot_main, cot_tail, gate, *weights)


def weight_grads_kernel(
    links, x_ref, slot_grad_ref, grad_ref, act_ref, up_1, up_2, down_1, down_2, *theirs
):
    their_x, their_slot_grad, their_grad, their_act = theirs
    for index in range(4):
        links.arrive(index)

    def part(step, carry):
        span = pl.ds(pl.multiple_of(step * 512, 512), 512)
        for slot, up, down in ((0, up_1, down_1), (1, up_2, down_2)):
            up[span, :] = (
                lax.dot_general(
                    x_ref[:, span], grad_ref[slot], FIRST, preferred_element_type=F32
                )
                + lax.dot_general(
                    their_x[:, span], their_grad[slot], FIRST, preferred_element_type=F32
                )
            ).astype(BF)
            down[:, span] = (
                lax.dot_general(
                    act_ref[slot], slot_grad_ref[:, span], FIRST, preferred_element_type=F32
                )
                + lax.dot_general(
                    their_act[slot],
                    their_slot_grad[:, span],
                    FIRST,
                    preferred_element_type=F32,
                )
            ).astype(BF)
        return carry

    lax.fori_loop(0, 4, part, 0)


def return_rows(main, tail, x, slot_grad, grads, acts):
    whole = lambda s, me, p: s
    other = lambda s, me, p: s.at[pl.ds(2, 2)]
    return from_experts(
        main,
        tail,
        9,
        first_sends=[
            (SIBLING, ("work", 0), whole, ("scratch", 0), whole),
            (SIBLING, ("work", 1), whole, ("scratch", 1), whole),
            (SIBLING, ("work", 2), other, ("scratch", 2), whole),
            (SIBLING, ("work", 3), other, ("scratch", 3), whole),
        ],
        work=weight_grads_kernel,
        work_in=[x, slot_grad, grads, acts],
        work_out=[shape((WIDTH, 512))] * 2 + [shape((256, WIDTH))] * 2,
        work_scratch=[
            pltpu.VMEM((SLOTS, WIDTH), BF),
            pltpu.VMEM((SLOTS, WIDTH), BF),
            pltpu.VMEM((2, SLOTS, 512), BF),
            pltpu.VMEM((2, SLOTS, 256), BF),
        ],
    )


def pack_kernel(up_1, up_2, down_1, down_2, up_ref, down_ref):
    upper = lax.axis_index("row") // 2
    for which, up, down in ((upper, up_1, down_1), (1 - upper, up_2, down_2)):
        value = up[...].astype(F32)
        up_ref[which, :, 0, :] = value[:, :256]
        up_ref[which, :, 1, :] = value[:, 256:]
        down_ref[which] = down[...].astype(F32)


def pack_grads(up_1, up_2, down_1, down_2):
    steps = 8
    up, down = (WIDTH // steps, 512), (256 // steps, WIDTH)
    return pl.pallas_call(
        pack_kernel,
        grid=(steps,),
        out_shape=[shape((2, WIDTH, 2, 256), F32), shape((2, 256, WIDTH), F32)],
        in_specs=[pl.BlockSpec(up, lambda i: (i, 0))] * 2
        + [pl.BlockSpec(down, lambda i: (i, 0))] * 2,
        out_specs=[
            pl.BlockSpec((2, up[0], 2, 256), lambda i: (0, i, 0, 0)),
            pl.BlockSpec((2,) + down, lambda i: (0, i, 0)),
        ],
    )(up_1, up_2, down_1, down_2)


def dot(left, right):
    return jnp.dot(left, right, preferred_element_type=F32)


def dot_last(left, right):
    return lax.dot_general(left, right, LAST, preferred_element_type=F32)


def dot_first(left, right):
    return lax.dot_general(left, right, FIRST, preferred_element_type=F32)


def pieces(value):
    high = value.astype(BF)
    rest = value - high.astype(F32)
    middle = rest.astype(BF)
    low = (rest - middle.astype(F32)).astype(BF)
    return [high, middle, low]


def aux_rows(values, count):
    held = [jnp.stack(pieces(value), axis=1) for value in values]
    padded = [jnp.pad(rows_of, ((0, 0), (USED, 1), (0, HEAD - MAIN - TAIL))) for rows_of in held]
    width = 512 - HEAD * len(values)
    padded.append(jnp.zeros((held[0].shape[0], TAIL, width), BF))
    return jnp.concatenate(padded * count, axis=2)


def aux_value(tail, index):
    part = tail[:, USED : USED + 3, index * HEAD : index * HEAD + MAIN + TAIL]
    return jnp.sum(part.astype(F32), axis=1)


def join_values(values):
    return jnp.concatenate([values[:, :MAIN].reshape(-1), values[:, MAIN:].reshape(-1)])


def split_values(values):
    return jnp.concatenate(
        [values[: 16 * MAIN].reshape(16, MAIN), values[16 * MAIN :].reshape(16, TAIL)], axis=1
    )


FIRST_HOP = [
    ((2 * y + k) * 4 + x, (2 * y + 1 - x % 2) * 4 + 2 * k + x // 2)
    for y in range(4)
    for k in range(2)
    for x in range(4)
]
SECOND_HOP = [
    ((2 * y + k) * 4 + x, (2 * y + x % 2) * 4 + 2 * k + 1 - x // 2)
    for y in range(4)
    for k in range(2)
    for x in range(4)
]
PAIR = [(d, d ^ 1) for d in range(8)]


def hop(operand, pairs):
    return lax.ppermute(operand, ("dp", "row"), pairs)


def after(*operands):
    return lax.optimization_barrier(operands)


def inverse_pairs(pairs):
    return [(b, a) for a, b in pairs]


def shards(
    tokens,
    positions,
    routes,
    attention_norm_gain,
    experts_norm_gain,
    w_qkv,
    q_gain,
    k_gain,
    w_out,
    w_router,
    w_gate_up,
    w_down,
    cotangent,
):
    core = lax.axis_index("dp") % 2
    experts = jnp.arange(EXPERTS, dtype=jnp.int32)
    named = jnp.any(routes[:, :, None] == experts[None, None, :], axis=1)
    place = jnp.arange(512, dtype=jnp.int32)
    earlier = (place[None, :] < place[:, None]).astype(BF)
    rank = dot(earlier, named.astype(BF))
    rank = jnp.where(named, rank, -1.0).T
    (
        token_rows,
        w_group,
        position_rows,
        gain_rows,
        w_all,
        down_1,
        down_2,
        send_up_1,
        send_up_2,
        send_cot_main,
        send_cot_tail,
    ) = gather_inputs(
        tokens,
        w_qkv,
        w_out,
        w_down,
        positions.reshape(4, HEAD),
        attention_norm_gain.reshape(4, HEAD),
        [w_gate_up, rank, cotangent],
    )
    w_all = w_all.reshape(WIDTH, 512)
    w_group = w_group.reshape(WIDTH, 1536)
    gain_full = gain_rows.reshape(WIDTH)

    gate_up_1, gate_up_2 = hop(send_up_1, FIRST_HOP), hop(send_up_2, SECOND_HOP)
    sibling = lambda w: lax.ppermute(w, "dp", PAIR)
    frequency = THETA ** (-2.0 * jnp.arange(HEAD // 2, dtype=F32) / HEAD)
    half_signs = jnp.where(jnp.arange(HEAD) < HEAD // 2, -1.0, 1.0).astype(F32)
    frequency = jnp.concatenate(
        [jnp.concatenate([frequency] * 2)[None], half_signs[None], jnp.zeros((6, HEAD), F32)]
    )
    position_column = position_rows.reshape(SEQ, 1).astype(F32)
    gains = jnp.concatenate([q_gain[None], k_gain[None], jnp.zeros((6, HEAD), F32)], axis=0)

    main_pick = (
        (rank[:, None, :] == jnp.arange(MAIN, dtype=F32)[None, :, None])
        .astype(BF)
        .reshape(EXPERTS * MAIN, 512)
    )
    tail_pick = (
        (rank[:, None, :] == jnp.arange(MAIN, MAIN + TAIL, dtype=F32)[None, :, None])
        .astype(BF)
        .reshape(EXPERTS * TAIL, 512)
    )

    def pick_rows(operand):
        return (
            dot(main_pick, operand).astype(BF).reshape(EXPERTS, MAIN, 512),
            dot(tail_pick, operand).astype(BF).reshape(EXPERTS, TAIL, 512),
        )

    def place_rows(main, tail):
        return dot_first(main_pick, main.reshape(EXPERTS * MAIN, 512)) + dot_first(
            tail_pick, tail.reshape(EXPERTS * TAIL, 512)
        )

    def pick_values(values):
        return jnp.concatenate(
            [
                jnp.sum(pick.reshape(EXPERTS, -1, 512).astype(F32) * values[:, None, :], axis=2)
                for pick in (main_pick, tail_pick)
            ],
            axis=1,
        )

    def place_values(values):
        return sum(
            jnp.sum(pick.reshape(EXPERTS, -1, 512).astype(F32) * part[:, :, None], axis=1)
            for pick, part in ((main_pick, values[:, :MAIN]), (tail_pick, values[:, MAIN:]))
        )

    token_full = token_rows.astype(F32)
    inverse_attention = lax.rsqrt(jnp.mean(token_full * token_full, axis=1) + EPS)
    normed_exact = token_full * inverse_attention[:, None] * gain_full[None, :]
    normed = normed_exact.astype(BF)
    qkv = to_heads(dot(normed, w_group).astype(BF))
    cot_main, cot_tail, attended, query, key, lse, cosine, sine = attend(
        qkv, position_column, frequency, gains, send_cot_main, send_cot_tail
    )
    attended, gate_up_1, gate_up_2, down_1, down_2 = after(
        attended, gate_up_1, gate_up_2, down_1, down_2
    )
    up_ws = [gate_up_1, gate_up_2, sibling(gate_up_1), sibling(gate_up_2)]
    down_ws = [down_1, down_2, sibling(down_1), sibling(down_2)]
    attended_rows = gather_attended(attended)

    token_float = tokens.astype(F32)
    hidden = token_float + dot(attended_rows, w_all)
    scaled_hidden = hidden * experts_norm_gain
    partial_stats = jnp.concatenate(
        [
            lax.dot_general(
                w_router.astype(F32),
                scaled_hidden,
                (((0,), (1,)), ((), ())),
                precision=EXACT,
                preferred_element_type=F32,
            ),
            jnp.sum(hidden * hidden, axis=1)[None],
            jnp.zeros((7, 512), F32),
        ],
        axis=0,
    )
    stats = jnp.sum(row_stack(partial_stats, 7), axis=0)
    inverse_experts = lax.rsqrt(stats[EXPERTS] / WIDTH + EPS)
    logits = stats[:EXPERTS] * inverse_experts[None, :]
    unit_experts = hidden * inverse_experts[:, None]
    experts_input = (unit_experts * experts_norm_gain).astype(BF)
    named_t = rank >= 0
    largest = jnp.max(jnp.where(named_t, logits, -jnp.inf), axis=0, keepdims=True)
    shifted = jnp.where(named_t, jnp.exp(jnp.where(named_t, logits - largest, 0.0)), 0.0)
    gates = shifted / jnp.sum(shifted, axis=0, keepdims=True)
    slot_gates = pick_values(gates)

    send_main, send_tail = pick_rows(experts_input)
    in_main, in_tail = to_experts(
        send_main, send_tail + aux_rows([slot_gates], 1), 8
    )
    gate_of = aux_value(in_tail[:, :, :512], 0)
    gate_of = jnp.where(jnp.arange(MAIN + TAIL)[None, :] < CAP, gate_of, 0.0)
    gate_of = join_values(gate_of)[:, None]
    (
        slot_in,
        slot_grad,
        out_main,
        out_tail,
        back_main,
        back_tail,
        acts,
        gate_up_grads,
        slot_gate_grad,
        slot_inner,
    ) = run_expert(
        in_main.reshape(16 * MAIN, WIDTH),
        in_tail.reshape(16 * TAIL, WIDTH),
        cot_main.reshape(16 * MAIN, WIDTH),
        cot_tail.reshape(16 * TAIL, WIDTH),
        gate_of,
        up_ws + down_ws,
    )
    aux = aux_rows([split_values(slot_gate_grad[:, 0]), split_values(slot_inner[:, 0])], 4)
    back_main, back_tail, up_1, up_2, down_1, down_2 = return_rows(
        back_main.reshape(16, MAIN, WIDTH),
        back_tail.reshape(16, TAIL, WIDTH) + aux,
        slot_in,
        slot_grad,
        gate_up_grads,
        acts,
    )
    gate_grad = place_values(aux_value(back_tail, 0))
    inner = jnp.sum(place_values(aux_value(back_tail, 1)), axis=0)
    first_back, second_back = inverse_pairs(FIRST_HOP), inverse_pairs(SECOND_HOP)
    logit_grad = gates * (gate_grad - jnp.sum(gates * gate_grad, axis=0, keepdims=True))
    experts_input_grad = place_rows(back_main, back_tail) + lax.dot_general(
        logit_grad,
        w_router.astype(F32),
        (((0,), (1,)), ((), ())),
        precision=EXACT,
        preferred_element_type=F32,
    )
    mean_experts = (inner + jnp.sum(logit_grad * logits, axis=0)) / WIDTH
    cot_float = cotangent.astype(F32)
    middle_grad = cot_float + inverse_experts[:, None] * (
        experts_input_grad * experts_norm_gain - unit_experts * mean_experts[:, None]
    )
    router_part = lax.dot_general(
        logit_grad,
        experts_input.astype(F32),
        (((1,), (0,)), ((), ())),
        precision=EXACT,
        preferred_element_type=F32,
    )
    experts_gain_part = jnp.sum(experts_input_grad * unit_experts, axis=0)
    attended_grad = middle_grad.astype(BF)
    out_part = dot_first(attended_rows, attended_grad).astype(BF).reshape(16, HEAD, 512)
    small_part = jnp.concatenate(
        [
            router_part.reshape(256, HEAD),
            experts_gain_part.reshape(4, HEAD),
            jnp.zeros((124, HEAD), F32),
        ],
        axis=0,
    )
    grad_parts, out_other, small_other = spread_attended_grad(
        dot_last(attended_grad, w_all).astype(BF), out_part, small_part
    )
    out_half = (
        lax.dynamic_slice_in_dim(out_part, core * 64, 64, 1).astype(F32)
        + out_other.astype(F32)
    ).astype(BF)
    small = (small_part + small_other).reshape(16, 24, HEAD)
    out_main, out_tail, qkv_grad, head_gain_part = attend_back(
        [qkv, query, key, lse, grad_parts, cosine, sine, gains],
        out_main.reshape(16, MAIN, WIDTH),
        out_tail.reshape(16, TAIL, WIDTH),
    )
    qkv_grad, up_1, up_2, down_1, down_2 = after(qkv_grad, up_1, up_2, down_1, down_2)
    up_1, up_2 = hop(up_1, first_back), hop(up_2, second_back)
    down_1, down_2 = hop(down_1, first_back), hop(down_2, second_back)
    qkv_grad, output = from_heads(
        qkv_grad,
        [
            hidden,
            main_pick,
            tail_pick,
            out_main.reshape(EXPERTS * MAIN, 512),
            out_tail.reshape(EXPERTS * TAIL, 512),
        ],
    )
    normed_grad_part = dot_last(qkv_grad, w_group)
    stat_part = jnp.sum(normed_grad_part * normed_exact, axis=1)
    normed_grad, row_stats, out_pieces, small_pieces, qkv_piece = spread_features(
        normed_grad_part.astype(BF),
        jnp.concatenate([stat_part.reshape(4, HEAD), head_gain_part[:4]], axis=0),
        out_half,
        small,
        normed,
        qkv_grad,
    )
    normed_grad = jnp.sum(normed_grad.astype(F32), axis=0)
    row_stats = jnp.sum(row_stats, axis=0)
    mean_attention = row_stats[:4].reshape(512) / WIDTH
    unit_attention = token_float * inverse_attention[:, None]
    token_grad = middle_grad + inverse_attention[:, None] * (
        normed_grad * attention_norm_gain - unit_attention * mean_attention[:, None]
    )
    attention_gain_part = jnp.sum(normed_grad * unit_attention, axis=0)

    out_piece = jnp.sum(out_pieces.astype(F32), axis=0).astype(BF)
    out_total, small_total, late, qkv_total = collect_sums(
        qkv_piece,
        out_piece,
        jnp.sum(small_pieces, axis=0),
        jnp.concatenate([attention_gain_part.reshape(4, HEAD), row_stats[4:]], axis=0),
    )
    small_total = small_total.reshape(384, HEAD)
    late = jnp.sum(late, axis=0)
    grad_gate_up, grad_down = pack_grads(up_1, up_2, down_1, down_2)
    return (
        output,
        token_grad.astype(BF),
        late[:4].reshape(512),
        small_total[256:260].reshape(512),
        qkv_total.astype(F32).reshape(512, 4, 384),
        late[4],
        late[5],
        out_total.astype(F32).reshape(512, 512),
        small_total[:256].reshape(EXPERTS, 512).T,
        grad_gate_up,
        grad_down,
    )


def solution(mesh):
    tokens_like = P(("dp", "col"), "row")
    up_like = P(("dp", "col"), None, None, "row")
    down_like = P(("dp", "col"), "row", None)
    return jax.shard_map(
        shards,
        mesh=mesh,
        in_specs=(
            tokens_like,
            P("dp", "row"),
            P(("dp", "col"), None),
            P("row"),
            P("row"),
            P("row", "col", None),
            P(),
            P(),
            P("col", "row"),
            P("row", None),
            up_like,
            down_like,
            tokens_like,
        ),
        out_specs=(
            tokens_like,
            tokens_like,
            P("row"),
            P("row"),
            P("row", "col", None),
            P(),
            P(),
            P("col", "row"),
            P("row", None),
            up_like,
            down_like,
        ),
        check_vma=False,
    )
```

time: 682 us -> 582 us (0.85)
  local copies, waits for them, and re-layouts: 93.3 us -> 25.8 us
  other arithmetic: 50.1 us -> 26.3 us
  Pallas kernels: 461 us -> 478 us
  matrix products: 46.6 us -> 31 us
    reshape x17 -> x0, local copies, waits for them, and re-layouts: 28.1 us -> none  [the longest x1 7.58 us: shards(): gate_up_w = w_gate_up.reshape(2, WIDTH, 512)]
    dot_general x7 -> x3, matrix products: 19.8 us -> 8.05 us  [dot_first(): return lax.dot_general(left, right, FIRST, preferred_element_type=F32)]
    squeeze x5 -> x0, local copies, waits for them, and re-layouts: 11.5 us -> none  [the longest x2 7.64 us: shards(): own = lambda w, which: lax.dynamic_index_in_dim(w, which, 0, keepdims=False)]
    convert_element_type x7 -> x3, other arithmetic: 13 us -> 2.82 us  [the longest x1 1.87 us: shards(): main_pick = (rank[:, None, :] == jnp.arange(MAIN, dtype=F32)[None, :, Non...]
    pallas_call x0 -> x1, Pallas kernels: none -> 9.63 us  [pack_grads(): pl.pallas_call(pack_kernel, grid=(steps,), out_shape=[shape((2, WIDTH, 2,...]
    slice x8 -> x6, local copies, waits for them, and re-layouts: 8.89 us -> 0.43 us  [the longest x4 0.28 us: place_values(): values[:, MAIN:]]
    another operation x3 -> x2, local copies, waits for them, and re-layouts: 8.06 us -> 0.11 us  [the longest x1 0.11 us: aux_rows(): held = [jnp.stack(pieces(value), axis=1) for value in values]]
    unnamed x122 -> x73, local copies, waits for them, and re-layouts: 19.1 us -> 13.1 us
  transfers between devices with their start and end apart: 16 -> 10, of which waited for: 0 -> 0; matrix products, arithmetic and copies ran while one was open for 17% -> 8% of each run, Pallas kernels for 58% -> 38%
where the time goes in v2:
time: 582 us; the launch traced here: 578 us
  Pallas kernels  478 us (82%)
  matrix products  31 us (5%)
  other arithmetic  26.3 us (5%)
  local copies, waits for them, and re-layouts  25.8 us (4%)
  starting transfers between devices  15.5 us (3%)
    pallas_call x12, Pallas kernels, exchange(): pl.pallas_call(kernel, out_shape=list(outputs) + list(work_out), in_specs...  440 us
    pallas_call x1, Pallas kernels, run_expert(): pl.pallas_call(expert_kernel, out_shape=[shape((SLOTS, WIDTH)), shape((SL...  27.6 us
    unnamed x73, local copies, waits for them, and re-layouts  13.1 us
    ppermute x6, starting transfers between devices, hop(): return lax.ppermute(operand, ('dp', 'row'), pairs)  12.1 us
  transfers between devices with their start and end apart: 10, of which 0 were waited for; matrix products, arithmetic and copies ran while one was open for 8% of the time, Pallas kernels for 38%

profile of v2, /device:TPU:1, one launch (start us, length us, event | category | flops | bytes accessed | tf_op | source)
XLA Modules:
  0.0 577.8 jit_solution(12470648044296008590)
XLA Ops:
  2.4 2.8 copy.77
  5.2 61.2 %shard_map.212 = (bf16[512,2048]{1,0:T(8,128)(2,1)}, bf16[4,512,1536]{2,1,0:T(8,128)(2,1)}, s32[4,4,128]{2,1,0:T(4,128)}, f32[4,4,128]{2,1,0:T(4,128)}, bf16[4,4...) custom-call(bf16[512,512]{1,0:T(8,128)(2,1)} %refs_0_.1, ...), custom_call_target="tpu_custom_call" | custom-call | bytes 105000000 | tf_op jit(solution)/shard_map/pallas_call | solution.py:180
  67.9 3.7 collective-permute-start.1
  75.6 6.2 %convolution_convert_fusion.3.refs_0_ = bf16[512,1536]{1,0:T(8,128)(2,1)S(1)} fusion(bf16[512,2048]{1,0:T(8,128)(2,1)S(1)} %fusion.3.refs_4_, bf16[2048,1536]{1,0:T(8,128)(2,1)} %bitcast.144), kind=kOutput, calls=%fused_computation.21 | convolution fusion | flops 3222011904 | bytes 9961472 | tf_op jit(solution)/shard_map/dot_general | solution.py:1012
  81.8 21.5 %shard_map.213.refs_2_ = bf16[2048,384]{1,0:T(8,128)(2,1)S(1)} custom-call(bf16[512,1536]{1,0:T(8,128)(2,1)S(1)} %convolution_convert_fusion.3.refs_0_), custom_call_target="tpu_custom_call" | custom-call | bytes 105000000 | tf_op jit(solution)/shard_map/pallas_call | solution.py:180
  109.0 44.0 %shard_map.214 = (bf16[16,32,2048]{2,1,0:T(8,128)(2,1)}, bf16[16,8,2048]{2,1,0:T(8,128)(2,1)}, bf16[2048,128]{1,0:T(8,128)(2,1)}, bf16[2048,128]{1,0:T(8,128)(2,...) custom-call(bf16[64,32,512]{2,1,0:T(8,128)(2,1)} %get-tuple-element.78.refs_0_, ...), custom_call_target="tpu_custom_call" | custom-call | bytes 105000000 | tf_op jit(solution)/shard_map/pallas_call | solution.py:180
  155.0 30.2 %shard_map.215 = bf16[512,2048]{1,0:T(8,128)(2,1)S(1)} custom-call(bf16[2048,128]{1,0:T(8,128)(2,1)S(1)} %copy-done.6), custom_call_target="tpu_custom_call" | custom-call | bytes 105000000 | tf_op jit(solution)/shard_map/pallas_call | solution.py:180
  187.3 9.1 %shard_map.216 = f32[4,72,512]{2,1,0:T(8,128)S(1)} custom-call(f32[72,512]{1,0:T(8,128)S(1)} %maximum_maximum_fusion.1.refs_0_), custom_call_target="tpu_custom_call" | custom-call | bytes 105000000 | tf_op jit(solution)/shard_map/pallas_call | solution.py:180
  196.6 2.4 collective-permute-start.2
  203.0 41.2 %shard_map.217 = (bf16[16,32,2048]{2,1,0:T(8,128)(2,1)S(1)}, bf16[16,8,2048]{2,1,0:T(8,128)(2,1)S(1)}) custom-call(bf16[64,32,512]{2,1,0:T(8,128)(2,1)S(1)} %bitcast.100, bf16[64,8,512]{2,1,0:T(8,128)(2,1)S(1)} %fusion.22.refs_1_), custom_call_target="tpu_custom_call" | custom-call | bytes 105000000 | tf_op jit(solution)/shard_map/pallas_call | solution.py:180
  246.8 27.6 %shard_map.218 = (bf16[640,2048]{1,0:T(8,128)(2,1)}, bf16[640,2048]{1,0:T(8,128)(2,1)}, bf16[512,2048]{1,0:T(8,128)(2,1)}, bf16[128,2048]{1,0:T(8,128)(2,1)}, bf...) custom-call(bf16[512,2048]{1,0:T(8,128)(2,1)} %bitcast.102, ...), custom_call_target="tpu_custom_call" | custom-call | flops 16106127360 | bytes 100000000 | tf_op jit(solution)/shard_map/pallas_call | solution.py:891
  279.7 46.0 %shard_map.219 = (bf16[64,32,512]{2,1,0:T(8,128)(2,1)}, bf16[64,8,512]{2,1,0:T(8,128)(2,1)}, bf16[2048,512]{1,0:T(8,128)(2,1)}, bf16[2048,512]{1,0:T(8,128)(2,1)...) custom-call(bf16[16,32,2048]{2,1,0:T(8,128)(2,1)} %bitcast.105, bf16[16,8,2048]{2,1,0:T(8,128)(2,1)} %bitcast_add_fusion.refs_1_, ...), custom_call_target="tpu_custom_call" | custom-call | bytes 105000000 | tf_op jit(solution)/shard_map/pallas_call | solution.py:180
  326.9 2.6 convolution_bitcast_fusion
  332.1 4.1 fusion.16
  339.4 2.6 convolution_convert_fusion.1.refs_0_
  343.8 29.0 %shard_map.220 = (bf16[4,2048,128]{2,1,0:T(8,128)(2,1)S(1)}, bf16[16,64,512]{2,1,0:T(8,128)(2,1)S(1)}, f32[384,128]{1,0:T(8,128)S(1)}) custom-call(bf16[512,2048]{1,0:T(8,128)(2,1)S(1)} %copy-done.5, bf16[16,128,512]{2,1,0:T(8,128)(2,1)S(1)} %bitcast.98, f32[384,128]{1,0:T(8,128)S(1)} %maximum_maximum_fusion.refs_2_), custom_call_target="tpu_custom_call" | custom-call | bytes 105000000 | tf_op jit(solution)/shard_map/pallas_call | solution.py:180
  374.1 44.0 %shard_map.221 = (bf16[64,32,512]{2,1,0:T(8,128)(2,1)}, bf16[64,8,512]{2,1,0:T(8,128)(2,1)}, bf16[2048,384]{1,0:T(8,128)(2,1)}, f32[8,128]{1,0:T(8,128)}) custom-call(bf16[16,32,2048]{2,1,0:T(8,128)(2,1)} %bitcast.104, bf16[16,8,2048]{2,1,0:T(8,128)(2,1)} %bitcast.110, bf16[2048,384]{1,0:T(8,128)(2,1)} %copy-done.1, ...), custom_call_target="tpu_custom_call" | custom-call | bytes 105000000 | tf_op jit(solution)/shard_map/pallas_call | solution.py:180
  418.2 2.5 collective-permute-start.6
  425.9 25.1 %shard_map.222 = (bf16[512,1536]{1,0:T(8,128)(2,1)}, bf16[512,512]{1,0:T(8,128)(2,1)}) custom-call(bf16[2048,384]{1,0:T(8,128)(2,1)} %get-tuple-element.122.refs_0_, f32[512,512]{1,0:T(8,128)} %copy-done.9, bf16[2048,512]{1,0:T(8,128)(2,1)} %get-tuple-element.167.refs_2_, bf16[512,512]{1,0:T(8,128)(2,1)} %fusion.31.refs_3_, bf16[2048,512]{1,0:T(8,128)(2,1)} %bitcast.106, ...), custom_call_target="tpu_custom_call" | custom-call | bytes 1050000000 | tf_op jit(solution)/shard_map/pallas_call | solution.py:180
  451.0 8.1 %fusion.4 = (f32[512]{0:T(512)S(1)}, bf16[512,2048]{1,0:T(8,128)(2,1)}) fusion(bf16[512,2048]{1,0:T(8,128)(2,1)S(1)} %copy-done.13, f32[2048]{0:T(1024)S(1)} %bitcast.136, f32[512]{0:T(512)S(1)} %add_rsqrt_fusion, bf16[512,1536]{1,0:T(8,128)(2,1)} %get-tuple-element.126.refs_5_, bf16[2048,1536]{1,0:T(8,128)(2,1)} %bitcast.145), kind=kOutput, calls=%fused_computation.9 | convolution fusion | flops 3227516416 | bytes 12070912 | tf_op jit(solution)/shard_map/dot_general | solution.py:1016
  461.0 54.3 %shard_map.223 = (bf16[4,512,512]{2,1,0:T(8,128)(2,1)}, f32[4,8,128]{2,1,0:T(8,128)}, bf16[16,64,512]{2,1,0:T(8,128)(2,1)}, f32[16,24,128]{2,1,0:T(8,128)}, bf16[4,64,1536]{2,1,0:T(8,128)(2,1)}) custom-call(bf16[512,2048]{1,0:T(8,128)(2,1)} %get-tuple-element.162.refs_0_, f32[8,128]{1,0:T(8,128)} %pad_maximum_fusion.5.refs_1_, ...), custom_call_target="tpu_custom_call" | custom-call | bytes 105000000 | tf_op jit(solution)/shard_map/pallas_call | solution.py:180
  523.6 34.7 %shard_map.224 = (bf16[4,2,64,512]{3,2,1,0:T(8,128)(2,1)}, f32[16,24,128]{2,1,0:T(8,128)}, f32[32,8,128]{2,1,0:T(8,128)}, bf16[2,4,64,1536]{3,2,1,0:T(8,128)(2,1)}) custom-call(bf16[64,512]{1,0:T(8,128)(2,1)} %reduce_sum.239.refs_0_, f32[24,128]{1,0:T(8,128)} %reduce_sum.240.refs_1_, f32[8,128]{1,0:T(8,128)} %pad_maximum_fusion.6.refs_2_, ...), custom_call_target="tpu_custom_call" | custom-call | bytes 105000000 | tf_op jit(solution)/shard_map/pallas_call | solution.py:180
  558.3 4.3 reshape.587
  567.2 9.6 %shard_map.225 = (f32[2,2048,2,256]{3,2,1,0:T(2,128)}, f32[2,256,2048]{2,1,0:T(8,128)}) custom-call(bf16[2048,512]{1,0:T(8,128)(2,1)} %collective-permute-done.6.up_1, bf16[2048,512]{1,0:T(8,128)(2,1)} %collective-permute-done.7.up_2, bf16[256,2048]{1,0:T(8,128)(2,1)} %copy-done.19, bf16[256,2048]{1,0:T(8,128)(2,1)} %collective-permute-done.9.down_2), custom_call_target="tpu_custom_call" | custom-call | tf_op jit(solution)/shard_map/pallas_call | solution.py:998
  (194 shorter events, 59.3 us)
Async XLA Ops:
  0.6 185.9 %copy-start = (bf16[512,64]{0,1:T(8,128)(2,1)S(1)}, bf16[512,64]{0,1:T(8,128)(2,1)}, u32[]{:S(2)}) copy-start(bf16[512,64]{0,1:T(8,128)(2,1)} %param.22) | copy-start | bytes 196612
  66.4 7.3 %copy-start.12 = (bf16[512,2048]{1,0:T(8,128)(2,1)S(1)}, bf16[512,2048]{1,0:T(8,128)(2,1)}, u32[]{:S(2)}) copy-start(bf16[512,2048]{1,0:T(8,128)(2,1)} %get-tuple-element.80) | copy-start | bytes 6291460
  66.4 7.3 %copy-start.25 = (f32[4,4,128]{2,1,0:T(4,128)S(1)}, f32[4,4,128]{2,1,0:T(4,128)}, u32[]{:S(2)}) copy-start(f32[4,4,128]{2,1,0:T(4,128)} %get-tuple-element.81) | copy-start | bytes 24580
  66.4 87.5 %collective-permute-start = (bf16[2048,512]{1,0:T(8,128)(2,1)}, bf16[2048,512]{1,0:T(8,128)(2,1)}, u32[]{:S(2)}, u32[]{:S(2)}) collective-permute-start(bf16[2048,512]{1,0:T(8,128)(2,1)} %get-tuple-element.85), channel_id=1, source_target_pairs={{0,16},{4,0},{8,20},{12,4},{16,24},{20,8},{24,28},{28,12},{32,48},... | collective-permute-start | bytes 6291464 | tf_op jit(solution)/shard_map/ppermute | solution.py:1070
  67.9 86.0 %collective-permute-start.1 = (bf16[2048,512]{1,0:T(8,128)(2,1)}, bf16[2048,512]{1,0:T(8,128)(2,1)}, u32[]{:S(2)}, u32[]{:S(2)}) collective-permute-start(bf16[2048,512]{1,0:T(8,128)(2,1)} %get-tuple-element.86), channel_id=1, source_target_pairs={{0,4},{4,20},{8,0},{12,16},{16,12},{20,28},{24,8},{28,24},{32,36},... | collective-permute-start | bytes 6291464 | tf_op jit(solution)/shard_map/ppermute | solution.py:1070
  81.8 22.7 %copy-start.27 = (s32[4,4,128]{2,1,0:T(4,128)S(1)}, s32[4,4,128]{2,1,0:T(4,128)}, u32[]{:S(2)}) copy-start(s32[4,4,128]{2,1,0:T(4,128)} %get-tuple-element.83) | copy-start | bytes 24580
  81.8 24.4 %copy-start.10 = (f32[64,512]{1,0:T(8,128)S(1)}, f32[64,512]{1,0:T(8,128)}, u32[]{:S(2)}) copy-start(f32[64,512]{1,0:T(8,128)} %convolution_select_fusion.refs_7_) | copy-start | bytes 393220
  109.0 76.2 %copy-start.31 = (bf16[4,4,128,512]{3,2,1,0:T(8,128)(2,1)S(1)}, bf16[4,4,128,512]{3,2,1,0:T(8,128)(2,1)}, u32[]{:S(2)}) copy-start(bf16[4,4,128,512]{3,2,1,0:T(8,128)(2,1)} %get-tuple-element.90) | copy-start | bytes 6291460
  152.9 32.2 %copy-start.16 = (bf16[512,512]{1,0:T(8,128)(2,1)S(1)}, bf16[512,512]{1,0:T(8,128)(2,1)}, u32[]{:S(2)}) copy-start(bf16[512,512]{1,0:T(8,128)(2,1)} %refs_0_.1) | copy-start | bytes 1572868
  186.5 149.8 %copy-start.9 = (f32[512,512]{1,0:T(8,128)}, f32[512,512]{1,0:T(8,128)S(1)}, u32[]{:S(2)}) copy-start(f32[512,512]{1,0:T(8,128)S(1)} %get-tuple-element.182.refs_1_) | copy-start | bytes 3145732
  196.6 50.2 %collective-permute-start.2 = (bf16[2048,512]{1,0:T(8,128)(2,1)}, bf16[2048,512]{1,0:T(8,128)(2,1)}, u32[]{:S(2)}, u32[]{:S(2)}) collective-permute-start(bf16[2048,512]{1,0:T(8,128)(2,1)} %collective-permute-done.refs_5_), channel_id=1, source_target_pairs={{0,16},{16,0},{32,48},{48,32},{64,80},{80,64},{96,112},{112,96},{1... | collective-permute-start | bytes 6291464 | tf_op jit(solution)/shard_map/ppermute | solution.py:1129
  199.0 47.8 %collective-permute-start.3 = (bf16[2048,512]{1,0:T(8,128)(2,1)}, bf16[2048,512]{1,0:T(8,128)(2,1)}, u32[]{:S(2)}, u32[]{:S(2)}) collective-permute-start(bf16[2048,512]{1,0:T(8,128)(2,1)} %collective-permute-done.1.refs_6_), channel_id=1, source_target_pairs={{0,16},{16,0},{32,48},{48,32},{64,80},{80,64},{96,112},{112,96},{1... | collective-permute-start | bytes 6291464 | tf_op jit(solution)/shard_map/ppermute | solution.py:1129
  199.0 47.7 %collective-permute-start.4 = (bf16[256,2048]{1,0:T(8,128)(2,1)}, bf16[256,2048]{1,0:T(8,128)(2,1)}, u32[]{:S(2)}, u32[]{:S(2)}) collective-permute-start(bf16[256,2048]{1,0:T(8,128)(2,1)} %get-tuple-element.97.refs_9_), channel_id=1, source_target_pairs={{0,16},{16,0},{32,48},{48,32},{64,80},{80,64},{96,112},{112,96},{1... | collective-permute-start | bytes 3145736 | tf_op jit(solution)/shard_map/ppermute | solution.py:1129
  199.5 47.3 %collective-permute-start.5 = (bf16[256,2048]{1,0:T(8,128)(2,1)}, bf16[256,2048]{1,0:T(8,128)(2,1)}, u32[]{:S(2)}, u32[]{:S(2)}) collective-permute-start(bf16[256,2048]{1,0:T(8,128)(2,1)} %get-tuple-element.98.refs_10_), channel_id=1, source_target_pairs={{0,16},{16,0},{32,48},{48,32},{64,80},{80,64},{96,112},{112,96},{1... | collective-permute-start | bytes 3145736 | tf_op jit(solution)/shard_map/ppermute | solution.py:1129
  418.2 148.1 %collective-permute-start.6 = (bf16[2048,512]{1,0:T(8,128)(2,1)}, bf16[2048,512]{1,0:T(8,128)(2,1)}, u32[]{:S(2)}, u32[]{:S(2)}) collective-permute-start(bf16[2048,512]{1,0:T(8,128)(2,1)} %get-tuple-element.139), channel_id=1, source_target_pairs={{16,0},{0,4},{20,8},{4,12},{24,16},{8,20},{28,24},{12,28},{48,32},... | collective-permute-start | bytes 6291464 | tf_op jit(solution)/shard_map/ppermute | solution.py:1070
  420.7 145.6 %collective-permute-start.7 = (bf16[2048,512]{1,0:T(8,128)(2,1)}, bf16[2048,512]{1,0:T(8,128)(2,1)}, u32[]{:S(2)}, u32[]{:S(2)}) collective-permute-start(bf16[2048,512]{1,0:T(8,128)(2,1)} %get-tuple-element.140), channel_id=1, source_target_pairs={{4,0},{20,4},{0,8},{16,12},{12,16},{28,20},{8,24},{24,28},{36,32},... | collective-permute-start | bytes 6291464 | tf_op jit(solution)/shard_map/ppermute | solution.py:1070
  422.6 143.7 %collective-permute-start.8 = (bf16[256,2048]{1,0:T(8,128)(2,1)}, bf16[256,2048]{1,0:T(8,128)(2,1)S(1)}, u32[]{:S(2)}, u32[]{:S(2)}) collective-permute-start(bf16[256,2048]{1,0:T(8,128)(2,1)} %get-tuple-element.141), channel_id=1, source_target_pairs={{16,0},{0,4},{20,8},{4,12},{24,16},{8,20},{28,24},{12,28},{48,32},... | collective-permute-start | bytes 3145736 | tf_op jit(solution)/shard_map/ppermute | solution.py:1070
  423.1 143.1 %collective-permute-start.9 = (bf16[256,2048]{1,0:T(8,128)(2,1)}, bf16[256,2048]{1,0:T(8,128)(2,1)}, u32[]{:S(2)}, u32[]{:S(2)}) collective-permute-start(bf16[256,2048]{1,0:T(8,128)(2,1)} %get-tuple-element.142), channel_id=1, source_target_pairs={{4,0},{20,4},{0,8},{16,12},{12,16},{28,20},{8,24},{24,28},{36,32},... | collective-permute-start | bytes 3145736 | tf_op jit(solution)/shard_map/ppermute | solution.py:1070
  425.9 25.1 %copy-start.13 = (bf16[512,2048]{1,0:T(8,128)(2,1)S(1)}, bf16[512,2048]{1,0:T(8,128)(2,1)}, u32[]{:S(2)}) copy-start(bf16[512,2048]{1,0:T(8,128)(2,1)} %get-tuple-element.80) | copy-start | bytes 6291460
  451.0 8.1 %copy-start.28 = (f32[8,128]{1,0:T(8,128)S(1)}, f32[8,128]{1,0:T(8,128)}, u32[]{:S(2)}) copy-start(f32[8,128]{1,0:T(8,128)} %get-tuple-element.127) | copy-start | bytes 12292
  558.3 4.4 copy-start.23
  558.3 5.1 copy-start.22
  558.3 6.8 %copy-start.20 = (bf16[4,2,64,512]{3,2,1,0:T(8,128)(2,1)S(1)}, bf16[4,2,64,512]{3,2,1,0:T(8,128)(2,1)}, u32[]{:S(2)}) copy-start(bf16[4,2,64,512]{3,2,1,0:T(8,128)(2,1)} %get-tuple-element.138) | copy-start | bytes 1572868
  566.2 10.6 %copy-start.21 = (bf16[512,512]{1,0:T(8,128)(2,1)S(1)}, bf16[512,512]{1,0:T(8,128)(2,1)}, u32[]{:S(2)}) copy-start(bf16[512,512]{1,0:T(8,128)(2,1)} %get-tuple-element.199) | copy-start | bytes 1572868
  (20 other events, 44.1 us)

commit v3 on v2

--- a/solution.py
+++ b/solution.py
@@ -9,9 +9,7 @@
 HEAD = 128
 EXPERTS = 64
 CAP = 36
-MAIN = 32
-TAIL = 8
-USED = CAP - MAIN
+ROOM = 40
 SEQ = 2048
 EPS = 1e-06
 THETA = 10000.0
@@ -25,11 +23,11 @@
 SIBLING = (0, 1, 0, 0)
 PLANE = [(0, 0, i, (i + s) % 4) for s in range(4) for i in range(4) if (i, s) != (0, 0)]
 CUBE = [
-    (i, 0, (i + s) % 4, (i + t) % 4)
+    (i, 0, (i + s) % 4, (g - i) % 4)
+    for g in range(4)
     for s in range(4)
-    for t in range(4)
     for i in range(4)
-    if (i, s, t) != (0, 0, 0)
+    if (g, s, i) != (0, 0, 0)
 ]
 SOURCES = [(i, 0, 0, (i + s) % 4) for s in range(4) for i in range(4) if (i, s) != (0, 0)]
 LINES = [(d, 0, 0, 0) for d in (2, 1, 3)]
@@ -63,8 +61,8 @@
 
 
 class Links:
-    def __init__(self, send, arrive):
-        self.send, self.arrive = send, arrive
+    def __init__(self, send, arrive, ins, outs):
+        self.send, self.arrive, self.ins, self.outs = send, arrive, ins, outs
 
 
 def moved(place, offset):
@@ -152,7 +150,7 @@
             )
             copies[index].start()
 
-        links = Links(start, arrive)
+        links = Links(start, arrive, ins, outs)
         parts = work(links, *worked, *made, *refs) if stages else ()
         first = [i for i in range(n_send) if len(sends[i]) < 6 and i not in deferred]
         for index in first:
@@ -194,7 +192,7 @@
         compiler_params=pltpu.CompilerParams(
             collective_id=call_id,
             has_side_effects=True,
-            vmem_limit_bytes=(8 if work is None else 56) * 2**20,
+            vmem_limit_bytes=(8 if work is None else 60) * 2**20,
         ),
         cost_estimate=pl.CostEstimate(
             flops=0, bytes_accessed=micros * 3_500_000, transcendentals=0
@@ -227,7 +225,7 @@
         return list(range(first, len(self)))
 
 
-def early_kernel(links, up_ref, rank_ref, cot_ref, up_1, up_2, main_ref, tail_ref):
+def early_kernel(links, up_ref, rank_ref, cot_ref, up_1, up_2, rows_ref):
     upper = lax.axis_index("row") // 2
 
     def unpack(which, target):
@@ -242,13 +240,12 @@
     def pick():
         def part(step, carry):
             ranks = rank_ref[pl.ds(pl.multiple_of(step * 8, 8), 8), :]
-            slots = lax.broadcasted_iota(jnp.int32, (8, MAIN + TAIL, 512), 1).astype(F32)
-            chosen = (ranks[:, None, :] == slots).astype(F32).reshape(8 * (MAIN + TAIL), 512)
+            slots = lax.broadcasted_iota(jnp.int32, (8, ROOM, 512), 1).astype(F32)
+            chosen = (ranks[:, None, :] == slots).astype(F32).reshape(8 * ROOM, 512)
             rows_of = jnp.dot(chosen.astype(BF), cot_ref[...], preferred_element_type=F32)
-            rows_of = rows_of.reshape(8, MAIN + TAIL, 512)
-            group = pl.ds(pl.multiple_of(step * 8, 8), 8)
-            main_ref[group] = rows_of[:, :MAIN].astype(BF)
-            tail_ref[group] = rows_of[:, MAIN:].astype(BF)
+            rows_ref[pl.ds(pl.multiple_of(step * 8, 8), 8)] = rows_of.reshape(
+                8, ROOM, 512
+            ).astype(BF)
             return carry
 
         lax.fori_loop(0, EXPERTS // 8, part, 0)
@@ -371,8 +368,7 @@
         work_out=[
             shape((WIDTH, 512)),
             shape((WIDTH, 512)),
-            shape((EXPERTS, MAIN, 512)),
-            shape((EXPERTS, TAIL, 512)),
+            shape((EXPERTS, ROOM, 512)),
         ],
         stages=stages,
     )
@@ -390,58 +386,30 @@
     )[0]
 
 
-def combine_kernel(links, hidden_ref, main_pick, tail_pick, main_ref, tail_ref, out_ref):
-    total = hidden_ref[...]
-    total = total + lax.dot_general(
-        main_pick[...], main_ref[...], FIRST, preferred_element_type=F32
-    )
-    total = total + lax.dot_general(
-        tail_pick[...], tail_ref[...], FIRST, preferred_element_type=F32
-    )
-    out_ref[...] = total.astype(BF)
-
-
-def from_heads(grads, combine):
+def combine_kernel(links, hidden_ref, pick_ref, rows_ref, out_ref):
+    out_ref[...] = (
+        hidden_ref[...]
+        + lax.dot_general(pick_ref[...], rows_ref[...], FIRST, preferred_element_type=F32)
+    ).astype(BF)
+
+
+def from_heads(grads, out_part, small_part, combine):
     take = lambda s, me, p: s.at[rows(p[3] * 512, 512)]
     put = lambda o, me, p: o.at[:, rows(me[3] * 384, 384)]
     return exchange(
-        [grads],
-        [shape((512, 1536))],
-        [(offset, 0, take, 0, put) for offset in COLS],
+        [grads, out_part, small_part],
+        [shape((512, 1536)), shape((16, 64, 512)), shape(small_part.shape, F32)],
+        [(offset, 0, take, 0, put) for offset in COLS]
+        + [
+            (SIBLING, 1, lambda s, me, p: s.at[:, rows(p[1] * 64, 64)], 1, lambda o, me, p: o),
+            (SIBLING, 2, lambda s, me, p: s, 2, lambda o, me, p: o),
+        ],
         [(0, lambda s, me: take(s, me, me), 0, lambda o, me: put(o, me, me), (512, 384))],
         2,
         micros=300,
         work=combine_kernel,
         work_in=combine,
         work_out=[shape((512, 512))],
-    )
-
-
-def gather_attended(attended):
-    take = lambda s, me, p: s.at[rows(p[3] * 512, 512)]
-    put = lambda o, me, p: o.at[:, rows((me[2] * 4 + me[3]) * HEAD, HEAD)]
-    return exchange(
-        [attended],
-        [shape((512, WIDTH))],
-        [(offset, 0, take, 0, put) for offset in PLANE],
-        [(0, lambda s, me: take(s, me, me), 0, lambda o, me: put(o, me, me), (512, HEAD))],
-        3,
-    )[0]
-
-
-def spread_attended_grad(partial, out_part, small_part):
-    take = lambda s, me, p: s.at[:, rows((p[2] * 4 + p[3]) * HEAD, HEAD)]
-    put = lambda o, me, p: o.at[me[2], rows(me[3] * 512, 512)]
-    return exchange(
-        [partial, out_part, small_part],
-        [shape((4, SEQ, HEAD)), shape((16, 64, 512)), shape(small_part.shape, F32)],
-        [(offset, 0, take, 0, put) for offset in PLANE]
-        + [
-            (SIBLING, 1, lambda s, me, p: s.at[:, rows(p[1] * 64, 64)], 1, lambda o, me, p: o),
-            (SIBLING, 2, lambda s, me, p: s, 2, lambda o, me, p: o),
-        ],
-        [(0, lambda s, me: take(s, me, me), 0, lambda o, me: put(o, me, me), (512, HEAD))],
-        4,
     )
 
 
@@ -457,10 +425,26 @@
     )[0]
 
 
-def sum_weights_kernel(
-    links, first, normed_ref, grad_ref, piece_ref, their_half, came, half, spread
+def finish_kernel(
+    links,
+    numbers,
+    normed_ref,
+    grad_ref,
+    weight_ref,
+    gain_ref,
+    piece_ref,
+    feature_ref,
+    stat_ref,
+    their_half,
+    came,
+    half,
+    spread,
+    feature_part,
+    stat_part,
 ):
-    core, y = lax.axis_index("dp") % 2, lax.axis_index("dp") // 2
+    me = here()
+    y, core, row = me[0], me[1], me[2]
+    to_sibling, to_lines, to_rows, stats = numbers
 
     def product(start):
         return lax.dot_general(
@@ -469,48 +453,70 @@
 
     for r in range(4):
         their_half[r] = product(r * 512 + (1 - core) * 256).astype(BF)
-        links.send(first + r)
+        links.send(to_sibling[r])
+    inner = jnp.zeros((512, 1), F32)
+    for ahead in (2, 1, 3, 0):
+        span = rows(lax.rem(row + ahead, 4) * 512, 512)
+        part = lax.dot_general(
+            grad_ref[...], weight_ref[span, :], LAST, preferred_element_type=F32
+        )
+        inner = inner + jnp.sum(part * normed_ref[:, span].astype(F32), axis=1, keepdims=True)
+        if ahead:
+            feature_part[ahead - 1] = part.astype(BF)
+            links.send(to_rows[ahead])
+        else:
+            feature_ref[row] = part.astype(BF)
+    same = (
+        lax.broadcasted_iota(jnp.int32, (HEAD, HEAD), 0)
+        == lax.broadcasted_iota(jnp.int32, (HEAD, HEAD), 1)
+    ).astype(F32)
+    for block in range(4):
+        stat_part[block : block + 1, :] = jnp.sum(
+            same * inner[block * HEAD : (block + 1) * HEAD], axis=0, keepdims=True
+        )
+    stat_part[4:, :] = gain_ref[:4, :]
+    stat_ref[row] = stat_part[...]
+    for number in stats:
+        links.send(number)
     for r in range(4):
         mine = product(r * 512 + core * 256)
-        links.arrive(first + r)
+        links.arrive(to_sibling[r])
         half[r] = (mine + came[r].astype(F32)).astype(BF)
-        for line in range(3):
-            links.send(first + 4 + 3 * r + line)
+        for number in to_lines[r]:
+            links.send(number)
         spread[y, r] = half[r, rows(y * 64, 64), :]
     for r in range(4):
-        for line in range(3):
-            links.arrive(first + 4 + 3 * r + line)
+        for number in to_lines[r]:
+            links.arrive(number)
         total = spread[0, r].astype(F32)
         for source in range(1, 4):
             total = total + spread[source, r].astype(F32)
         piece_ref[r] = total.astype(BF)
 
 
-def spread_features(partial, stats, out_half, small, normed, grads):
-    take = lambda s, me, p: s.at[:, rows(p[2] * 512, 512)]
-    put = lambda o, me, p: o.at[me[2]]
-    whole = lambda s, me, p: s
+def finish(out_half, small, normed, grads, weights, gains):
     take_out = lambda s, me, p: s.at[p[0] * 4 + p[3]]
     put_out = lambda o, me, p: o.at[me[0] * 4 + me[3]]
-    keep = lambda i, take, put, dims: (
+    whole = lambda s, me, p: s
+    own_row = lambda o, me, p: o.at[me[2]]
+    keep = lambda i, dims: (
         i,
-        lambda s, me: take(s, me, me),
+        lambda s, me: take_out(s, me, me),
         i,
-        lambda o, me: put(o, me, me),
+        lambda o, me: put_out(o, me, me),
         dims,
     )
-    sends = (
-        [(offset, 0, take, 0, put) for offset in ROWS]
-        + [(offset, 1, whole, 1, put) for offset in ROWS]
-        + [(offset, 2, take_out, 2, put_out) for offset in SOURCES]
-        + [(offset, 3, take_out, 3, put_out) for offset in SOURCES]
-    )
-    first = len(sends)
+    sends = [(offset, 0, take_out, 0, put_out) for offset in SOURCES]
+    sends += [(offset, 1, take_out, 1, put_out) for offset in SOURCES]
+    later = len(sends)
+    to_sibling, to_lines, to_rows, stats = [], [[], [], [], []], {}, []
     for r in range(4):
         view = lambda ref, me, p, r=r: ref.at[r]
+        to_sibling.append(len(sends))
         sends.append((SIBLING, ("scratch", 0), view, ("scratch", 1), view))
     for r in range(4):
         for offset in LINES:
+            to_lines[r].append(len(sends))
             sends.append(
                 (
                     offset,
@@ -520,27 +526,31 @@
                     lambda o, me, p, r=r: o.at[me[0], r],
                 )
             )
+    for offset in ROWS:
+        ahead = offset[2]
+        to_rows[ahead] = len(sends)
+        part = lambda s, me, p, ahead=ahead: s.at[ahead - 1]
+        sends.append((offset, ("scratch", 4), part, ("made", 1), own_row))
+        stats.append(len(sends))
+        sends.append((offset, ("scratch", 5), whole, ("made", 2), own_row))
     return exchange(
-        [partial, stats, out_half, small],
-        [
-            shape((4, 512, 512)),
-            shape((4,) + stats.shape, F32),
-            shape((16, 64, 512)),
-            shape((16,) + small.shape[1:], F32),
+        [out_half, small],
+        [shape((16, 64, 512)), shape((16,) + small.shape[1:], F32)],
+        sends,
+        [keep(0, (64, 512)), keep(1, small.shape[1:])],
+        5,
+        work=lambda links, *refs: finish_kernel(
+            links, (to_sibling, to_lines, to_rows, stats), *refs
+        ),
+        work_in=[normed, grads, weights, gains],
+        work_out=[shape((4, 64, 1536)), shape((4, 512, 512)), shape((4, 8, HEAD), F32)],
+        work_scratch=[pltpu.VMEM((4, 256, 1536), BF)] * 3
+        + [
+            pltpu.VMEM((4, 4, 64, 1536), BF),
+            pltpu.VMEM((3, 512, 512), BF),
+            pltpu.VMEM((8, HEAD), F32),
         ],
-        sends,
-        [
-            keep(0, take, put, (512, 512)),
-            keep(1, whole, put, stats.shape),
-            keep(2, take_out, put_out, (64, 512)),
-            keep(3, take_out, put_out, small.shape[1:]),
-        ],
-        5,
-        work=lambda links, *refs: sum_weights_kernel(links, first, *refs),
-        work_in=[normed, grads],
-        work_out=[shape((4, 64, 1536))],
-        work_scratch=[pltpu.VMEM((4, 256, 1536), BF)] * 3 + [pltpu.VMEM((4, 4, 64, 1536), BF)],
-        deferred=range(first, len(sends)),
+        deferred=range(later, len(sends)),
     )
 
 
@@ -548,45 +558,17 @@
     return place[0] * 16 + (place[2] // 2) * 8 + place[3] * 2 + place[2] % 2
 
 
-def to_experts(main, tail, call_id, **work):
-    take = lambda s, me, p: s.at[expert_at(p)]
-    put_main = lambda o, me, p: o.at[me[0] * 4 + me[3], :, rows(me[2] * 512, 512)]
-    put_tail = lambda o, me, p: o.at[me[0] * 4 + me[3], :, rows(me[2] * 512, 512)]
-    sends = []
-    for offset in CUBE:
-        sends.append((offset, 0, take, 0, put_main))
-        sends.append((offset, 1, take, 1, put_tail))
-    return exchange(
-        [main, tail],
-        [shape((16, MAIN, WIDTH)), shape((16, TAIL, WIDTH))],
-        sends,
-        [
-            (0, lambda s, me: take(s, me, me), 0, lambda o, me: put_main(o, me, me), (MAIN, 512)),
-            (1, lambda s, me: take(s, me, me), 1, lambda o, me: put_tail(o, me, me), (TAIL, 512)),
-        ],
-        call_id,
-        **work,
-    )
-
-
-def from_experts(main, tail, call_id, first_sends=(), **work):
-    take_main = lambda s, me, p: s.at[p[0] * 4 + p[3], :, rows(p[2] * 512, 512)]
-    take_tail = lambda s, me, p: s.at[p[0] * 4 + p[3], :, rows(p[2] * 512, 512)]
-    put = lambda o, me, p: o.at[expert_at(me)]
-    sends = list(first_sends)
-    for offset in CUBE:
-        sends.append((offset, 0, take_main, 0, put))
-        sends.append((offset, 1, take_tail, 1, put))
-    return exchange(
-        [main, tail],
-        [shape((EXPERTS, MAIN, 512)), shape((EXPERTS, TAIL, 512))],
-        sends,
-        [
-            (0, lambda s, me: take_main(s, me, me), 0, lambda o, me: put(o, me, me), (MAIN, 512)),
-            (1, lambda s, me: take_tail(s, me, me), 1, lambda o, me: put(o, me, me), (TAIL, 512)),
-        ],
-        call_id,
-        **work,
+def expert_views():
+    return (
+        lambda s, me, p: s.at[expert_at(p)],
+        lambda o, me, p: o.at[me[0] * 4 + me[3], :, rows(me[2] * 512, 512)],
+    )
+
+
+def token_views():
+    return (
+        lambda s, me, p: s.at[p[0] * 4 + p[3], :, rows(p[2] * 512, 512)],
+        lambda o, me, p: o.at[expert_at(me)],
     )
 
 
@@ -674,16 +656,18 @@
 
 def attend_kernel(
     links,
+    ready,
     qkv_ref,
     position_ref,
     frequency_ref,
     gain_ref,
-    out_ref,
     query_ref,
     key_ref,
     lse_ref,
     cos_ref,
     sin_ref,
+    gathered,
+    out_ref,
 ):
     def prepare(step, carry):
         span = pl.ds(pl.multiple_of(step * BLOCK, BLOCK), BLOCK)
@@ -703,89 +687,129 @@
         return carry
 
     lax.fori_loop(0, SEQ // BLOCK, prepare, 0)
-
-    def block(step, carry):
-        span = pl.ds(pl.multiple_of(step * BLOCK, BLOCK), BLOCK)
-        scores = (
-            lax.dot_general(query_ref[span, :], key_ref[...], LAST, preferred_element_type=F32)
-            * SCALE
+    row, col = lax.axis_index("row"), lax.axis_index("col")
+    for ahead in (2, 1, 3, 0):
+        first = lax.rem(col + ahead, 4) * 512
+
+        def block(step, carry, first=first):
+            span = pl.ds(pl.multiple_of(first + step * BLOCK, BLOCK), BLOCK)
+            scores = (
+                lax.dot_general(
+                    query_ref[span, :], key_ref[...], LAST, preferred_element_type=F32
+                )
+                * SCALE
+            )
+            largest = jnp.max(scores, axis=1, keepdims=True)
+            weights = jnp.exp(scores - largest)
+            total = jnp.sum(weights, axis=1, keepdims=True)
+            mixed = jnp.dot(
+                weights.astype(BF), qkv_ref[:, 2 * HEAD :], preferred_element_type=F32
+            )
+            out_ref[span, :] = (mixed / total).astype(BF)
+            lse_ref[span, :] = largest + jnp.log(total)
+            return carry
+
+        lax.fori_loop(0, 512 // BLOCK, block, 0)
+        for number in ready[ahead]:
+            links.send(number)
+    gathered[:, rows((row * 4 + col) * HEAD, HEAD)] = out_ref[rows(col * 512, 512), :]
+
+
+def attend(qkv, position, frequency, gains, blocks):
+    take, put = expert_views()
+    sends = [(offset, 0, take, 0, put) for offset in CUBE]
+    ready = {ahead: [] for ahead in range(4)}
+    for offset in PLANE:
+        ready[offset[3]].append(len(sends))
+        sends.append(
+            (
+                offset,
+                ("scratch", 0),
+                lambda s, me, p: s.at[rows(p[3] * 512, 512)],
+                ("made", 5),
+                lambda o, me, p: o.at[:, rows((me[2] * 4 + me[3]) * HEAD, HEAD)],
+            )
         )
-        largest = jnp.max(scores, axis=1, keepdims=True)
-        weights = jnp.exp(scores - largest)
-        total = jnp.sum(weights, axis=1, keepdims=True)
-        mixed = jnp.dot(
-            weights.astype(BF), qkv_ref[:, 2 * HEAD :], preferred_element_type=F32
-        )
-        out_ref[span, :] = (mixed / total).astype(BF)
-        lse_ref[span, :] = largest + jnp.log(total)
-        return carry
-
-    lax.fori_loop(0, SEQ // BLOCK, block, 0)
-
-
-def attend(qkv, position, frequency, gains, main, tail):
-    return to_experts(
-        main,
-        tail,
+    return exchange(
+        [blocks],
+        [shape((16, ROOM, WIDTH))],
+        sends,
+        [(0, lambda s, me: take(s, me, me), 0, lambda o, me: put(o, me, me), (ROOM, 512))],
         6,
-        work=attend_kernel,
+        work=lambda links, *refs: attend_kernel(links, ready, *refs),
         work_in=[qkv, position, frequency, gains],
         work_out=[
-            shape((SEQ, HEAD)),
             shape((SEQ, HEAD)),
             shape((SEQ, HEAD)),
             shape((SEQ, 1), F32),
             shape((SEQ, HEAD), F32),
             shape((SEQ, HEAD), F32),
+            shape((512, WIDTH)),
         ],
+        work_scratch=[pltpu.VMEM((SEQ, HEAD), BF)],
+        deferred=range(len(CUBE), len(sends)),
     )
 
 
 def attend_back_kernel(
     links,
+    came,
+    later,
+    partial_ref,
     qkv_ref,
     query_ref,
     key_ref,
     lse_ref,
-    parts_ref,
     cos_ref,
     sin_ref,
     gain_ref,
     grad_ref,
     gain_grad_ref,
+    parts_ref,
     query_grad,
     key_grad,
     value_grad,
 ):
     key_grad[...] = jnp.zeros_like(key_grad)
     value_grad[...] = jnp.zeros_like(value_grad)
-
-    def block(step, carry):
-        span = pl.ds(pl.multiple_of(step * BLOCK, BLOCK), BLOCK)
-        query = query_ref[span, :]
-        out_grad = parts_ref[0, span, :].astype(F32)
-        for part in range(1, 4):
-            out_grad = out_grad + parts_ref[part, span, :].astype(F32)
-        out_grad = out_grad.astype(BF)
-        scores = (
-            lax.dot_general(query, key_ref[...], LAST, preferred_element_type=F32) * SCALE
-        )
-        soft = jnp.exp(scores - lse_ref[span, :])
-        prob_grad = lax.dot_general(
-            out_grad, qkv_ref[:, 2 * HEAD :], LAST, preferred_element_type=F32
-        )
-        inner = jnp.sum(soft * prob_grad, axis=1, keepdims=True)
-        score_grad = (soft * (prob_grad - inner)).astype(BF)
-        query_grad[span, :] = (
-            jnp.dot(score_grad, key_ref[...], preferred_element_type=F32) * SCALE
-        )
-        key_grad[...] += lax.dot_general(score_grad, query, FIRST, preferred_element_type=F32)
-        value_grad[...] += lax.dot_general(
-            soft.astype(BF), out_grad, FIRST, preferred_element_type=F32
-        )
-        return carry
-
-    lax.fori_loop(0, SEQ // BLOCK, block, 0)
+    row, col = lax.axis_index("row"), lax.axis_index("col")
+    parts_ref[row, rows(col * 512, 512), :] = partial_ref[:, rows((row * 4 + col) * HEAD, HEAD)]
+    for ahead in (0, 1, 3, 2):
+        for number in came[ahead]:
+            links.arrive(number)
+        if ahead == 3:
+            for number in later:
+                links.send(number)
+        first = lax.rem(col + ahead, 4) * 512
+
+        def block(step, carry, first=first):
+            span = pl.ds(pl.multiple_of(first + step * BLOCK, BLOCK), BLOCK)
+            query = query_ref[span, :]
+            out_grad = parts_ref[0, span, :].astype(F32)
+            for part in range(1, 4):
+                out_grad = out_grad + parts_ref[part, span, :].astype(F32)
+            out_grad = out_grad.astype(BF)
+            scores = (
+                lax.dot_general(query, key_ref[...], LAST, preferred_element_type=F32) * SCALE
+            )
+            soft = jnp.exp(scores - lse_ref[span, :])
+            prob_grad = lax.dot_general(
+                out_grad, qkv_ref[:, 2 * HEAD :], LAST, preferred_element_type=F32
+            )
+            inner = jnp.sum(soft * prob_grad, axis=1, keepdims=True)
+            score_grad = (soft * (prob_grad - inner)).astype(BF)
+            query_grad[span, :] = (
+                jnp.dot(score_grad, key_ref[...], preferred_element_type=F32) * SCALE
+            )
+            key_grad[...] += lax.dot_general(
+                score_grad, query, FIRST, preferred_element_type=F32
+            )
+            value_grad[...] += lax.dot_general(
+                soft.astype(BF), out_grad, FIRST, preferred_element_type=F32
+            )
+            return carry
+
+        lax.fori_loop(0, 512 // BLOCK, block, 0)
     gain_grad_ref[...] = jnp.zeros_like(gain_grad_ref)
 
     def finish(step, carry):
@@ -805,181 +829,252 @@
 
     lax.fori_loop(0, SEQ // BLOCK, finish, 0)
 
-def attend_back(operands, main, tail):
-    return from_experts(
-        main,
-        tail,
+
+def attend_back(operands, blocks):
+    take, put = token_views()
+    sends, came = [], {ahead: [] for ahead in range(4)}
+    for offset in PLANE:
+        came[(4 - offset[3]) % 4].append(len(sends))
+        sends.append(
+            (
+                offset,
+                ("work", 0),
+                lambda s, me, p: s.at[:, rows((p[2] * 4 + p[3]) * HEAD, HEAD)],
+                ("scratch", 0),
+                lambda o, me, p: o.at[me[2], rows(me[3] * 512, 512)],
+            )
+        )
+    later = range(len(sends), len(sends) + len(CUBE))
+    sends += [(offset, 0, take, 0, put) for offset in CUBE]
+    return exchange(
+        [blocks],
+        [shape((EXPERTS, ROOM, 512))],
+        sends,
+        [(0, lambda s, me: take(s, me, me), 0, lambda o, me: put(o, me, me), (ROOM, 512))],
         13,
-        work=attend_back_kernel,
+        deferred=later,
+        work=lambda links, *refs: attend_back_kernel(links, came, later, *refs),
         work_in=operands,
         work_out=[shape((SEQ, 3 * HEAD)), shape((8, HEAD), F32)],
-        work_scratch=[pltpu.VMEM((SEQ, HEAD), F32)] * 3,
-    )
-
-
-SLOTS = 16 * (MAIN + TAIL)
-
-
-def expert_kernel(*refs):
-    in_main, in_tail, cot_main, cot_tail, gate_ref = refs[:5]
-    weights, refs = refs[5:13], refs[13:]
-    x_ref, slot_grad_ref, out_main, out_tail, back_main, back_tail = refs[:6]
-    act_ref, grad_ref, gate_grad_ref, inner_ref = refs[6:10]
-    cot_ref, up_ref, down_ref, out_sum, back_sum, row_sem, weight_sem = refs[10:]
-    whole, first, last = pl.ds(0, SLOTS), pl.ds(0, 16 * MAIN), pl.ds(16 * MAIN, 16 * TAIL)
-    loads = [
-        pltpu.make_async_copy(source, target.at[span], row_sem.at[index])
-        for index, (source, target, span) in enumerate(
-            (
-                (in_main, x_ref, first),
-                (in_tail, x_ref, last),
-                (cot_main, cot_ref, first),
-                (cot_tail, cot_ref, last),
-            )
-        )
-    ]
+        work_scratch=[pltpu.VMEM((4, SEQ, HEAD), BF)] + [pltpu.VMEM((SEQ, HEAD), F32)] * 3,
+    )
+
+
+SLOTS = 16 * ROOM
+GROUP = 4 * ROOM
+
+
+def expert_kernel(
+    links,
+    came,
+    returns,
+    shares,
+    cot_ref,
+    gated_ref,
+    up_1,
+    up_2,
+    down_1,
+    down_2,
+    x_ref,
+    back_ref,
+    joined,
+    slot_grads,
+    acts,
+    grads,
+    their_x,
+    their_slot_grads,
+    their_acts,
+    their_grads,
+    up_ref,
+    down_ref,
+    out_sum,
+    back_sum,
+    weight_sem,
+    own_sem,
+):
+    me = here()
+    loads = []
+    for slot in range(4):
+        for part, target in ((1, up_ref), (5, down_ref)):
+            loads.append(
+                pltpu.make_async_copy(
+                    links.ins[part + slot], target.at[slot], weight_sem.at[part + slot - 1]
+                )
+            )
+    take, put = expert_views()
+    own_in = pltpu.make_async_copy(take(links.ins[0], me, me), put(x_ref, me, me), own_sem.at[0])
+    take, put = token_views()
+    own_out = pltpu.make_async_copy(
+        take(back_ref, me, me), put(links.outs[0], me, me), own_sem.at[1]
+    )
+    own_in.start()
     for load in loads:
         load.start()
-    weight_loads = []
-    for slot in range(4):
-        for part, target in ((0, up_ref), (4, down_ref)):
-            weight_loads.append(
-                pltpu.make_async_copy(
-                    weights[part + slot], target.at[slot], weight_sem.at[part + slot]
-                )
-            )
-            weight_loads[-1].start()
-    for load in loads:
-        load.wait()
-    slot_grad_ref[...] = (gate_ref[...] * cot_ref[...].astype(F32)).astype(BF)
-    for slot in range(4):
-        weight_loads[2 * slot].wait()
-        weight_loads[2 * slot + 1].wait()
-        gate_up = jnp.dot(x_ref[...], up_ref[slot], preferred_element_type=F32)
-        gate_part, up_part = gate_up[:, :256], gate_up[:, 256:]
-        sigmoid = 1.0 / (1.0 + jnp.exp(-gate_part))
-        silu = gate_part * sigmoid
-        act = (silu * up_part).astype(BF)
-        act_ref[slot] = act
-        act_grad = lax.dot_general(
-            slot_grad_ref[...], down_ref[slot], LAST, preferred_element_type=F32
-        )
-        slope = sigmoid * (1.0 + gate_part * (1.0 - sigmoid))
-        grad_ref[slot, :, :256] = (act_grad * up_part * slope).astype(BF)
-        grad_ref[slot, :, 256:] = (act_grad * silu).astype(BF)
-        out = jnp.dot(act, down_ref[slot], preferred_element_type=F32)
-        out_sum[...] = out if slot == 0 else out_sum[...] + out
-        in_grad = lax.dot_general(
-            grad_ref[slot], up_ref[slot], LAST, preferred_element_type=F32
-        )
-        back_sum[...] = in_grad if slot == 0 else back_sum[...] + in_grad
-    out = out_sum[...].astype(BF)
-    gated = (gate_ref[...] * out_sum[...]).astype(BF)
-    out_main[...] = gated[: 16 * MAIN]
-    out_tail[...] = gated[16 * MAIN :]
-    gate_grad_ref[...] = jnp.sum(
-        cot_ref[...].astype(F32) * out.astype(F32), axis=1, keepdims=True
-    )
-    inner_ref[...] = jnp.sum(back_sum[...] * x_ref[...].astype(F32), axis=1, keepdims=True)
-    in_grad = back_sum[...].astype(BF)
-    back_main[...] = in_grad[: 16 * MAIN]
-    back_tail[...] = in_grad[16 * MAIN :]
-
-
-def run_expert(in_main, in_tail, cot_main, cot_tail, gate, weights):
-    main, tail = shape((16 * MAIN, WIDTH)), shape((16 * TAIL, WIDTH))
-    return pl.pallas_call(
-        expert_kernel,
-        out_shape=[
-            shape((SLOTS, WIDTH)),
-            shape((SLOTS, WIDTH)),
-            main,
-            tail,
-            main,
-            tail,
-            shape((4, SLOTS, 256)),
-            shape((4, SLOTS, 512)),
-            shape((SLOTS, 1), F32),
-            shape((SLOTS, 1), F32),
-        ],
-        in_specs=[pl.BlockSpec(memory_space=pl.ANY)] * 4
-        + [pl.BlockSpec(memory_space=pltpu.VMEM)]
-        + [pl.BlockSpec(memory_space=pl.ANY)] * 8,
-        out_specs=[pl.BlockSpec(memory_space=pltpu.VMEM)] * 10,
-        scratch_shapes=[
-            pltpu.VMEM((SLOTS, WIDTH), BF),
-            pltpu.VMEM((4, WIDTH, 512), BF),
-            pltpu.VMEM((4, 256, WIDTH), BF),
-            pltpu.VMEM((SLOTS, WIDTH), F32),
-            pltpu.VMEM((SLOTS, WIDTH), F32),
-            pltpu.SemaphoreType.DMA((4,)),
-            pltpu.SemaphoreType.DMA((8,)),
-        ],
-        compiler_params=pltpu.CompilerParams(vmem_limit_bytes=60 * 2**20),
-        cost_estimate=pl.CostEstimate(
-            flops=2 * SLOTS * WIDTH * 1024 * 6,
-            bytes_accessed=100_000_000,
-            transcendentals=SLOTS * 1024,
-        ),
-    )(in_main, in_tail, cot_main, cot_tail, gate, *weights)
-
-
-def weight_grads_kernel(
-    links, x_ref, slot_grad_ref, grad_ref, act_ref, up_1, up_2, down_1, down_2, *theirs
-):
-    their_x, their_slot_grad, their_grad, their_act = theirs
-    for index in range(4):
-        links.arrive(index)
-
-    def part(step, carry):
+    line = lax.broadcasted_iota(jnp.int32, (ROOM, HEAD), 0)
+    lane = lax.broadcasted_iota(jnp.int32, (ROOM, HEAD), 1)
+    same = (line == lane).astype(F32)
+    for group in range(4):
+        if group == 0:
+            own_in.wait()
+        for number in came[group]:
+            links.arrive(number)
+        if group == 0:
+            for load in loads:
+                load.wait()
+        blocks = [
+            lax.rem(me[0] + 4 - i, 4) * 4 + lax.rem(me[3] + 4 - (group - i) % 4, 4)
+            for i in range(4)
+        ]
+        span = pl.ds(group * GROUP, GROUP)
+        received = jnp.concatenate([x_ref[block].astype(F32) for block in blocks], axis=0)
+        cot = jnp.concatenate([cot_ref[block].astype(F32) for block in blocks], axis=0)
+        gates = []
+        for i in range(4):
+            aux = jnp.where(line >= CAP, received[i * ROOM : (i + 1) * ROOM, :HEAD], 0.0)
+            gates.append(
+                jnp.sum(same * jnp.sum(aux, axis=0, keepdims=True), axis=1, keepdims=True)
+            )
+        gate = jnp.concatenate(gates, axis=0)
+        joined[span, :] = received.astype(BF)
+        slot_grads[span, :] = (gate * cot).astype(BF)
+        out_sum[...] = jnp.zeros_like(out_sum)
+        back_sum[...] = jnp.zeros_like(back_sum)
+
+        def quarter(slot, carry, span=span):
+            gate_up = jnp.dot(joined[span, :], up_ref[slot], preferred_element_type=F32)
+            gate_part, up_part = gate_up[:, :256], gate_up[:, 256:]
+            sigmoid = 1.0 / (1.0 + jnp.exp(-gate_part))
+            silu = gate_part * sigmoid
+            act = (silu * up_part).astype(BF)
+            acts[slot, span, :] = act
+            act_grad = lax.dot_general(
+                slot_grads[span, :], down_ref[slot], LAST, preferred_element_type=F32
+            )
+            slope = sigmoid * (1.0 + gate_part * (1.0 - sigmoid))
+            grads[slot, span, :256] = (act_grad * up_part * slope).astype(BF)
+            grads[slot, span, 256:] = (act_grad * silu).astype(BF)
+            out_sum[...] += jnp.dot(act, down_ref[slot], preferred_element_type=F32)
+            back_sum[...] += lax.dot_general(
+                grads[slot, span, :], up_ref[slot], LAST, preferred_element_type=F32
+            )
+            return carry
+
+        lax.fori_loop(0, 4, quarter, 0)
+        out = out_sum[...]
+        gated = gate * out
+        gate_grad = jnp.sum(cot * out.astype(BF).astype(F32), axis=1, keepdims=True)
+        back = back_sum[...]
+        inner = jnp.sum(back * joined[span, :].astype(F32), axis=1, keepdims=True)
+        for i, block in enumerate(blocks):
+            part = slice(i * ROOM, (i + 1) * ROOM)
+            gated_ref[block] = gated[part].astype(BF)
+            back_ref[block] = back[part].astype(BF)
+            for index, value in enumerate((gate_grad, inner)):
+                high, middle, low = pieces(jnp.sum(same * value[part], axis=0, keepdims=True))
+                aux = jnp.where(line == CAP, high.astype(F32), 0.0)
+                aux = aux + jnp.where(line == CAP + 1, middle.astype(F32), 0.0)
+                aux = aux + jnp.where(line == CAP + 2, low.astype(F32), 0.0)
+                for r in range(4):
+                    start = r * 512 + index * HEAD
+                    back_ref[block, :, start : start + HEAD] = (
+                        back[part, start : start + HEAD] + aux
+                    ).astype(BF)
+        for number in returns[group]:
+            links.send(number)
+        if group == 0:
+            own_out.start()
+        for number in shares[group]:
+            links.send(number)
+    for numbers in shares:
+        for number in numbers:
+            links.arrive(number)
+
+    def weight_grads(step, carry):
         span = pl.ds(pl.multiple_of(step * 512, 512), 512)
         for slot, up, down in ((0, up_1, down_1), (1, up_2, down_2)):
             up[span, :] = (
-                lax.dot_general(
-                    x_ref[:, span], grad_ref[slot], FIRST, preferred_element_type=F32
-                )
+                lax.dot_general(joined[:, span], grads[slot], FIRST, preferred_element_type=F32)
                 + lax.dot_general(
-                    their_x[:, span], their_grad[slot], FIRST, preferred_element_type=F32
+                    their_x[:, span], their_grads[slot], FIRST, preferred_element_type=F32
                 )
             ).astype(BF)
             down[:, span] = (
                 lax.dot_general(
-                    act_ref[slot], slot_grad_ref[:, span], FIRST, preferred_element_type=F32
+                    acts[slot], slot_grads[:, span], FIRST, preferred_element_type=F32
                 )
                 + lax.dot_general(
-                    their_act[slot],
-                    their_slot_grad[:, span],
+                    their_acts[slot],
+                    their_slot_grads[:, span],
                     FIRST,
                     preferred_element_type=F32,
                 )
             ).astype(BF)
         return carry
 
-    lax.fori_loop(0, 4, part, 0)
-
-
-def return_rows(main, tail, x, slot_grad, grads, acts):
-    whole = lambda s, me, p: s
-    other = lambda s, me, p: s.at[pl.ds(2, 2)]
-    return from_experts(
-        main,
-        tail,
-        9,
-        first_sends=[
-            (SIBLING, ("work", 0), whole, ("scratch", 0), whole),
-            (SIBLING, ("work", 1), whole, ("scratch", 1), whole),
-            (SIBLING, ("work", 2), other, ("scratch", 2), whole),
-            (SIBLING, ("work", 3), other, ("scratch", 3), whole),
-        ],
-        work=weight_grads_kernel,
-        work_in=[x, slot_grad, grads, acts],
-        work_out=[shape((WIDTH, 512))] * 2 + [shape((256, WIDTH))] * 2,
+    lax.fori_loop(0, 4, weight_grads, 0)
+    own_out.wait()
+
+
+def run_experts(blocks, cot_slots, weights):
+    take, put = expert_views()
+    came, returns, shares = ([[], [], [], []] for _ in range(3))
+    sends = []
+    for offset in CUBE:
+        came[(offset[0] + offset[3]) % 4].append(len(sends))
+        sends.append((offset, 0, take, ("scratch", 0), put))
+    take, put = token_views()
+    for offset in CUBE:
+        returns[-(offset[0] + offset[3]) % 4].append(len(sends))
+        sends.append((offset, ("scratch", 1), take, 0, put))
+    for place in range(4):
+        span = pl.ds(place * GROUP, GROUP)
+        for mine, theirs in ((2, 6), (3, 7)):
+            view = lambda ref, me, p, span=span: ref.at[span]
+            shares[place].append(len(sends))
+            sends.append((SIBLING, ("scratch", mine), view, ("scratch", theirs), view))
+        for mine, theirs in ((4, 8), (5, 9)):
+            shares[place].append(len(sends))
+            sends.append(
+                (
+                    SIBLING,
+                    ("scratch", mine),
+                    lambda ref, me, p, span=span: ref.at[pl.ds(2, 2), span],
+                    ("scratch", theirs),
+                    lambda ref, me, p, span=span: ref.at[:, span],
+                )
+            )
+    return exchange(
+        [blocks] + weights,
+        [shape((EXPERTS, ROOM, 512))],
+        sends,
+        [],
+        8,
+        work=lambda links, *refs: expert_kernel(
+            links, came, returns, shares, *refs
+        ),
+        work_in=[cot_slots],
+        work_out=[shape((16, ROOM, WIDTH))]
+        + [shape((WIDTH, 512))] * 2
+        + [shape((256, WIDTH))] * 2,
         work_scratch=[
+            pltpu.VMEM((16, ROOM, WIDTH), BF),
+            pltpu.VMEM((16, ROOM, WIDTH), BF),
             pltpu.VMEM((SLOTS, WIDTH), BF),
             pltpu.VMEM((SLOTS, WIDTH), BF),
+            pltpu.VMEM((4, SLOTS, 256), BF),
+            pltpu.VMEM((4, SLOTS, 512), BF),
+            pltpu.VMEM((SLOTS, WIDTH), BF),
+            pltpu.VMEM((SLOTS, WIDTH), BF),
+            pltpu.VMEM((2, SLOTS, 256), BF),
             pltpu.VMEM((2, SLOTS, 512), BF),
-            pltpu.VMEM((2, SLOTS, 256), BF),
+            pltpu.VMEM((4, WIDTH, 512), BF),
+            pltpu.VMEM((4, 256, WIDTH), BF),
+            pltpu.VMEM((GROUP, WIDTH), F32),
+            pltpu.VMEM((GROUP, WIDTH), F32),
+            pltpu.SemaphoreType.DMA((8,)),
+            pltpu.SemaphoreType.DMA((2,)),
         ],
+        deferred=range(len(CUBE), len(sends)),
     )
 
 
@@ -1028,27 +1123,14 @@
     return [high, middle, low]
 
 
-def aux_rows(values, count):
-    held = [jnp.stack(pieces(value), axis=1) for value in values]
-    padded = [jnp.pad(rows_of, ((0, 0), (USED, 1), (0, HEAD - MAIN - TAIL))) for rows_of in held]
-    width = 512 - HEAD * len(values)
-    padded.append(jnp.zeros((held[0].shape[0], TAIL, width), BF))
-    return jnp.concatenate(padded * count, axis=2)
-
-
-def aux_value(tail, index):
-    part = tail[:, USED : USED + 3, index * HEAD : index * HEAD + MAIN + TAIL]
+def aux_rows(value):
+    held = jnp.stack(pieces(value), axis=1)
+    return jnp.pad(held, ((0, 0), (CAP, ROOM - CAP - 3), (0, 512 - ROOM)))
+
+
+def aux_value(blocks, index):
+    part = blocks[:, CAP : CAP + 3, index * HEAD : index * HEAD + ROOM]
     return jnp.sum(part.astype(F32), axis=1)
-
-
-def join_values(values):
-    return jnp.concatenate([values[:, :MAIN].reshape(-1), values[:, MAIN:].reshape(-1)])
-
-
-def split_values(values):
-    return jnp.concatenate(
-        [values[: 16 * MAIN].reshape(16, MAIN), values[16 * MAIN :].reshape(16, TAIL)], axis=1
-    )
 
 
 FIRST_HOP = [
@@ -1110,8 +1192,7 @@
         down_2,
         send_up_1,
         send_up_2,
-        send_cot_main,
-        send_cot_tail,
+        send_cot,
     ) = gather_inputs(
         tokens,
         w_qkv,
@@ -1135,57 +1216,22 @@
     position_column = position_rows.reshape(SEQ, 1).astype(F32)
     gains = jnp.concatenate([q_gain[None], k_gain[None], jnp.zeros((6, HEAD), F32)], axis=0)
 
-    main_pick = (
-        (rank[:, None, :] == jnp.arange(MAIN, dtype=F32)[None, :, None])
-        .astype(BF)
-        .reshape(EXPERTS * MAIN, 512)
-    )
-    tail_pick = (
-        (rank[:, None, :] == jnp.arange(MAIN, MAIN + TAIL, dtype=F32)[None, :, None])
-        .astype(BF)
-        .reshape(EXPERTS * TAIL, 512)
-    )
-
-    def pick_rows(operand):
-        return (
-            dot(main_pick, operand).astype(BF).reshape(EXPERTS, MAIN, 512),
-            dot(tail_pick, operand).astype(BF).reshape(EXPERTS, TAIL, 512),
-        )
-
-    def place_rows(main, tail):
-        return dot_first(main_pick, main.reshape(EXPERTS * MAIN, 512)) + dot_first(
-            tail_pick, tail.reshape(EXPERTS * TAIL, 512)
-        )
-
-    def pick_values(values):
-        return jnp.concatenate(
-            [
-                jnp.sum(pick.reshape(EXPERTS, -1, 512).astype(F32) * values[:, None, :], axis=2)
-                for pick in (main_pick, tail_pick)
-            ],
-            axis=1,
-        )
-
-    def place_values(values):
-        return sum(
-            jnp.sum(pick.reshape(EXPERTS, -1, 512).astype(F32) * part[:, :, None], axis=1)
-            for pick, part in ((main_pick, values[:, :MAIN]), (tail_pick, values[:, MAIN:]))
-        )
+    pick = (rank[:, None, :] == jnp.arange(ROOM, dtype=F32)[None, :, None]).astype(BF)
+    flat_pick = pick.reshape(EXPERTS * ROOM, 512)
 
     token_full = token_rows.astype(F32)
     inverse_attention = lax.rsqrt(jnp.mean(token_full * token_full, axis=1) + EPS)
     normed_exact = token_full * inverse_attention[:, None] * gain_full[None, :]
     normed = normed_exact.astype(BF)
     qkv = to_heads(dot(normed, w_group).astype(BF))
-    cot_main, cot_tail, attended, query, key, lse, cosine, sine = attend(
-        qkv, position_column, frequency, gains, send_cot_main, send_cot_tail
-    )
-    attended, gate_up_1, gate_up_2, down_1, down_2 = after(
-        attended, gate_up_1, gate_up_2, down_1, down_2
+    cot_slots, query, key, lse, cosine, sine, attended_rows = attend(
+        qkv, position_column, frequency, gains, send_cot
+    )
+    attended_rows, gate_up_1, gate_up_2, down_1, down_2 = after(
+        attended_rows, gate_up_1, gate_up_2, down_1, down_2
     )
     up_ws = [gate_up_1, gate_up_2, sibling(gate_up_1), sibling(gate_up_2)]
     down_ws = [down_1, down_2, sibling(down_1), sibling(down_2)]
-    attended_rows = gather_attended(attended)
 
     token_float = tokens.astype(F32)
     hidden = token_float + dot(attended_rows, w_all)
@@ -1213,48 +1259,18 @@
     largest = jnp.max(jnp.where(named_t, logits, -jnp.inf), axis=0, keepdims=True)
     shifted = jnp.where(named_t, jnp.exp(jnp.where(named_t, logits - largest, 0.0)), 0.0)
     gates = shifted / jnp.sum(shifted, axis=0, keepdims=True)
-    slot_gates = pick_values(gates)
-
-    send_main, send_tail = pick_rows(experts_input)
-    in_main, in_tail = to_experts(
-        send_main, send_tail + aux_rows([slot_gates], 1), 8
-    )
-    gate_of = aux_value(in_tail[:, :, :512], 0)
-    gate_of = jnp.where(jnp.arange(MAIN + TAIL)[None, :] < CAP, gate_of, 0.0)
-    gate_of = join_values(gate_of)[:, None]
-    (
-        slot_in,
-        slot_grad,
-        out_main,
-        out_tail,
-        back_main,
-        back_tail,
-        acts,
-        gate_up_grads,
-        slot_gate_grad,
-        slot_inner,
-    ) = run_expert(
-        in_main.reshape(16 * MAIN, WIDTH),
-        in_tail.reshape(16 * TAIL, WIDTH),
-        cot_main.reshape(16 * MAIN, WIDTH),
-        cot_tail.reshape(16 * TAIL, WIDTH),
-        gate_of,
-        up_ws + down_ws,
-    )
-    aux = aux_rows([split_values(slot_gate_grad[:, 0]), split_values(slot_inner[:, 0])], 4)
-    back_main, back_tail, up_1, up_2, down_1, down_2 = return_rows(
-        back_main.reshape(16, MAIN, WIDTH),
-        back_tail.reshape(16, TAIL, WIDTH) + aux,
-        slot_in,
-        slot_grad,
-        gate_up_grads,
-        acts,
-    )
-    gate_grad = place_values(aux_value(back_tail, 0))
-    inner = jnp.sum(place_values(aux_value(back_tail, 1)), axis=0)
+    slot_gates = jnp.sum(pick.astype(F32) * gates[:, None, :], axis=2)
+    send_rows = dot(flat_pick, experts_input).astype(BF).reshape(EXPERTS, ROOM, 512)
+    back_rows, out_rows, up_1, up_2, down_1, down_2 = run_experts(
+        send_rows + aux_rows(slot_gates), cot_slots, up_ws + down_ws
+    )
+    gate_grad = jnp.sum(pick.astype(F32) * aux_value(back_rows, 0)[:, :, None], axis=1)
+    inner = jnp.sum(pick.astype(F32) * aux_value(back_rows, 1)[:, :, None], axis=(0, 1))
     first_back, second_back = inverse_pairs(FIRST_HOP), inverse_pairs(SECOND_HOP)
     logit_grad = gates * (gate_grad - jnp.sum(gates * gate_grad, axis=0, keepdims=True))
-    experts_input_grad = place_rows(back_main, back_tail) + lax.dot_general(
+    experts_input_grad = dot_first(
+        flat_pick, back_rows.reshape(EXPERTS * ROOM, 512)
+    ) + lax.dot_general(
         logit_grad,
         w_router.astype(F32),
         (((0,), (1,)), ((), ())),
@@ -1284,41 +1300,26 @@
         ],
         axis=0,
     )
-    grad_parts, out_other, small_other = spread_attended_grad(
-        dot_last(attended_grad, w_all).astype(BF), out_part, small_part
+    out_rows, qkv_grad, head_gain_part = attend_back(
+        [dot_last(attended_grad, w_all).astype(BF), qkv, query, key, lse, cosine, sine, gains],
+        out_rows,
+    )
+    qkv_grad, up_1, up_2, down_1, down_2 = after(qkv_grad, up_1, up_2, down_1, down_2)
+    up_1, up_2 = hop(up_1, first_back), hop(up_2, second_back)
+    down_1, down_2 = hop(down_1, first_back), hop(down_2, second_back)
+    qkv_grad, out_other, small_other, output = from_heads(
+        qkv_grad,
+        out_part,
+        small_part,
+        [hidden, flat_pick, out_rows.reshape(EXPERTS * ROOM, 512)],
     )
     out_half = (
         lax.dynamic_slice_in_dim(out_part, core * 64, 64, 1).astype(F32)
         + out_other.astype(F32)
     ).astype(BF)
     small = (small_part + small_other).reshape(16, 24, HEAD)
-    out_main, out_tail, qkv_grad, head_gain_part = attend_back(
-        [qkv, query, key, lse, grad_parts, cosine, sine, gains],
-        out_main.reshape(16, MAIN, WIDTH),
-        out_tail.reshape(16, TAIL, WIDTH),
-    )
-    qkv_grad, up_1, up_2, down_1, down_2 = after(qkv_grad, up_1, up_2, down_1, down_2)
-    up_1, up_2 = hop(up_1, first_back), hop(up_2, second_back)
-    down_1, down_2 = hop(down_1, first_back), hop(down_2, second_back)
-    qkv_grad, output = from_heads(
-        qkv_grad,
-        [
-            hidden,
-            main_pick,
-            tail_pick,
-            out_main.reshape(EXPERTS * MAIN, 512),
-            out_tail.reshape(EXPERTS * TAIL, 512),
-        ],
-    )
-    normed_grad_part = dot_last(qkv_grad, w_group)
-    stat_part = jnp.sum(normed_grad_part * normed_exact, axis=1)
-    normed_grad, row_stats, out_pieces, small_pieces, qkv_piece = spread_features(
-        normed_grad_part.astype(BF),
-        jnp.concatenate([stat_part.reshape(4, HEAD), head_gain_part[:4]], axis=0),
-        out_half,
-        small,
-        normed,
-        qkv_grad,
+    out_pieces, small_pieces, qkv_piece, normed_grad, row_stats = finish(
+        out_half, small, normed, qkv_grad, w_group, head_gain_part
     )
     normed_grad = jnp.sum(normed_grad.astype(F32), axis=0)
     row_stats = jnp.sum(row_stats, axis=0)

time: 582 us -> 533 us (0.916)
  Pallas kernels: 478 us -> 446 us
  local copies, waits for them, and re-layouts: 25.8 us -> 13.5 us
  matrix products: 31 us -> 23.7 us
    pallas_call x1 -> x0, Pallas kernels: 27.6 us -> none  [run_expert(): pl.pallas_call(expert_kernel, out_shape=[shape((SLOTS, WIDTH)), shape((SL...]
    unnamed x73 -> x62, local copies, waits for them, and re-layouts: 13.1 us -> 4.86 us
    dot_general x2 -> x1, matrix products: 10.7 us -> 2.61 us  [dot_last(): return lax.dot_general(left, right, LAST, preferred_element_type=F32)]
    pallas_call x12 -> x9, Pallas kernels: 440 us -> 436 us  [exchange(): pl.pallas_call(kernel, out_shape=list(outputs) + list(work_out), in_specs...]
    dot_general x5 -> x4, matrix products: 10.2 us -> 14.4 us  [dot(): return jnp.dot(left, right, preferred_element_type=F32)]
  transfers between devices with their start and end apart: 10 -> 10, of which waited for: 0 -> 2; matrix products, arithmetic and copies ran while one was open for 8% -> 8% of each run, Pallas kernels for 38% -> 40%
where the time goes in v3:
time: 533 us; the launch traced here: 527 us
  Pallas kernels  446 us (84%)
  other arithmetic  26.8 us (5%)
  matrix products  23.7 us (4%)
  local copies, waits for them, and re-layouts  13.5 us (3%)
  starting transfers between devices  11.4 us (2%)
    pallas_call x9, Pallas kernels, exchange(): pl.pallas_call(kernel, out_shape=list(outputs) + list(work_out), in_specs...  436 us
    dot_general x4, matrix products, dot(): return jnp.dot(left, right, preferred_element_type=F32)  14.4 us
  transfers between devices with their start and end apart: 10, of which 2 were waited for; matrix products, arithmetic and copies ran while one was open for 8% of the time, Pallas kernels for 40%

profile of v3, /device:TPU:1, one launch (start us, length us, event | category | flops | bytes accessed | tf_op | source)
XLA Modules:
  0.0 526.6 jit_solution(10848904507168893735)
XLA Ops:
  2.4 2.8 copy.47
  5.2 61.1 %shard_map.212 = (bf16[512,2048]{1,0:T(8,128)(2,1)}, bf16[4,512,1536]{2,1,0:T(8,128)(2,1)}, s32[4,4,128]{2,1,0:T(4,128)}, f32[4,4,128]{2,1,0:T(4,128)}, bf16[4,4...) custom-call(bf16[512,512]{1,0:T(8,128)(2,1)} %refs_0_.1, ...), custom_call_target="tpu_custom_call" | custom-call | bytes 105000000 | tf_op jit(solution)/shard_map/pallas_call | solution.py:178
  67.8 3.5 collective-permute-start.1
  74.0 7.0 %convolution_convert_fusion.3.refs_0_ = bf16[512,1536]{1,0:T(8,128)(2,1)S(1)} fusion(bf16[512,2048]{1,0:T(8,128)(2,1)S(1)} %fusion.7.refs_2_, bf16[2048,1536]{1,0:T(8,128)(2,1)} %bitcast.75), kind=kOutput, calls=%fused_computation.19 | convolution fusion | flops 3222011904 | bytes 9961472 | tf_op jit(solution)/shard_map/dot_general | solution.py:1107
  81.0 21.5 %shard_map.213.refs_1_.refs_2_ = bf16[2048,384]{1,0:T(8,128)(2,1)S(1)} custom-call(bf16[512,1536]{1,0:T(8,128)(2,1)S(1)} %convolution_convert_fusion.3.refs_0_), custom_call_target="tpu_custom_call" | custom-call | bytes 105000000 | tf_op jit(solution)/shard_map/pallas_call | solution.py:178
  105.4 2.9 fusion.35
  109.7 70.2 %shard_map.214 = (bf16[16,40,2048]{2,1,0:T(8,128)(2,1)}, bf16[2048,128]{1,0:T(8,128)(2,1)}, bf16[2048,128]{1,0:T(8,128)(2,1)}, f32[2048,1]{1,0:T(8,128)}, f32[20...) custom-call(bf16[64,40,512]{2,1,0:T(8,128)(2,1)} %get-tuple-element.62.refs_0_, ...), custom_call_target="tpu_custom_call" | custom-call | bytes 105000000 | tf_op jit(solution)/shard_map/pallas_call | solution.py:178
  180.0 3.6 multiply_reduce_fusion.1
  184.4 11.4 %shard_map.215 = f32[4,72,512]{2,1,0:T(8,128)S(1)} custom-call(f32[72,512]{1,0:T(8,128)S(1)} %maximum_maximum_fusion.1.refs_0_), custom_call_target="tpu_custom_call" | custom-call | bytes 105000000 | tf_op jit(solution)/shard_map/pallas_call | solution.py:178
  198.7 2.9 convolution_convert_fusion
  203.9 3.2 collective-permute-done.5.refs_8_
  207.1 80.6 %shard_map.216 = (bf16[64,40,512]{2,1,0:T(8,128)(2,1)}, bf16[16,40,2048]{2,1,0:T(8,128)(2,1)}, bf16[2048,512]{1,0:T(8,128)(2,1)}, bf16[2048,512]{1,0:T(8,128)(2,...) custom-call(bf16[64,40,512]{2,1,0:T(8,128)(2,1)} %pad_add_fusion.refs_0_, ...), custom_call_target="tpu_custom_call" | custom-call | bytes 105000000 | tf_op jit(solution)/shard_map/pallas_call | solution.py:178
  291.6 2.3 multiply_reduce_fusion
  293.9 2.6 convolution_convert_fusion.2.refs_1_
  296.5 2.6 convolution_convert_fusion.1
  299.1 69.9 %shard_map.217 = (bf16[64,40,512]{2,1,0:T(8,128)(2,1)}, bf16[2048,384]{1,0:T(8,128)(2,1)}, f32[8,128]{1,0:T(8,128)}) custom-call(bf16[16,40,2048]{2,1,0:T(8,128)(2,1)} %get-tuple-element.79.refs_0_, bf16[512,2048]{1,0:T(8,128)(2,1)} %convolution_convert_fusion.2.refs_1_, bf16[2048,384]{1,0:T(8,128)(2,1)} %copy-done.2, ...), custom_call_target="tpu_custom_call" | custom-call | bytes 105000000 | tf_op jit(solution)/shard_map/pallas_call | solution.py:178
  370.2 2.2 collective-permute-start.8
  374.4 26.7 %shard_map.218 = (bf16[512,1536]{1,0:T(8,128)(2,1)}, bf16[16,64,512]{2,1,0:T(8,128)(2,1)}, f32[384,128]{1,0:T(8,128)}, bf16[512,512]{1,0:T(8,128)(2,1)}) custom-call(bf16[2048,384]{1,0:T(8,128)(2,1)} %get-tuple-element.91.refs_0_, bf16[16,128,512]{2,1,0:T(8,128)(2,1)} %bitcast.78, f32[384,128]{1,0:T(8,128)} %maximum_maximum_fusion.refs_2_, ...), custom_call_target="tpu_custom_call" | custom-call | bytes 1050000000 | tf_op jit(solution)/shard_map/pallas_call | solution.py:178
  402.9 2.5 add_convert_fusion.refs_0_
  405.4 60.9 %shard_map.219 = (bf16[16,64,512]{2,1,0:T(8,128)(2,1)}, f32[16,24,128]{2,1,0:T(8,128)}, bf16[4,64,1536]{2,1,0:T(8,128)(2,1)}, bf16[4,512,512]{2,1,0:T(8,128)(2,1)}, f32[4,8,128]{2,1,0:T(8,128)}) custom-call(bf16[16,64,512]{2,1,0:T(8,128)(2,1)} %add_convert_fusion.refs_0_, f32[16,24,128]{2,1,0:T(8,128)} %bitcast.83, bf16[512,2048]{1,0:T(8,128)(2,1)} %copy-done.4, ...), custom_call_target="tpu_custom_call" | custom-call | bytes 105000000 | tf_op jit(solution)/shard_map/pallas_call | solution.py:178
  468.6 2.1 reduce_sum.182.refs_0_
  474.6 33.7 %shard_map.220 = (bf16[4,2,64,512]{3,2,1,0:T(8,128)(2,1)}, f32[16,24,128]{2,1,0:T(8,128)}, f32[32,8,128]{2,1,0:T(8,128)}, bf16[2,4,64,1536]{3,2,1,0:T(8,128)(2,1)}) custom-call(bf16[64,512]{1,0:T(8,128)(2,1)} %reduce_sum.182.refs_0_, f32[24,128]{1,0:T(8,128)} %reduce_sum.183.refs_1_, f32[8,128]{1,0:T(8,128)} %pad_maximum_fusion.1.refs_2_, ...), custom_call_target="tpu_custom_call" | custom-call | bytes 105000000 | tf_op jit(solution)/shard_map/pallas_call | solution.py:178
  508.4 4.3 reshape.212
  515.7 9.7 %shard_map.221 = (f32[2,2048,2,256]{3,2,1,0:T(2,128)}, f32[2,256,2048]{2,1,0:T(8,128)}) custom-call(bf16[2048,512]{1,0:T(8,128)(2,1)} %collective-permute-done.6.up_1, bf16[2048,512]{1,0:T(8,128)(2,1)} %collective-permute-done.7.up_2, bf16[256,2048]{1,0:T(8,128)(2,1)} %collective-permute-done.8.down_1, bf16[256,2048]{1,0:T(8,128)(2,1)} %collective-permute-done.9.down_2), custom_call_target="tpu_custom_call" | custom-call | tf_op jit(solution)/shard_map/pallas_call | solution.py:1093
  (134 shorter events, 34.5 us)
Async XLA Ops:
  0.6 182.9 %copy-start = (bf16[512,64]{0,1:T(8,128)(2,1)S(1)}, bf16[512,64]{0,1:T(8,128)(2,1)}, u32[]{:S(2)}) copy-start(bf16[512,64]{0,1:T(8,128)(2,1)} %param.22) | copy-start | bytes 196612
  66.3 7.2 %copy-start.5 = (bf16[512,2048]{1,0:T(8,128)(2,1)S(1)}, bf16[512,2048]{1,0:T(8,128)(2,1)}, u32[]{:S(2)}) copy-start(bf16[512,2048]{1,0:T(8,128)(2,1)} %get-tuple-element.63) | copy-start | bytes 6291460
  66.3 7.2 %copy-start.20 = (f32[4,4,128]{2,1,0:T(4,128)S(1)}, f32[4,4,128]{2,1,0:T(4,128)}, u32[]{:S(2)}) copy-start(f32[4,4,128]{2,1,0:T(4,128)} %get-tuple-element.64) | copy-start | bytes 24580
  66.3 113.6 %collective-permute-start = (bf16[2048,512]{1,0:T(8,128)(2,1)}, bf16[2048,512]{1,0:T(8,128)(2,1)}, u32[]{:S(2)}, u32[]{:S(2)}) collective-permute-start(bf16[2048,512]{1,0:T(8,128)(2,1)} %get-tuple-element.68), channel_id=1, source_target_pairs={{0,16},{4,0},{8,20},{12,4},{16,24},{20,8},{24,28},{28,12},{32,48},... | collective-permute-start | bytes 6291464 | tf_op jit(solution)/shard_map/ppermute | solution.py:1152
  67.8 112.1 %collective-permute-start.1 = (bf16[2048,512]{1,0:T(8,128)(2,1)}, bf16[2048,512]{1,0:T(8,128)(2,1)}, u32[]{:S(2)}, u32[]{:S(2)}) collective-permute-start(bf16[2048,512]{1,0:T(8,128)(2,1)} %get-tuple-element.69), channel_id=1, source_target_pairs={{0,4},{4,20},{8,0},{12,16},{16,12},{20,28},{24,8},{28,24},{32,36},... | collective-permute-start | bytes 6291464 | tf_op jit(solution)/shard_map/ppermute | solution.py:1152
  74.0 7.0 %copy-start.4 = (bf16[512,2048]{1,0:T(8,128)(2,1)}, bf16[512,2048]{1,0:T(8,128)(2,1)S(1)}, u32[]{:S(2)}) copy-start(bf16[512,2048]{1,0:T(8,128)(2,1)S(1)} %fusion.7.refs_2_) | copy-start | bytes 6291460
  81.0 22.7 %copy-start.24 = (s32[4,4,128]{2,1,0:T(4,128)S(1)}, s32[4,4,128]{2,1,0:T(4,128)}, u32[]{:S(2)}) copy-start(s32[4,4,128]{2,1,0:T(4,128)} %get-tuple-element.66) | copy-start | bytes 24580
  81.0 24.3 %copy-start.7 = (f32[64,512]{1,0:T(8,128)S(1)}, f32[64,512]{1,0:T(8,128)}, u32[]{:S(2)}) copy-start(f32[64,512]{1,0:T(8,128)} %convolution_select_fusion.refs_7_) | copy-start | bytes 393220
  109.7 70.3 %copy-start.8 = (bf16[512,512]{1,0:T(8,128)(2,1)S(1)}, bf16[512,512]{1,0:T(8,128)(2,1)}, u32[]{:S(2)}) copy-start(bf16[512,512]{1,0:T(8,128)(2,1)} %refs_0_.1) | copy-start | bytes 1572868
  183.5 108.0 %copy-start.3 = (f32[512,512]{1,0:T(8,128)}, f32[512,512]{1,0:T(8,128)S(1)}, u32[]{:S(2)}) copy-start(f32[512,512]{1,0:T(8,128)S(1)} %get-tuple-element.136.refs_3_) | copy-start | bytes 3145732
  183.5 13.5 %copy-start.9 = (bf16[256,2048]{1,0:T(8,128)(2,1)S(1)}, bf16[256,2048]{1,0:T(8,128)(2,1)}, u32[]{:S(2)}) copy-start(bf16[256,2048]{1,0:T(8,128)(2,1)} %get-tuple-element.76.refs_5_) | copy-start | bytes 3145732
  195.8 11.3 %collective-permute-start.2 = (bf16[2048,512]{1,0:T(8,128)(2,1)}, bf16[2048,512]{1,0:T(8,128)(2,1)}, u32[]{:S(2)}, u32[]{:S(2)}) collective-permute-start(bf16[2048,512]{1,0:T(8,128)(2,1)} %collective-permute-done.refs_1_), channel_id=1, source_target_pairs={{0,16},{16,0},{32,48},{48,32},{64,80},{80,64},{96,112},{112,96},{1... | collective-permute-start | bytes 6291464 | tf_op jit(solution)/shard_map/ppermute | solution.py:1210
  197.0 10.1 %collective-permute-start.3 = (bf16[2048,512]{1,0:T(8,128)(2,1)}, bf16[2048,512]{1,0:T(8,128)(2,1)}, u32[]{:S(2)}, u32[]{:S(2)}) collective-permute-start(bf16[2048,512]{1,0:T(8,128)(2,1)} %collective-permute-done.1.refs_2_), channel_id=1, source_target_pairs={{0,16},{16,0},{32,48},{48,32},{64,80},{80,64},{96,112},{112,96},{1... | collective-permute-start | bytes 6291464 | tf_op jit(solution)/shard_map/ppermute | solution.py:1210
  197.1 6.8 %collective-permute-start.4 = (bf16[256,2048]{1,0:T(8,128)(2,1)S(1)}, bf16[256,2048]{1,0:T(8,128)(2,1)}, u32[]{:S(2)}, u32[]{:S(2)}) collective-permute-start(bf16[256,2048]{1,0:T(8,128)(2,1)S(1)} %copy-done.9), channel_id=1, source_target_pairs={{0,16},{16,0},{32,48},{48,32},{64,80},{80,64},{96,112},{112,96},{1... | collective-permute-start | bytes 3145736 | tf_op jit(solution)/shard_map/ppermute | solution.py:1210
  197.6 9.5 %collective-permute-start.5 = (bf16[256,2048]{1,0:T(8,128)(2,1)}, bf16[256,2048]{1,0:T(8,128)(2,1)}, u32[]{:S(2)}, u32[]{:S(2)}) collective-permute-start(bf16[256,2048]{1,0:T(8,128)(2,1)} %get-tuple-element.77.refs_6_), channel_id=1, source_target_pairs={{0,16},{16,0},{32,48},{48,32},{64,80},{80,64},{96,112},{112,96},{1... | collective-permute-start | bytes 3145736 | tf_op jit(solution)/shard_map/ppermute | solution.py:1210
  299.1 74.5 %copy-start.19 = (f32[384]{0:T(512)S(1)}, f32[384]{0:T(512)}, u32[]{:S(2)}) copy-start(f32[384]{0:T(512)} %pad.9.clone) | copy-start | bytes 4612
  369.1 146.6 %collective-permute-start.6 = (bf16[2048,512]{1,0:T(8,128)(2,1)}, bf16[2048,512]{1,0:T(8,128)(2,1)}, u32[]{:S(2)}, u32[]{:S(2)}) collective-permute-start(bf16[2048,512]{1,0:T(8,128)(2,1)} %get-tuple-element.107), channel_id=1, source_target_pairs={{16,0},{0,4},{20,8},{4,12},{24,16},{8,20},{28,24},{12,28},{48,32},... | collective-permute-start | bytes 6291464 | tf_op jit(solution)/shard_map/ppermute | solution.py:1152
  369.1 146.5 %collective-permute-start.7 = (bf16[2048,512]{1,0:T(8,128)(2,1)}, bf16[2048,512]{1,0:T(8,128)(2,1)}, u32[]{:S(2)}, u32[]{:S(2)}) collective-permute-start(bf16[2048,512]{1,0:T(8,128)(2,1)} %get-tuple-element.108), channel_id=1, source_target_pairs={{4,0},{20,4},{0,8},{16,12},{12,16},{28,20},{8,24},{24,28},{36,32},... | collective-permute-start | bytes 6291464 | tf_op jit(solution)/shard_map/ppermute | solution.py:1152
  370.2 145.5 %collective-permute-start.8 = (bf16[256,2048]{1,0:T(8,128)(2,1)}, bf16[256,2048]{1,0:T(8,128)(2,1)}, u32[]{:S(2)}, u32[]{:S(2)}) collective-permute-start(bf16[256,2048]{1,0:T(8,128)(2,1)} %get-tuple-element.109), channel_id=1, source_target_pairs={{16,0},{0,4},{20,8},{4,12},{24,16},{8,20},{28,24},{12,28},{48,32},... | collective-permute-start | bytes 3145736 | tf_op jit(solution)/shard_map/ppermute | solution.py:1152
  372.4 143.3 %collective-permute-start.9 = (bf16[256,2048]{1,0:T(8,128)(2,1)}, bf16[256,2048]{1,0:T(8,128)(2,1)}, u32[]{:S(2)}, u32[]{:S(2)}) collective-permute-start(bf16[256,2048]{1,0:T(8,128)(2,1)} %get-tuple-element.110), channel_id=1, source_target_pairs={{4,0},{20,4},{0,8},{16,12},{12,16},{28,20},{8,24},{24,28},{36,32},... | collective-permute-start | bytes 3145736 | tf_op jit(solution)/shard_map/ppermute | solution.py:1152
  374.4 28.5 %copy-start.6 = (bf16[2048,512]{1,0:T(8,128)(2,1)S(1)}, bf16[2048,512]{1,0:T(8,128)(2,1)}, u32[]{:S(2)}) copy-start(bf16[2048,512]{1,0:T(8,128)(2,1)} %convolution_convert_fusion.1) | copy-start | bytes 6291460
  508.3 6.2 %copy-start.13 = (bf16[4,2,64,512]{3,2,1,0:T(8,128)(2,1)S(1)}, bf16[4,2,64,512]{3,2,1,0:T(8,128)(2,1)}, u32[]{:S(2)}) copy-start(bf16[4,2,64,512]{3,2,1,0:T(8,128)(2,1)} %get-tuple-element.106) | copy-start | bytes 1572868
  515.7 9.7 %copy-start.14 = (bf16[512,512]{1,0:T(8,128)(2,1)S(1)}, bf16[512,512]{1,0:T(8,128)(2,1)}, u32[]{:S(2)}) copy-start(bf16[512,512]{1,0:T(8,128)(2,1)} %get-tuple-element.150) | copy-start | bytes 1572868
  515.7 10.5 %copy-start.1 = (bf16[512,64]{0,1:T(8,128)(2,1)S(1)}, bf16[512,64]{0,1:T(8,128)(2,1)}, u32[]{:S(2)}) copy-start(bf16[512,64]{0,1:T(8,128)(2,1)} %param.22) | copy-start | bytes 196612
  (16 other events, 52.2 us)

commit v4 on v3

--- a/solution.py
+++ b/solution.py
@@ -30,6 +30,7 @@
     if (g, s, i) != (0, 0, 0)
 ]
 SOURCES = [(i, 0, 0, (i + s) % 4) for s in range(4) for i in range(4) if (i, s) != (0, 0)]
+SIDES = [(i, 0, (i + s) % 4, 0) for s in range(4) for i in range(4) if (i, s) != (0, 0)]
 LINES = [(d, 0, 0, 0) for d in (2, 1, 3)]
 OTHERS = [
     (a, k, 0, d) for a in range(4) for k in range(2) for d in range(4) if (a, k, d) != (0, 0, 0)
@@ -58,6 +59,9 @@
     lambda p: (p[0], p[2] % 2, 2 * p[1] + 1 - p[2] // 2, p[3]),
     lambda p: (p[0], p[2] // 2, 2 * (1 - p[2] % 2) + p[1], p[3]),
 )
+
+
+ONE_BACK, OTHER_BACK = Hop(ONE_WAY.origin, ONE_WAY.to), Hop(OTHER_WAY.origin, OTHER_WAY.to)
 
 
 class Links:
@@ -228,29 +232,28 @@
 def early_kernel(links, up_ref, rank_ref, cot_ref, up_1, up_2, rows_ref):
     upper = lax.axis_index("row") // 2
 
-    def unpack(which, target):
-        def part(step, carry):
-            span = pl.ds(pl.multiple_of(step * 256, 256), 256)
-            target[span, :256] = up_ref[which, span, 0, :]
-            target[span, 256:] = up_ref[which, span, 1, :]
-            return carry
-
-        return lambda: lax.fori_loop(0, WIDTH // 256, part, 0)
-
-    def pick():
-        def part(step, carry):
-            ranks = rank_ref[pl.ds(pl.multiple_of(step * 8, 8), 8), :]
+    def unpack(which, target, first):
+        def part():
+            for step in range(4):
+                span = pl.ds(first + step * 64, 64)
+                target[span, :256] = up_ref[which, span, 0, :]
+                target[span, 256:] = up_ref[which, span, 1, :]
+
+        return part
+
+    def pick(step):
+        def part():
+            ranks = rank_ref[step * 8 : step * 8 + 8, :]
             slots = lax.broadcasted_iota(jnp.int32, (8, ROOM, 512), 1).astype(F32)
             chosen = (ranks[:, None, :] == slots).astype(F32).reshape(8 * ROOM, 512)
             rows_of = jnp.dot(chosen.astype(BF), cot_ref[...], preferred_element_type=F32)
-            rows_ref[pl.ds(pl.multiple_of(step * 8, 8), 8)] = rows_of.reshape(
-                8, ROOM, 512
-            ).astype(BF)
-            return carry
-
-        lax.fori_loop(0, EXPERTS // 8, part, 0)
-
-    return [unpack(upper, up_1), unpack(1 - upper, up_2), pick]
+            rows_ref[pl.ds(step * 8, 8)] = rows_of.reshape(8, ROOM, 512).astype(BF)
+
+        return part
+
+    parts = [unpack(upper, up_1, step * 256) for step in range(8)]
+    parts += [unpack(1 - upper, up_2, step * 256) for step in range(8)]
+    return parts + [pick(step) for step in range(8)]
 
 
 def gather_inputs(tokens, w_qkv, w_out, w_down, small_int, small_float, early):
@@ -273,25 +276,28 @@
         lambda o, me, p: o.at[me[2], eighth(64), own_cols(me)],
         1,
     )
-    sends.add(ROWS, lambda s, me, p: s, 0, lambda o, me, p: o.at[:, rows(me[2] * 512, 512)], 0)
+    both = [(0, 0, 1, 0), (0, 0, 3, 0)]
+    beside = sends.add(
+        both, lambda s, me, p: s, 0, lambda o, me, p: o.at[:, rows(me[2] * 512, 512)], 0
+    )
     sends.add(ROWS, lambda s, me, p: s, 2, lambda o, me, p: o.at[me[2]], 2)
     sends.add(ROWS, lambda s, me, p: s, 3, lambda o, me, p: o.at[me[2]], 3)
     sends.append((ONE_WAY, 5, lambda s, me, p: s.at[me[2] // 2], 5, lambda o, me, p: o))
     sends.append((OTHER_WAY, 5, lambda s, me, p: s.at[1 - me[2] // 2], 6, lambda o, me, p: o))
     out_z = sends.add(COLS, lambda o, me: o.at[low, me[3], eighth(16)], 4, needs=[-2])
     out_y = sends.add(LINES, lambda o, me: o.at[high, me[3], eighth(16)], 4, needs=[-2])
-    stages = [len(sends)]
+    stages = [len(sends)] * 3
     by_z = sends.add(
         COLS, lambda o, me: o.at[low, eighth(64), own_cols(me)], 1, needs=[-1] + first
     )
     by_y = sends.add(LINES, lambda o, me: o.at[high, eighth(64), own_cols(me)], 1, needs=first)
     sends.add(LINES, lambda o, me: o.at[low, eighth(64), own_cols(me)], 1, needs=first)
     sends.add(COLS, lambda o, me: o.at[high, eighth(64), own_cols(me)], 1, needs=first)
-    stages.append(len(sends))
     last_z, last_y = {0: [len(sends) - 6 + i for i in range(3)]}, {0: list(range(len(sends) - 3, len(sends)))}
     for d in (1, 3, 2):
         came = by_z[[offset[3] for offset in COLS].index(d)]
         cols = lambda me, d=d: rows((me[3] + 4 - d) % 4 * 384, 384)
+        stages += [len(sends)] * (3 if d == 1 else 1)
         last_z[d] = sends.add(
             LINES,
             lambda o, me, cols=cols: o.at[low, eighth(64), cols(me)],
@@ -300,13 +306,21 @@
         )
         came = by_y[[offset[0] for offset in LINES].index(d)]
         span = lambda me, d=d: rows((me[1] * 4 + (me[0] + 4 - d) % 4) * 64, 64)
+        stages.append(len(sends))
         last_y[d] = sends.add(
             COLS,
             lambda o, me, span=span: o.at[high, span(me), own_cols(me)],
             1,
             needs=[came],
         )
+    for index, offset in enumerate(both):
+        passed = lambda o, me, index=index, d=offset[2]: o.at[
+            pl.ds(index * 256, 256), rows((me[2] + 4 - d) % 4 * 512, 512)
+        ]
+        sends.add([offset], passed, 0, needs=[beside[index]])
+    stages.append(len(sends))
     out_zy = sends.add(LINES, lambda o, me: o.at[low, :, eighth(16)], 4, needs=out_z)
+    stages.append(len(sends))
     out_yz = sends.add(COLS, lambda o, me: o.at[high, me[3], half(64)], 4, needs=out_y)
     stages.append(len(sends))
     pair = [SIBLING]
@@ -314,6 +328,7 @@
     sends.add(pair, lambda o, me: o.at[high, half(256), own_cols(me)], 1, needs=by_y)
     for d in (1, 3, 2):
         line = [offset[0] for offset in LINES].index(d)
+        stages += [len(sends)] * (4 if d == 1 else 2)
         span = lambda me, d=d: rows((me[1] * 4 + (me[0] + 4 - d) % 4) * 64, 64)
         sends.add(
             pair,
@@ -322,6 +337,7 @@
             needs=[numbers[line] for numbers in last_z.values()],
         )
         col = [offset[3] for offset in COLS].index(d)
+        stages += [len(sends)] * (24 - len(stages) if d == 2 else 1)
         cols = lambda me, d=d: rows((me[3] + 4 - d) % 4 * 384, 384)
         sends.add(
             pair,
@@ -386,33 +402,6 @@
     )[0]
 
 
-def combine_kernel(links, hidden_ref, pick_ref, rows_ref, out_ref):
-    out_ref[...] = (
-        hidden_ref[...]
-        + lax.dot_general(pick_ref[...], rows_ref[...], FIRST, preferred_element_type=F32)
-    ).astype(BF)
-
-
-def from_heads(grads, out_part, small_part, combine):
-    take = lambda s, me, p: s.at[rows(p[3] * 512, 512)]
-    put = lambda o, me, p: o.at[:, rows(me[3] * 384, 384)]
-    return exchange(
-        [grads, out_part, small_part],
-        [shape((512, 1536)), shape((16, 64, 512)), shape(small_part.shape, F32)],
-        [(offset, 0, take, 0, put) for offset in COLS]
-        + [
-            (SIBLING, 1, lambda s, me, p: s.at[:, rows(p[1] * 64, 64)], 1, lambda o, me, p: o),
-            (SIBLING, 2, lambda s, me, p: s, 2, lambda o, me, p: o),
-        ],
-        [(0, lambda s, me: take(s, me, me), 0, lambda o, me: put(o, me, me), (512, 384))],
-        2,
-        micros=300,
-        work=combine_kernel,
-        work_in=combine,
-        work_out=[shape((512, 512))],
-    )
-
-
 def row_stack(operand, call_id):
     take = lambda s, me, p: s
     put = lambda o, me, p: o.at[me[2]]
@@ -432,19 +421,27 @@
     grad_ref,
     weight_ref,
     gain_ref,
-    piece_ref,
+    hidden_ref,
+    pick_ref,
+    rows_ref,
+    by_y_ref,
+    by_z_ref,
     feature_ref,
     stat_ref,
+    out_ref,
     their_half,
     came,
     half,
-    spread,
+    spread_y,
+    spread_z,
     feature_part,
     stat_part,
+    feature_sum,
+    passing,
 ):
     me = here()
-    y, core, row = me[0], me[1], me[2]
-    to_sibling, to_lines, to_rows, stats = numbers
+    y, core, row, col = me
+    to_sibling, to_lines, to_cols, to_rows, last = numbers
 
     def product(start):
         return lax.dot_general(
@@ -461,11 +458,20 @@
             grad_ref[...], weight_ref[span, :], LAST, preferred_element_type=F32
         )
         inner = inner + jnp.sum(part * normed_ref[:, span].astype(F32), axis=1, keepdims=True)
-        if ahead:
-            feature_part[ahead - 1] = part.astype(BF)
-            links.send(to_rows[ahead])
+        if ahead == 2:
+            feature_part[1] = part.astype(BF)
+            for number in to_rows[2]:
+                links.send(number)
+        elif ahead:
+            feature_sum[ahead // 2] = part
         else:
-            feature_ref[row] = part.astype(BF)
+            feature_ref[0] = part.astype(BF)
+    for index, ahead in enumerate((1, 3)):
+        links.arrive(to_rows[2][index])
+        part = slice(index * 256, (index + 1) * 256)
+        feature_sum[index, part, :] += passing[index].astype(F32)
+        feature_part[ahead - 1] = feature_sum[index].astype(BF)
+        links.send(to_rows[ahead])
     same = (
         lax.broadcasted_iota(jnp.int32, (HEAD, HEAD), 0)
         == lax.broadcasted_iota(jnp.int32, (HEAD, HEAD), 1)
@@ -476,25 +482,34 @@
         )
     stat_part[4:, :] = gain_ref[:4, :]
     stat_ref[row] = stat_part[...]
-    for number in stats:
+    for number in last:
         links.send(number)
     for r in range(4):
         mine = product(r * 512 + core * 256)
         links.arrive(to_sibling[r])
         half[r] = (mine + came[r].astype(F32)).astype(BF)
-        for number in to_lines[r]:
+        for number in to_lines[r] + to_cols[r]:
             links.send(number)
-        spread[y, r] = half[r, rows(y * 64, 64), :]
+        spread_y[y, r] = half[r, rows(y * 32, 32), :]
+        spread_z[col, r] = half[r, 128:, rows(col * 384, 384)]
+    out_ref[...] = (
+        hidden_ref[...]
+        + lax.dot_general(pick_ref[...], rows_ref[...], FIRST, preferred_element_type=F32)
+    ).astype(BF)
     for r in range(4):
-        for number in to_lines[r]:
-            links.arrive(number)
-        total = spread[0, r].astype(F32)
-        for source in range(1, 4):
-            total = total + spread[source, r].astype(F32)
-        piece_ref[r] = total.astype(BF)
-
-
-def finish(out_half, small, normed, grads, weights, gains):
+        for numbers_of, target, spread in (
+            (to_lines, by_y_ref, spread_y),
+            (to_cols, by_z_ref, spread_z),
+        ):
+            for number in numbers_of[r]:
+                links.arrive(number)
+            total = spread[0, r].astype(F32)
+            for source in range(1, 4):
+                total = total + spread[source, r].astype(F32)
+            target[r] = total.astype(BF)
+
+
+def finish(out_half, small, down_1, down_2, operands):
     take_out = lambda s, me, p: s.at[p[0] * 4 + p[3]]
     put_out = lambda o, me, p: o.at[me[0] * 4 + me[3]]
     whole = lambda s, me, p: s
@@ -509,7 +524,8 @@
     sends = [(offset, 0, take_out, 0, put_out) for offset in SOURCES]
     sends += [(offset, 1, take_out, 1, put_out) for offset in SOURCES]
     later = len(sends)
-    to_sibling, to_lines, to_rows, stats = [], [[], [], [], []], {}, []
+    to_sibling, to_lines, to_cols = [], [[], [], [], []], [[], [], [], []]
+    to_rows, last = {}, []
     for r in range(4):
         view = lambda ref, me, p, r=r: ref.at[r]
         to_sibling.append(len(sends))
@@ -521,34 +537,64 @@
                 (
                     offset,
                     ("scratch", 2),
-                    lambda s, me, p, r=r: s.at[r, rows(p[0] * 64, 64)],
+                    lambda s, me, p, r=r: s.at[r, rows(p[0] * 32, 32)],
                     ("scratch", 3),
                     lambda o, me, p, r=r: o.at[me[0], r],
                 )
             )
+        for offset in COLS:
+            to_cols[r].append(len(sends))
+            sends.append(
+                (
+                    offset,
+                    ("scratch", 2),
+                    lambda s, me, p, r=r: s.at[r, pl.ds(128, 128), rows(p[3] * 384, 384)],
+                    ("scratch", 4),
+                    lambda o, me, p, r=r: o.at[me[3], r],
+                )
+            )
+    to_rows[2] = [len(sends), len(sends) + 1]
+    for index, offset in enumerate(((0, 0, 1, 0), (0, 0, 3, 0))):
+        part = lambda s, me, p, index=index: s.at[1, pl.ds(index * 256, 256)]
+        slot = lambda o, me, p, index=index: o.at[index]
+        sends.append((offset, ("scratch", 5), part, ("scratch", 8), slot))
+    for index, offset in enumerate(((0, 0, 1, 0), (0, 0, 3, 0))):
+        to_rows[offset[2]] = len(sends)
+        part = lambda s, me, p, ahead=offset[2]: s.at[ahead - 1]
+        slot = lambda o, me, p, index=index: o.at[1 + index]
+        sends.append((offset, ("scratch", 5), part, ("made", 2), slot))
     for offset in ROWS:
-        ahead = offset[2]
-        to_rows[ahead] = len(sends)
-        part = lambda s, me, p, ahead=ahead: s.at[ahead - 1]
-        sends.append((offset, ("scratch", 4), part, ("made", 1), own_row))
-        stats.append(len(sends))
-        sends.append((offset, ("scratch", 5), whole, ("made", 2), own_row))
+        last.append(len(sends))
+        sends.append((offset, ("scratch", 6), whole, ("made", 3), own_row))
+    for way, index in ((ONE_BACK, 2), (OTHER_BACK, 3)):
+        last.append(len(sends))
+        sends.append((way, index, whole, index, whole))
     return exchange(
-        [out_half, small],
-        [shape((16, 64, 512)), shape((16,) + small.shape[1:], F32)],
+        [out_half, small, down_1, down_2],
+        [shape((16, 64, 512)), shape((16,) + small.shape[1:], F32)]
+        + [shape(down_1.shape)] * 2,
         sends,
         [keep(0, (64, 512)), keep(1, small.shape[1:])],
         5,
         work=lambda links, *refs: finish_kernel(
-            links, (to_sibling, to_lines, to_rows, stats), *refs
+            links, (to_sibling, to_lines, to_cols, to_rows, last), *refs
         ),
-        work_in=[normed, grads, weights, gains],
-        work_out=[shape((4, 64, 1536)), shape((4, 512, 512)), shape((4, 8, HEAD), F32)],
+        work_in=operands,
+        work_out=[
+            shape((4, 32, 1536)),
+            shape((4, 128, 384)),
+            shape((3, 512, 512)),
+            shape((4, 8, HEAD), F32),
+            shape((512, 512)),
+        ],
         work_scratch=[pltpu.VMEM((4, 256, 1536), BF)] * 3
         + [
-            pltpu.VMEM((4, 4, 64, 1536), BF),
+            pltpu.VMEM((4, 4, 32, 1536), BF),
+            pltpu.VMEM((4, 4, 128, 384), BF),
             pltpu.VMEM((3, 512, 512), BF),
             pltpu.VMEM((8, HEAD), F32),
+            pltpu.VMEM((2, 512, 512), F32),
+            pltpu.VMEM((2, 256, 512), BF),
         ],
         deferred=range(later, len(sends)),
     )
@@ -572,8 +618,8 @@
     )
 
 
-def collect_sums(qkv_piece, out_piece, small_piece, late):
-    put_qkv = lambda o, me, p: o.at[me[1], me[0]]
+def collect_sums(by_y, by_z, out_piece, small_piece, late, up_grad):
+    put_qkv = lambda o, me, p: o.at[me[1], :, me[0]]
     put_out = lambda o, me, p: o.at[me[0], me[1]]
     put_small = lambda o, me, p: o.at[me[0] * 4 + me[3]]
     put_late = lambda o, me, p: o.at[(me[0] * 2 + me[1]) * 4 + me[3]]
@@ -586,13 +632,21 @@
         lambda o, me, p: o.at[me[3], me[2]],
         ("work", 0),
     )
+    heads += sends.add(
+        SIDES,
+        lambda s, me, p: s.at[p[2], rows(p[0] * 32, 32)],
+        ("scratch", 1),
+        lambda o, me, p: o.at[me[0], me[2]],
+        ("work", 1),
+    )
     out_sent = sends.add(LINES, whole, 0, put_out, 0)
     sends.add([SIBLING], whole, 0, put_out, 0)
     sends.add(SOURCES, whole, 1, put_small, 1)
     sends.add(OTHERS, whole, 2, put_late, 2)
+    sends.add([OTHER_BACK], whole, 3, whole, 3)
     later = len(sends)
-    qkv_sent = sends.add(LINES, whole, ("made", 0), put_qkv, ("scratch", 1))
-    sends.add([SIBLING], whole, ("made", 0), put_qkv, ("scratch", 1))
+    qkv_sent = sends.add(LINES, whole, ("made", 0), put_qkv, ("scratch", 2))
+    sends.add([SIBLING], whole, ("made", 0), put_qkv, ("scratch", 2))
     relays = []
     for index in (1, 2, 0):
         origin = lambda me, d=LINES[index][0]: (me[0] + 4 - d) % 4
@@ -601,33 +655,37 @@
         sends.append((SIBLING, 0, view, 0, view, [out_sent[index]]))
     for index in (1, 2, 0):
         origin = lambda me, d=LINES[index][0]: (me[0] + 4 - d) % 4
-        view = lambda ref, me, p, origin=origin: ref.at[me[1], origin(me)]
+        view = lambda ref, me, p, origin=origin: ref.at[me[1], :, origin(me)]
         relays.append((qkv_sent[index], len(sends)))
         sends.append((SIBLING, ("made", 0), view, ("made", 0), view, [qkv_sent[index]]))
 
-    def work(links, piece_ref, total_ref, spread, mine):
-        group, row, col = lax.axis_index("dp"), lax.axis_index("row"), lax.axis_index("col")
-        spread[col, row] = piece_ref[row, :, rows(col * 384, 384)]
+    def work(links, by_y_ref, by_z_ref, total_ref, spread_z, spread_y, mine):
+        me = here()
+        spread_z[me[3], me[2]] = by_y_ref[me[2], :, rows(me[3] * 384, 384)]
+        spread_y[me[0], me[2]] = by_z_ref[me[2], rows(me[0] * 32, 32), :]
         for number in heads:
             links.arrive(number)
-        for head in range(4):
-            total = spread[0, head].astype(F32)
-            for source in range(1, 4):
-                total = total + spread[source, head].astype(F32)
-            mine[:, head * 384 : (head + 1) * 384] = total.astype(BF)
+        for part, spread in ((0, spread_z), (1, spread_y)):
+            for head in range(4):
+                total = spread[0, head].astype(F32)
+                for source in range(1, 4):
+                    total = total + spread[source, head].astype(F32)
+                mine[part, :, head * 384 : (head + 1) * 384] = total.astype(BF)
         for number in range(later, later + 4):
             links.send(number)
-        total_ref[group % 2, group // 2] = mine[...]
+        for part in range(2):
+            total_ref[me[1], part, me[0]] = mine[part]
         for came, number in relays:
             links.arrive(came)
             links.send(number)
 
     return exchange(
-        [out_piece, small_piece, late],
+        [out_piece, small_piece, late, up_grad],
         [
             shape((4, 2, 64, 512)),
             shape((16,) + small_piece.shape, F32),
             shape((32,) + late.shape, F32),
+            shape(up_grad.shape),
         ],
         sends,
         [
@@ -637,9 +695,13 @@
         ],
         12,
         work=work,
-        work_in=[qkv_piece],
-        work_out=[shape((2, 4, 64, 1536))],
-        work_scratch=[pltpu.VMEM((4, 4, 64, 384), BF), pltpu.VMEM((64, 1536), BF)],
+        work_in=[by_y, by_z],
+        work_out=[shape((2, 2, 4, 32, 1536))],
+        work_scratch=[
+            pltpu.VMEM((4, 4, 32, 384), BF),
+            pltpu.VMEM((4, 4, 32, 384), BF),
+            pltpu.VMEM((2, 32, 1536), BF),
+        ],
         deferred=range(later, len(sends)),
     )
 
@@ -688,7 +750,7 @@
 
     lax.fori_loop(0, SEQ // BLOCK, prepare, 0)
     row, col = lax.axis_index("row"), lax.axis_index("col")
-    for ahead in (2, 1, 3, 0):
+    for ahead in (1, 3, 2, 0):
         first = lax.rem(col + ahead, 4) * 512
 
         def block(step, carry, first=first):
@@ -751,10 +813,12 @@
     )
 
 
+NEAR_FIRST = (1, 3, 2, 0)
+
+
 def attend_back_kernel(
     links,
-    came,
-    later,
+    numbers,
     partial_ref,
     qkv_ref,
     query_ref,
@@ -763,32 +827,45 @@
     cos_ref,
     sin_ref,
     gain_ref,
+    qkv_grad_ref,
+    gain_grad_ref,
+    cross,
+    mixed,
+    out_grads,
     grad_ref,
-    gain_grad_ref,
-    parts_ref,
     query_grad,
     key_grad,
     value_grad,
 ):
+    to_rows, to_cols, back_query, back_to_cols, last = numbers
+    row, col = lax.axis_index("row"), lax.axis_index("col")
+    for ahead in NEAR_FIRST:
+        for number in to_rows[ahead]:
+            links.send(number)
     key_grad[...] = jnp.zeros_like(key_grad)
     value_grad[...] = jnp.zeros_like(value_grad)
-    row, col = lax.axis_index("row"), lax.axis_index("col")
-    parts_ref[row, rows(col * 512, 512), :] = partial_ref[:, rows((row * 4 + col) * HEAD, HEAD)]
-    for ahead in (0, 1, 3, 2):
-        for number in came[ahead]:
+
+    def mix(ahead):
+        head = lax.rem(col + ahead, 4)
+        for number in to_rows[ahead]:
             links.arrive(number)
-        if ahead == 3:
-            for number in later:
-                links.send(number)
-        first = lax.rem(col + ahead, 4) * 512
-
-        def block(step, carry, first=first):
+        total = partial_ref[:, rows((row * 4 + head) * HEAD, HEAD)].astype(F32)
+        for part in range(3):
+            total = total + cross[part, ahead].astype(F32)
+        if ahead:
+            mixed[ahead] = total.astype(BF)
+            links.send(to_cols[ahead])
+        else:
+            out_grads[rows(col * 512, 512), :] = total.astype(BF)
+
+    def attend_block(ahead):
+        if ahead:
+            links.arrive(to_cols[ahead])
+        first = lax.rem(col + 4 - ahead, 4) * 512
+
+        def block(step, carry):
             span = pl.ds(pl.multiple_of(first + step * BLOCK, BLOCK), BLOCK)
-            query = query_ref[span, :]
-            out_grad = parts_ref[0, span, :].astype(F32)
-            for part in range(1, 4):
-                out_grad = out_grad + parts_ref[part, span, :].astype(F32)
-            out_grad = out_grad.astype(BF)
+            query, out_grad = query_ref[span, :], out_grads[span, :]
             scores = (
                 lax.dot_general(query, key_ref[...], LAST, preferred_element_type=F32) * SCALE
             )
@@ -810,53 +887,123 @@
             return carry
 
         lax.fori_loop(0, 512 // BLOCK, block, 0)
+        finish_part(first, ((0, query_grad, 1.0),))
+        if ahead:
+            links.send(back_query[(4 - ahead) % 4])
+
+    def finish_part(first, sources):
+        def finish_block(step, carry):
+            span = pl.ds(pl.multiple_of(first + step * BLOCK, BLOCK), BLOCK)
+            for part, source, factor in sources:
+                turned = source[span, :] * factor
+                grad = turned * cos_ref[span, :] + swapped(turned * sin_ref[span, :])
+                raw = qkv_ref[span, part * HEAD : (part + 1) * HEAD].astype(F32)
+                inverse = lax.rsqrt(jnp.mean(raw * raw, axis=1, keepdims=True) + EPS)
+                unit = raw * inverse
+                gain_grad_ref[part : part + 1, :] += jnp.sum(grad * unit, axis=0, keepdims=True)
+                scaled = grad * gain_ref[part : part + 1, :]
+                raw_grad = inverse * (
+                    scaled - unit * jnp.mean(scaled * unit, axis=1, keepdims=True)
+                )
+                grad_ref[span, part * HEAD : (part + 1) * HEAD] = raw_grad.astype(BF)
+                if part:
+                    grad_ref[span, 2 * HEAD :] = value_grad[span, :].astype(BF)
+            return carry
+
+        lax.fori_loop(0, 512 // BLOCK, finish_block, 0)
+
     gain_grad_ref[...] = jnp.zeros_like(gain_grad_ref)
-
-    def finish(step, carry):
-        span = pl.ds(pl.multiple_of(step * BLOCK, BLOCK), BLOCK)
-        for part, source, factor in ((0, query_grad, 1.0), (1, key_grad, SCALE)):
-            turned = source[span, :] * factor
-            grad = turned * cos_ref[span, :] + swapped(turned * sin_ref[span, :])
-            raw = qkv_ref[span, part * HEAD : (part + 1) * HEAD].astype(F32)
-            inverse = lax.rsqrt(jnp.mean(raw * raw, axis=1, keepdims=True) + EPS)
-            unit = raw * inverse
-            gain_grad_ref[part : part + 1, :] += jnp.sum(grad * unit, axis=0, keepdims=True)
-            scaled = grad * gain_ref[part : part + 1, :]
-            raw_grad = inverse * (scaled - unit * jnp.mean(scaled * unit, axis=1, keepdims=True))
-            grad_ref[span, part * HEAD : (part + 1) * HEAD] = raw_grad.astype(BF)
-        grad_ref[span, 2 * HEAD :] = value_grad[span, :].astype(BF)
-        return carry
-
-    lax.fori_loop(0, SEQ // BLOCK, finish, 0)
-
-
-def attend_back(operands, blocks):
-    take, put = token_views()
-    sends, came = [], {ahead: [] for ahead in range(4)}
-    for offset in PLANE:
-        came[(4 - offset[3]) % 4].append(len(sends))
+    mix(1)
+    mix(3)
+    attend_block(1)
+    mix(2)
+    attend_block(3)
+    mix(0)
+    for number in last:
+        links.send(number)
+    attend_block(2)
+    attend_block(0)
+    for ahead in NEAR_FIRST:
+        finish_part(lax.rem(col + ahead, 4) * 512, ((1, key_grad, SCALE),))
+        if ahead:
+            links.send(back_to_cols[ahead])
+    qkv_grad_ref[:, rows(col * 384, 384)] = grad_ref[rows(col * 512, 512), :]
+
+
+def attend_back(operands, out_part, small_part, up_grad):
+    whole = lambda s, me, p: s
+    sends = [
+        (SIBLING, 0, lambda s, me, p: s.at[:, rows(p[1] * 64, 64)], 0, whole),
+        (SIBLING, 1, whole, 1, whole),
+    ]
+    later = len(sends)
+    to_rows, to_cols, back_query, back_to_cols = {}, {}, {}, {}
+    for ahead in NEAR_FIRST:
+        to_rows[ahead] = []
+        for part, offset in enumerate(ROWS):
+            to_rows[ahead].append(len(sends))
+            head = lambda me, p, ahead=ahead: p[2] * 4 + (me[3] + ahead) % 4
+            sends.append(
+                (
+                    offset,
+                    ("work", 0),
+                    lambda s, me, p, head=head: s.at[:, rows(head(me, p) * HEAD, HEAD)],
+                    ("scratch", 0),
+                    lambda o, me, p, part=part, ahead=ahead: o.at[part, ahead],
+                )
+            )
+    for offset in COLS:
+        ahead = offset[3]
+        to_cols[ahead] = len(sends)
         sends.append(
             (
                 offset,
-                ("work", 0),
-                lambda s, me, p: s.at[:, rows((p[2] * 4 + p[3]) * HEAD, HEAD)],
-                ("scratch", 0),
-                lambda o, me, p: o.at[me[2], rows(me[3] * 512, 512)],
+                ("scratch", 1),
+                lambda s, me, p, ahead=ahead: s.at[ahead],
+                ("scratch", 2),
+                lambda o, me, p: o.at[rows(me[3] * 512, 512)],
             )
         )
-    later = range(len(sends), len(sends) + len(CUBE))
-    sends += [(offset, 0, take, 0, put) for offset in CUBE]
+        for numbers, skip, size in ((back_query, 0, HEAD), (back_to_cols, HEAD, 2 * HEAD)):
+            numbers[ahead] = len(sends)
+            sends.append(
+                (
+                    offset,
+                    ("scratch", 3),
+                    lambda s, me, p, skip=skip, size=size: s.at[
+                        rows(p[3] * 512, 512), pl.ds(skip, size)
+                    ],
+                    ("made", 0),
+                    lambda o, me, p, skip=skip, size=size: o.at[
+                        :, pl.ds(pl.multiple_of(me[3] * 384 + skip, HEAD), size)
+                    ],
+                )
+            )
+    last = [len(sends)]
+    sends.append((ONE_BACK, 2, whole, 2, whole))
     return exchange(
-        [blocks],
-        [shape((EXPERTS, ROOM, 512))],
+        [out_part, small_part, up_grad],
+        [
+            shape((16, 64, 512)),
+            shape(small_part.shape, F32),
+            shape(up_grad.shape),
+        ],
         sends,
-        [(0, lambda s, me: take(s, me, me), 0, lambda o, me: put(o, me, me), (ROOM, 512))],
+        [],
         13,
-        deferred=later,
-        work=lambda links, *refs: attend_back_kernel(links, came, later, *refs),
+        deferred=range(later, len(sends)),
+        work=lambda links, *refs: attend_back_kernel(
+            links, (to_rows, to_cols, back_query, back_to_cols, last), *refs
+        ),
         work_in=operands,
-        work_out=[shape((SEQ, 3 * HEAD)), shape((8, HEAD), F32)],
-        work_scratch=[pltpu.VMEM((4, SEQ, HEAD), BF)] + [pltpu.VMEM((SEQ, HEAD), F32)] * 3,
+        work_out=[shape((512, 1536)), shape((8, HEAD), F32)],
+        work_scratch=[
+            pltpu.VMEM((3, 4, 512, HEAD), BF),
+            pltpu.VMEM((4, 512, HEAD), BF),
+            pltpu.VMEM((SEQ, HEAD), BF),
+            pltpu.VMEM((SEQ, 3 * HEAD), BF),
+        ]
+        + [pltpu.VMEM((SEQ, HEAD), F32)] * 3,
     )
 
 
@@ -868,6 +1015,7 @@
     links,
     came,
     returns,
+    results,
     shares,
     cot_ref,
     gated_ref,
@@ -907,6 +1055,9 @@
     own_out = pltpu.make_async_copy(
         take(back_ref, me, me), put(links.outs[0], me, me), own_sem.at[1]
     )
+    own_result = pltpu.make_async_copy(
+        take(gated_ref, me, me), put(links.outs[1], me, me), own_sem.at[2]
+    )
     own_in.start()
     for load in loads:
         load.start()
@@ -983,7 +1134,8 @@
             links.send(number)
         if group == 0:
             own_out.start()
-        for number in shares[group]:
+            own_result.start()
+        for number in shares[group] + results[group]:
             links.send(number)
     for numbers in shares:
         for number in numbers:
@@ -1013,11 +1165,12 @@
 
     lax.fori_loop(0, 4, weight_grads, 0)
     own_out.wait()
+    own_result.wait()
 
 
 def run_experts(blocks, cot_slots, weights):
     take, put = expert_views()
-    came, returns, shares = ([[], [], [], []] for _ in range(3))
+    came, returns, results, shares = ([[], [], [], []] for _ in range(4))
     sends = []
     for offset in CUBE:
         came[(offset[0] + offset[3]) % 4].append(len(sends))
@@ -1026,6 +1179,9 @@
     for offset in CUBE:
         returns[-(offset[0] + offset[3]) % 4].append(len(sends))
         sends.append((offset, ("scratch", 1), take, 0, put))
+    for offset in CUBE:
+        results[-(offset[0] + offset[3]) % 4].append(len(sends))
+        sends.append((offset, ("made", 0), take, 1, put))
     for place in range(4):
         span = pl.ds(place * GROUP, GROUP)
         for mine, theirs in ((2, 6), (3, 7)):
@@ -1045,12 +1201,12 @@
             )
     return exchange(
         [blocks] + weights,
-        [shape((EXPERTS, ROOM, 512))],
+        [shape((EXPERTS, ROOM, 512))] * 2,
         sends,
         [],
         8,
         work=lambda links, *refs: expert_kernel(
-            links, came, returns, shares, *refs
+            links, came, returns, results, shares, *refs
         ),
         work_in=[cot_slots],
         work_out=[shape((16, ROOM, WIDTH))]
@@ -1072,35 +1228,43 @@
             pltpu.VMEM((GROUP, WIDTH), F32),
             pltpu.VMEM((GROUP, WIDTH), F32),
             pltpu.SemaphoreType.DMA((8,)),
-            pltpu.SemaphoreType.DMA((2,)),
+            pltpu.SemaphoreType.DMA((3,)),
         ],
         deferred=range(len(CUBE), len(sends)),
     )
 
 
-def pack_kernel(up_1, up_2, down_1, down_2, up_ref, down_ref):
+def pack_kernel(up_1, up_2, down_1, down_2, qkv, up_ref, down_ref, qkv_ref):
     upper = lax.axis_index("row") // 2
     for which, up, down in ((upper, up_1, down_1), (1 - upper, up_2, down_2)):
         value = up[...].astype(F32)
         up_ref[which, :, 0, :] = value[:, :256]
         up_ref[which, :, 1, :] = value[:, 256:]
         down_ref[which] = down[...].astype(F32)
-
-
-def pack_grads(up_1, up_2, down_1, down_2):
+    for head in range(4):
+        qkv_ref[:, head, :] = qkv[:, head * 384 : (head + 1) * 384].astype(F32)
+
+
+def pack_grads(up_1, up_2, down_1, down_2, qkv):
     steps = 8
     up, down = (WIDTH // steps, 512), (256 // steps, WIDTH)
     return pl.pallas_call(
         pack_kernel,
         grid=(steps,),
-        out_shape=[shape((2, WIDTH, 2, 256), F32), shape((2, 256, WIDTH), F32)],
+        out_shape=[
+            shape((2, WIDTH, 2, 256), F32),
+            shape((2, 256, WIDTH), F32),
+            shape((512, 4, 384), F32),
+        ],
         in_specs=[pl.BlockSpec(up, lambda i: (i, 0))] * 2
-        + [pl.BlockSpec(down, lambda i: (i, 0))] * 2,
+        + [pl.BlockSpec(down, lambda i: (i, 0))] * 2
+        + [pl.BlockSpec((512 // steps, 1536), lambda i: (i, 0))],
         out_specs=[
             pl.BlockSpec((2, up[0], 2, 256), lambda i: (0, i, 0, 0)),
             pl.BlockSpec((2,) + down, lambda i: (0, i, 0)),
+            pl.BlockSpec((512 // steps, 4, 384), lambda i: (i, 0, 0)),
         ],
-    )(up_1, up_2, down_1, down_2)
+    )(up_1, up_2, down_1, down_2, qkv)
 
 
 def dot(left, right):
@@ -1154,10 +1318,6 @@
 
 def after(*operands):
     return lax.optimization_barrier(operands)
-
-
-def inverse_pairs(pairs):
-    return [(b, a) for a, b in pairs]
 
 
 def shards(
@@ -1261,12 +1421,11 @@
     gates = shifted / jnp.sum(shifted, axis=0, keepdims=True)
     slot_gates = jnp.sum(pick.astype(F32) * gates[:, None, :], axis=2)
     send_rows = dot(flat_pick, experts_input).astype(BF).reshape(EXPERTS, ROOM, 512)
-    back_rows, out_rows, up_1, up_2, down_1, down_2 = run_experts(
+    back_rows, out_rows, _, up_1, up_2, down_1, down_2 = run_experts(
         send_rows + aux_rows(slot_gates), cot_slots, up_ws + down_ws
     )
     gate_grad = jnp.sum(pick.astype(F32) * aux_value(back_rows, 0)[:, :, None], axis=1)
     inner = jnp.sum(pick.astype(F32) * aux_value(back_rows, 1)[:, :, None], axis=(0, 1))
-    first_back, second_back = inverse_pairs(FIRST_HOP), inverse_pairs(SECOND_HOP)
     logit_grad = gates * (gate_grad - jnp.sum(gates * gate_grad, axis=0, keepdims=True))
     experts_input_grad = dot_first(
         flat_pick, back_rows.reshape(EXPERTS * ROOM, 512)
@@ -1300,26 +1459,31 @@
         ],
         axis=0,
     )
-    out_rows, qkv_grad, head_gain_part = attend_back(
+    out_other, small_other, up_1, qkv_grad, head_gain_part = attend_back(
         [dot_last(attended_grad, w_all).astype(BF), qkv, query, key, lse, cosine, sine, gains],
-        out_rows,
-    )
-    qkv_grad, up_1, up_2, down_1, down_2 = after(qkv_grad, up_1, up_2, down_1, down_2)
-    up_1, up_2 = hop(up_1, first_back), hop(up_2, second_back)
-    down_1, down_2 = hop(down_1, first_back), hop(down_2, second_back)
-    qkv_grad, out_other, small_other, output = from_heads(
-        qkv_grad,
         out_part,
         small_part,
-        [hidden, flat_pick, out_rows.reshape(EXPERTS * ROOM, 512)],
+        up_1,
     )
     out_half = (
         lax.dynamic_slice_in_dim(out_part, core * 64, 64, 1).astype(F32)
         + out_other.astype(F32)
     ).astype(BF)
     small = (small_part + small_other).reshape(16, 24, HEAD)
-    out_pieces, small_pieces, qkv_piece, normed_grad, row_stats = finish(
-        out_half, small, normed, qkv_grad, w_group, head_gain_part
+    out_pieces, small_pieces, down_1, down_2, by_y, by_z, normed_grad, row_stats, output = finish(
+        out_half,
+        small,
+        down_1,
+        down_2,
+        [
+            normed,
+            qkv_grad,
+            w_group,
+            head_gain_part,
+            hidden,
+            flat_pick,
+            out_rows.reshape(EXPERTS * ROOM, 512),
+        ],
     )
     normed_grad = jnp.sum(normed_grad.astype(F32), axis=0)
     row_stats = jnp.sum(row_stats, axis=0)
@@ -1331,21 +1495,25 @@
     attention_gain_part = jnp.sum(normed_grad * unit_attention, axis=0)
 
     out_piece = jnp.sum(out_pieces.astype(F32), axis=0).astype(BF)
-    out_total, small_total, late, qkv_total = collect_sums(
-        qkv_piece,
+    out_total, small_total, late, up_2, qkv_total = collect_sums(
+        by_y,
+        by_z,
         out_piece,
         jnp.sum(small_pieces, axis=0),
         jnp.concatenate([attention_gain_part.reshape(4, HEAD), row_stats[4:]], axis=0),
+        up_2,
     )
     small_total = small_total.reshape(384, HEAD)
     late = jnp.sum(late, axis=0)
-    grad_gate_up, grad_down = pack_grads(up_1, up_2, down_1, down_2)
+    grad_gate_up, grad_down, grad_qkv = pack_grads(
+        up_1, up_2, down_1, down_2, qkv_total.reshape(512, 1536)
+    )
     return (
         output,
         token_grad.astype(BF),
         late[:4].reshape(512),
         small_total[256:260].reshape(512),
-        qkv_total.astype(F32).reshape(512, 4, 384),
+        grad_qkv,
         late[4],
         late[5],
         out_total.astype(F32).reshape(512, 512),

time: 533 us -> 515 us (0.966)
  Pallas kernels: 446 us -> 427 us
  starting transfers between devices: 11.4 us -> 18.2 us
    pallas_call x9 -> x8, Pallas kernels: 436 us -> 416 us  [exchange(): pl.pallas_call(kernel, out_shape=list(outputs) + list(work_out), in_specs...]
    ppermute x4, starting transfers between devices: 1.83 us -> 12.8 us  [shards(): sibling = lambda w: lax.ppermute(w, 'dp', PAIR)]
  transfers between devices with their start and end apart: 10 -> 6, of which waited for: 2 -> 0; matrix products, arithmetic and copies ran while one was open for 8% -> 4% of each run, Pallas kernels for 40% -> 17%
where the time goes in v4:
time: 515 us; the launch traced here: 508 us
  Pallas kernels  427 us (83%)
  other arithmetic  26.8 us (5%)
  matrix products  23.7 us (5%)
  starting transfers between devices  18.2 us (4%)
  local copies, waits for them, and re-layouts  10.7 us (2%)
    pallas_call x8, Pallas kernels, exchange(): pl.pallas_call(kernel, out_shape=list(outputs) + list(work_out), in_specs...  416 us
    dot_general x4, matrix products, dot(): return jnp.dot(left, right, preferred_element_type=F32)  14.4 us
    ppermute x4, starting transfers between devices, shards(): sibling = lambda w: lax.ppermute(w, 'dp', PAIR)  12.8 us
    pallas_call x1, Pallas kernels, pack_grads(): pl.pallas_call(pack_kernel, grid=(steps,), out_shape=[shape((2, WIDTH, 2,...  11.2 us
  transfers between devices with their start and end apart: 6, of which 0 were waited for; matrix products, arithmetic and copies ran while one was open for 4% of the time, Pallas kernels for 17%

profile of v4, /device:TPU:1, one launch (start us, length us, event | category | flops | bytes accessed | tf_op | source)
XLA Modules:
  0.0 508.2 jit_solution(7488650110897989852)
XLA Ops:
  2.4 2.8 copy.47
  5.2 54.4 %shard_map.212 = (bf16[512,2048]{1,0:T(8,128)(2,1)}, bf16[4,512,1536]{2,1,0:T(8,128)(2,1)}, s32[4,4,128]{2,1,0:T(4,128)}, f32[4,4,128]{2,1,0:T(4,128)}, bf16[4,4...) custom-call(bf16[512,512]{1,0:T(8,128)(2,1)} %refs_0_.1, ...), custom_call_target="tpu_custom_call" | custom-call | bytes 105000000 | tf_op jit(solution)/shard_map/pallas_call | solution.py:182
  59.6 3.0 collective-permute-start
  62.6 2.4 collective-permute-start.1
  65.0 2.1 fusion.5
  67.7 7.0 %convolution_convert_fusion.3.refs_0_ = bf16[512,1536]{1,0:T(8,128)(2,1)S(1)} fusion(bf16[512,2048]{1,0:T(8,128)(2,1)S(1)} %fusion.7.refs_4_, bf16[2048,1536]{1,0:T(8,128)(2,1)} %bitcast.74), kind=kOutput, calls=%fused_computation.19 | convolution fusion | flops 3222011904 | bytes 9961472 | tf_op jit(solution)/shard_map/dot_general | solution.py:1271
  74.7 21.9 %shard_map.213.refs_1_.refs_4_ = bf16[2048,384]{1,0:T(8,128)(2,1)S(1)} custom-call(bf16[512,1536]{1,0:T(8,128)(2,1)S(1)} %convolution_convert_fusion.3.refs_0_), custom_call_target="tpu_custom_call" | custom-call | bytes 105000000 | tf_op jit(solution)/shard_map/pallas_call | solution.py:182
  99.4 2.9 fusion.35
  103.7 65.7 %shard_map.214 = (bf16[16,40,2048]{2,1,0:T(8,128)(2,1)}, bf16[2048,128]{1,0:T(8,128)(2,1)}, bf16[2048,128]{1,0:T(8,128)(2,1)}, f32[2048,1]{1,0:T(8,128)}, f32[20...) custom-call(bf16[64,40,512]{2,1,0:T(8,128)(2,1)} %get-tuple-element.61.refs_0_, ...), custom_call_target="tpu_custom_call" | custom-call | bytes 105000000 | tf_op jit(solution)/shard_map/pallas_call | solution.py:182
  169.5 3.6 multiply_reduce_fusion.1
  173.9 12.0 %shard_map.215 = f32[4,72,512]{2,1,0:T(8,128)S(1)} custom-call(f32[72,512]{1,0:T(8,128)S(1)} %maximum_maximum_fusion.1.refs_0_), custom_call_target="tpu_custom_call" | custom-call | bytes 105000000 | tf_op jit(solution)/shard_map/pallas_call | solution.py:182
  187.3 11.5 %collective-permute-start.5 = (bf16[256,2048]{1,0:T(8,128)(2,1)}, bf16[256,2048]{1,0:T(8,128)(2,1)}, u32[]{:S(2)}, u32[]{:S(2)}) collective-permute-start(bf16[256,2048]{1,0:T(8,128)(2,1)} %get-tuple-element.76.refs_6_), channel_id=1, source_target_pairs={{0,16},{16,0},{32,48},{48,32},{64,80},{80,64},{96,112},{112,96},{1... | collective-permute-start | bytes 3145736 | tf_op jit(solution)/shard_map/ppermute | solution.py:1370
  199.9 2.9 convolution_convert_fusion
  204.6 105.1 %shard_map.216 = (bf16[64,40,512]{2,1,0:T(8,128)(2,1)}, bf16[64,40,512]{2,1,0:T(8,128)(2,1)}, bf16[16,40,2048]{2,1,0:T(8,128)(2,1)}, bf16[2048,512]{1,0:T(8,128)...) custom-call(bf16[64,40,512]{2,1,0:T(8,128)(2,1)} %pad_add_fusion.refs_0_, ...), custom_call_target="tpu_custom_call" | custom-call | bytes 105000000 | tf_op jit(solution)/shard_map/pallas_call | solution.py:182
  313.5 2.3 multiply_reduce_fusion
  315.8 2.6 convolution_convert_fusion.1.refs_3_
  318.4 2.6 convolution_convert_fusion.2
  321.9 56.3 %shard_map.217 = (bf16[16,64,512]{2,1,0:T(8,128)(2,1)}, f32[384,128]{1,0:T(8,128)}, bf16[2048,512]{1,0:T(8,128)(2,1)}, bf16[512,1536]{1,0:T(8,128)(2,1)}, f32[8,128]{1,0:T(8,128)}) custom-call(bf16[16,128,512]{2,1,0:T(8,128)(2,1)} %bitcast.77, f32[384,128]{1,0:T(8,128)} %maximum_maximum_fusion.refs_1_, bf16[2048,512]{1,0:T(8,128)(2,1)} %get-tuple-element.79.refs_2_, ...), custom_call_target="tpu_custom_call" | custom-call | bytes 105000000 | tf_op jit(solution)/shard_map/pallas_call | solution.py:182
  379.9 2.5 add_convert_fusion.refs_0_
  382.4 57.3 %shard_map.218 = (bf16[16,64,512]{2,1,0:T(8,128)(2,1)}, f32[16,24,128]{2,1,0:T(8,128)}, bf16[256,2048]{1,0:T(8,128)(2,1)}, bf16[256,2048]{1,0:T(8,128)(2,1)}, bf...) custom-call(bf16[16,64,512]{2,1,0:T(8,128)(2,1)} %add_convert_fusion, ...), custom_call_target="tpu_custom_call" | custom-call | bytes 105000000 | tf_op jit(solution)/shard_map/pallas_call | solution.py:182
  444.0 2.0 reduce_sum.182.refs_0_
  446.0 43.5 %shard_map.219 = (bf16[4,2,64,512]{3,2,1,0:T(8,128)(2,1)}, f32[16,24,128]{2,1,0:T(8,128)}, f32[32,8,128]{2,1,0:T(8,128)}, bf16[2048,512]{1,0:T(8,128)(2,1)}, bf16[2,2,4,32,1536]{4,3,2,1,0:T(8,128)(2,1)}) custom-call(bf16[64,512]{1,0:T(8,128)(2,1)} %reduce_sum.182.refs_0_, f32[24,128]{1,0:T(8,128)} %reduce_sum.183.refs_1_, ...), custom_call_target="tpu_custom_call" | custom-call | bytes 105000000 | tf_op jit(solution)/shard_map/pallas_call | solution.py:182
  493.2 2.1 bitcast_convert_fusion
  496.0 11.2 %shard_map.220 = (f32[2,2048,2,256]{3,2,1,0:T(2,128)}, f32[2,256,2048]{2,1,0:T(8,128)}, f32[512,4,384]{2,1,0:T(4,128)}) custom-call(bf16[2048,512]{1,0:T(8,128)(2,1)} %get-tuple-element.102.up_1, bf16[2048,512]{1,0:T(8,128)(2,1)} %get-tuple-element.103.up_2, bf16[256,2048]{1,0:T(8,128)(2,1)} %get-tuple-element.104.down_1, ...), custom_call_target="tpu_custom_call" | custom-call | tf_op jit(solution)/shard_map/pallas_call | solution.py:1251
  (122 shorter events, 27.2 us)
Async XLA Ops:
  0.6 172.5 %copy-start = (bf16[512,64]{0,1:T(8,128)(2,1)S(1)}, bf16[512,64]{0,1:T(8,128)(2,1)}, u32[]{:S(2)}) copy-start(bf16[512,64]{0,1:T(8,128)(2,1)} %param.22) | copy-start | bytes 196612
  59.6 7.5 %copy-start.4 = (bf16[512,2048]{1,0:T(8,128)(2,1)S(1)}, bf16[512,2048]{1,0:T(8,128)(2,1)}, u32[]{:S(2)}) copy-start(bf16[512,2048]{1,0:T(8,128)(2,1)} %get-tuple-element.62) | copy-start | bytes 6291460
  59.6 7.5 %copy-start.19 = (f32[4,4,128]{2,1,0:T(4,128)S(1)}, f32[4,4,128]{2,1,0:T(4,128)}, u32[]{:S(2)}) copy-start(f32[4,4,128]{2,1,0:T(4,128)} %get-tuple-element.63) | copy-start | bytes 24580
  59.6 109.9 %collective-permute-start = (bf16[2048,512]{1,0:T(8,128)(2,1)}, bf16[2048,512]{1,0:T(8,128)(2,1)}, u32[]{:S(2)}, u32[]{:S(2)}) collective-permute-start(bf16[2048,512]{1,0:T(8,128)(2,1)} %get-tuple-element.67), channel_id=1, source_target_pairs={{0,16},{4,0},{8,20},{12,4},{16,24},{20,8},{24,28},{28,12},{32,48},... | collective-permute-start | bytes 6291464 | tf_op jit(solution)/shard_map/ppermute | solution.py:1316
  62.6 106.9 %collective-permute-start.1 = (bf16[2048,512]{1,0:T(8,128)(2,1)}, bf16[2048,512]{1,0:T(8,128)(2,1)}, u32[]{:S(2)}, u32[]{:S(2)}) collective-permute-start(bf16[2048,512]{1,0:T(8,128)(2,1)} %get-tuple-element.68), channel_id=1, source_target_pairs={{0,4},{4,20},{8,0},{12,16},{16,12},{20,28},{24,8},{28,24},{32,36},... | collective-permute-start | bytes 6291464 | tf_op jit(solution)/shard_map/ppermute | solution.py:1316
  67.7 7.0 %copy-start.5 = (bf16[512,2048]{1,0:T(8,128)(2,1)}, bf16[512,2048]{1,0:T(8,128)(2,1)S(1)}, u32[]{:S(2)}) copy-start(bf16[512,2048]{1,0:T(8,128)(2,1)S(1)} %fusion.7.refs_4_) | copy-start | bytes 6291460
  74.7 23.1 %copy-start.23 = (s32[4,4,128]{2,1,0:T(4,128)S(1)}, s32[4,4,128]{2,1,0:T(4,128)}, u32[]{:S(2)}) copy-start(s32[4,4,128]{2,1,0:T(4,128)} %get-tuple-element.65) | copy-start | bytes 24580
  74.7 24.7 %copy-start.7 = (f32[64,512]{1,0:T(8,128)S(1)}, f32[64,512]{1,0:T(8,128)}, u32[]{:S(2)}) copy-start(f32[64,512]{1,0:T(8,128)} %convolution_select_fusion.refs_7_) | copy-start | bytes 393220
  99.1 3.9 copy-start.25
  99.1 3.9 copy-start.26
  103.7 65.8 %copy-start.8 = (bf16[512,512]{1,0:T(8,128)(2,1)S(1)}, bf16[512,512]{1,0:T(8,128)(2,1)}, u32[]{:S(2)}) copy-start(bf16[512,512]{1,0:T(8,128)(2,1)} %refs_0_.1) | copy-start | bytes 1572868
  169.5 3.6 copy-start.20
  173.1 140.3 %copy-start.3 = (f32[512,512]{1,0:T(8,128)}, f32[512,512]{1,0:T(8,128)S(1)}, u32[]{:S(2)}) copy-start(f32[512,512]{1,0:T(8,128)S(1)} %get-tuple-element.134.refs_8_) | copy-start | bytes 3145732
  173.1 13.7 %copy-start.9 = (bf16[256,2048]{1,0:T(8,128)(2,1)S(1)}, bf16[256,2048]{1,0:T(8,128)(2,1)}, u32[]{:S(2)}) copy-start(bf16[256,2048]{1,0:T(8,128)(2,1)} %get-tuple-element.75.refs_5_) | copy-start | bytes 3145732
  185.9 18.6 %collective-permute-start.2 = (bf16[2048,512]{1,0:T(8,128)(2,1)}, bf16[2048,512]{1,0:T(8,128)(2,1)}, u32[]{:S(2)}, u32[]{:S(2)}) collective-permute-start(bf16[2048,512]{1,0:T(8,128)(2,1)} %collective-permute-done.refs_1_), channel_id=1, source_target_pairs={{0,16},{16,0},{32,48},{48,32},{64,80},{80,64},{96,112},{112,96},{1... | collective-permute-start | bytes 6291464 | tf_op jit(solution)/shard_map/ppermute | solution.py:1370
  186.7 17.8 %collective-permute-start.3 = (bf16[2048,512]{1,0:T(8,128)(2,1)}, bf16[2048,512]{1,0:T(8,128)(2,1)}, u32[]{:S(2)}, u32[]{:S(2)}) collective-permute-start(bf16[2048,512]{1,0:T(8,128)(2,1)} %collective-permute-done.1.refs_2_), channel_id=1, source_target_pairs={{0,16},{16,0},{32,48},{48,32},{64,80},{80,64},{96,112},{112,96},{1... | collective-permute-start | bytes 6291464 | tf_op jit(solution)/shard_map/ppermute | solution.py:1370
  186.8 17.7 %collective-permute-start.4 = (bf16[256,2048]{1,0:T(8,128)(2,1)S(1)}, bf16[256,2048]{1,0:T(8,128)(2,1)}, u32[]{:S(2)}, u32[]{:S(2)}) collective-permute-start(bf16[256,2048]{1,0:T(8,128)(2,1)S(1)} %copy-done.9), channel_id=1, source_target_pairs={{0,16},{16,0},{32,48},{48,32},{64,80},{80,64},{96,112},{112,96},{1... | collective-permute-start | bytes 3145736 | tf_op jit(solution)/shard_map/ppermute | solution.py:1370
  187.3 17.2 %collective-permute-start.5 = (bf16[256,2048]{1,0:T(8,128)(2,1)}, bf16[256,2048]{1,0:T(8,128)(2,1)}, u32[]{:S(2)}, u32[]{:S(2)}) collective-permute-start(bf16[256,2048]{1,0:T(8,128)(2,1)} %get-tuple-element.76.refs_6_), channel_id=1, source_target_pairs={{0,16},{16,0},{32,48},{48,32},{64,80},{80,64},{96,112},{112,96},{1... | collective-permute-start | bytes 3145736 | tf_op jit(solution)/shard_map/ppermute | solution.py:1370
  309.6 3.3 copy-start.21
  309.6 3.8 copy-start.12
  318.4 2.7 copy-start.17
  321.9 58.0 %copy-start.6 = (bf16[2048,512]{1,0:T(8,128)(2,1)S(1)}, bf16[2048,512]{1,0:T(8,128)(2,1)}, u32[]{:S(2)}) copy-start(bf16[2048,512]{1,0:T(8,128)(2,1)} %convolution_convert_fusion.2) | copy-start | bytes 6291460
  496.0 11.2 %copy-start.13 = (bf16[512,512]{1,0:T(8,128)(2,1)S(1)}, bf16[512,512]{1,0:T(8,128)(2,1)}, u32[]{:S(2)}) copy-start(bf16[512,512]{1,0:T(8,128)(2,1)} %get-tuple-element.148) | copy-start | bytes 1572868
  496.0 12.0 %copy-start.1 = (bf16[512,64]{0,1:T(8,128)(2,1)S(1)}, bf16[512,64]{0,1:T(8,128)(2,1)}, u32[]{:S(2)}) copy-start(bf16[512,64]{0,1:T(8,128)(2,1)} %param.22) | copy-start | bytes 196612
  (11 other events, 23.2 us)

commit v5 on v4

--- a/solution.py
+++ b/solution.py
@@ -424,11 +424,23 @@
     hidden_ref,
     pick_ref,
     rows_ref,
+    out_part_ref,
+    out_other_ref,
+    small_part_ref,
+    small_other_ref,
+    middle_ref,
+    tokens_ref,
+    inverse_ref,
+    norm_gain_ref,
     by_y_ref,
     by_z_ref,
     feature_ref,
     stat_ref,
     out_ref,
+    out_piece_ref,
+    small_piece_ref,
+    token_grad_ref,
+    late_ref,
     their_half,
     came,
     half,
@@ -438,10 +450,15 @@
     stat_part,
     feature_sum,
     passing,
+    out_half,
+    out_came,
+    small_sum,
+    small_came,
 ):
     me = here()
     y, core, row, col = me
-    to_sibling, to_lines, to_cols, to_rows, last = numbers
+    to_sibling, to_lines, to_cols, to_rows, stats, last, spread_out = numbers
+    own = y * 4 + col
 
     def product(start):
         return lax.dot_general(
@@ -451,6 +468,17 @@
     for r in range(4):
         their_half[r] = product(r * 512 + (1 - core) * 256).astype(BF)
         links.send(to_sibling[r])
+    for block in range(16):
+        out_half[block] = (
+            out_part_ref[block, rows(core * 64, 64), :].astype(F32)
+            + out_other_ref[block].astype(F32)
+        ).astype(BF)
+        span = slice(block * 24, (block + 1) * 24)
+        small_sum[block] = small_part_ref[span, :] + small_other_ref[span, :]
+    for number in spread_out:
+        links.send(number)
+    out_came[own] = out_half[own]
+    small_came[own] = small_sum[own]
     inner = jnp.zeros((512, 1), F32)
     for ahead in (2, 1, 3, 0):
         span = rows(lax.rem(row + ahead, 4) * 512, 512)
@@ -465,7 +493,7 @@
         elif ahead:
             feature_sum[ahead // 2] = part
         else:
-            feature_ref[0] = part.astype(BF)
+            feature_sum[2] = part
     for index, ahead in enumerate((1, 3)):
         links.arrive(to_rows[2][index])
         part = slice(index * 256, (index + 1) * 256)
@@ -482,7 +510,7 @@
         )
     stat_part[4:, :] = gain_ref[:4, :]
     stat_ref[row] = stat_part[...]
-    for number in last:
+    for number in stats + last:
         links.send(number)
     for r in range(4):
         mine = product(r * 512 + core * 256)
@@ -507,25 +535,50 @@
             for source in range(1, 4):
                 total = total + spread[source, r].astype(F32)
             target[r] = total.astype(BF)
-
-
-def finish(out_half, small, down_1, down_2, operands):
+    for number in (to_rows[1], to_rows[3], *stats):
+        links.arrive(number)
+    row_stats = stat_ref[0] + stat_ref[1] + stat_ref[2] + stat_ref[3]
+    late_ref[4:, :] = row_stats[4:, :]
+    for block in range(4):
+        span = pl.ds(block * HEAD, HEAD)
+        mean = jnp.sum(same * row_stats[block : block + 1, :], axis=1, keepdims=True) / WIDTH
+        features = feature_sum[2, span, :]
+        for part in range(2):
+            features = features + feature_ref[part, span, :].astype(F32)
+        inverse = inverse_ref[span, :]
+        unit = tokens_ref[span, :].astype(F32) * inverse
+        token_grad_ref[span, :] = (
+            middle_ref[span, :] + inverse * (features * norm_gain_ref[0:1, :] - unit * mean)
+        ).astype(BF)
+        share = jnp.sum(features * unit, axis=0, keepdims=True)
+        for part in range(4):
+            lanes = share[:, part * HEAD : (part + 1) * HEAD]
+            if block == 0:
+                late_ref[part : part + 1, :] = lanes
+            else:
+                late_ref[part : part + 1, :] += lanes
+    for number in spread_out:
+        links.arrive(number)
+    out_total, small_total = out_came[0].astype(F32), small_came[0]
+    for source in range(1, 16):
+        out_total = out_total + out_came[source].astype(F32)
+        small_total = small_total + small_came[source]
+    out_piece_ref[...] = out_total.astype(BF)
+    small_piece_ref[...] = small_total
+
+
+def finish(down_1, down_2, operands):
     take_out = lambda s, me, p: s.at[p[0] * 4 + p[3]]
     put_out = lambda o, me, p: o.at[me[0] * 4 + me[3]]
     whole = lambda s, me, p: s
     own_row = lambda o, me, p: o.at[me[2]]
-    keep = lambda i, dims: (
-        i,
-        lambda s, me: take_out(s, me, me),
-        i,
-        lambda o, me: put_out(o, me, me),
-        dims,
-    )
-    sends = [(offset, 0, take_out, 0, put_out) for offset in SOURCES]
-    sends += [(offset, 1, take_out, 1, put_out) for offset in SOURCES]
-    later = len(sends)
+    sends = []
     to_sibling, to_lines, to_cols = [], [[], [], [], []], [[], [], [], []]
-    to_rows, last = {}, []
+    to_rows, stats, last, spread_out = {}, [], [], []
+    for offset in SOURCES:
+        for mine, theirs in ((9, 10), (11, 12)):
+            spread_out.append(len(sends))
+            sends.append((offset, ("scratch", mine), take_out, ("scratch", theirs), put_out))
     for r in range(4):
         view = lambda ref, me, p, r=r: ref.at[r]
         to_sibling.append(len(sends))
@@ -561,31 +614,34 @@
     for index, offset in enumerate(((0, 0, 1, 0), (0, 0, 3, 0))):
         to_rows[offset[2]] = len(sends)
         part = lambda s, me, p, ahead=offset[2]: s.at[ahead - 1]
-        slot = lambda o, me, p, index=index: o.at[1 + index]
+        slot = lambda o, me, p, index=index: o.at[index]
         sends.append((offset, ("scratch", 5), part, ("made", 2), slot))
     for offset in ROWS:
-        last.append(len(sends))
+        stats.append(len(sends))
         sends.append((offset, ("scratch", 6), whole, ("made", 3), own_row))
-    for way, index in ((ONE_BACK, 2), (OTHER_BACK, 3)):
+    for way, index in ((ONE_BACK, 0), (OTHER_BACK, 1)):
         last.append(len(sends))
         sends.append((way, index, whole, index, whole))
     return exchange(
-        [out_half, small, down_1, down_2],
-        [shape((16, 64, 512)), shape((16,) + small.shape[1:], F32)]
-        + [shape(down_1.shape)] * 2,
+        [down_1, down_2],
+        [shape(down_1.shape)] * 2,
         sends,
-        [keep(0, (64, 512)), keep(1, small.shape[1:])],
+        [],
         5,
         work=lambda links, *refs: finish_kernel(
-            links, (to_sibling, to_lines, to_cols, to_rows, last), *refs
+            links, (to_sibling, to_lines, to_cols, to_rows, stats, last, spread_out), *refs
         ),
         work_in=operands,
         work_out=[
             shape((4, 32, 1536)),
             shape((4, 128, 384)),
-            shape((3, 512, 512)),
+            shape((2, 512, 512)),
             shape((4, 8, HEAD), F32),
             shape((512, 512)),
+            shape((64, 512)),
+            shape((24, HEAD), F32),
+            shape((512, 512)),
+            shape((8, HEAD), F32),
         ],
         work_scratch=[pltpu.VMEM((4, 256, 1536), BF)] * 3
         + [
@@ -593,10 +649,14 @@
             pltpu.VMEM((4, 4, 128, 384), BF),
             pltpu.VMEM((3, 512, 512), BF),
             pltpu.VMEM((8, HEAD), F32),
-            pltpu.VMEM((2, 512, 512), F32),
+            pltpu.VMEM((3, 512, 512), F32),
             pltpu.VMEM((2, 256, 512), BF),
+            pltpu.VMEM((16, 64, 512), BF),
+            pltpu.VMEM((16, 64, 512), BF),
+            pltpu.VMEM((16, 24, HEAD), F32),
+            pltpu.VMEM((16, 24, HEAD), F32),
         ],
-        deferred=range(later, len(sends)),
+        deferred=range(len(sends)),
     )
 
 
@@ -1234,18 +1294,19 @@
     )
 
 
-def pack_kernel(up_1, up_2, down_1, down_2, qkv, up_ref, down_ref, qkv_ref):
+def pack_kernel(up_1, up_2, down_1, down_2, qkv, out, up_ref, down_ref, qkv_ref, out_ref):
     upper = lax.axis_index("row") // 2
     for which, up, down in ((upper, up_1, down_1), (1 - upper, up_2, down_2)):
         value = up[...].astype(F32)
         up_ref[which, :, 0, :] = value[:, :256]
         up_ref[which, :, 1, :] = value[:, 256:]
         down_ref[which] = down[...].astype(F32)
+    out_ref[...] = out[...].astype(F32)
     for head in range(4):
         qkv_ref[:, head, :] = qkv[:, head * 384 : (head + 1) * 384].astype(F32)
 
 
-def pack_grads(up_1, up_2, down_1, down_2, qkv):
+def pack_grads(up_1, up_2, down_1, down_2, qkv, out):
     steps = 8
     up, down = (WIDTH // steps, 512), (256 // steps, WIDTH)
     return pl.pallas_call(
@@ -1255,16 +1316,19 @@
             shape((2, WIDTH, 2, 256), F32),
             shape((2, 256, WIDTH), F32),
             shape((512, 4, 384), F32),
+            shape((512, 512), F32),
         ],
         in_specs=[pl.BlockSpec(up, lambda i: (i, 0))] * 2
         + [pl.BlockSpec(down, lambda i: (i, 0))] * 2
-        + [pl.BlockSpec((512 // steps, 1536), lambda i: (i, 0))],
+        + [pl.BlockSpec((512 // steps, 1536), lambda i: (i, 0))]
+        + [pl.BlockSpec((512 // steps, 512), lambda i: (i, 0))],
         out_specs=[
             pl.BlockSpec((2, up[0], 2, 256), lambda i: (0, i, 0, 0)),
             pl.BlockSpec((2,) + down, lambda i: (0, i, 0)),
             pl.BlockSpec((512 // steps, 4, 384), lambda i: (i, 0, 0)),
+            pl.BlockSpec((512 // steps, 512), lambda i: (i, 0)),
         ],
-    )(up_1, up_2, down_1, down_2, qkv)
+    )(up_1, up_2, down_1, down_2, qkv, out)
 
 
 def dot(left, right):
@@ -1465,14 +1529,7 @@
         small_part,
         up_1,
     )
-    out_half = (
-        lax.dynamic_slice_in_dim(out_part, core * 64, 64, 1).astype(F32)
-        + out_other.astype(F32)
-    ).astype(BF)
-    small = (small_part + small_other).reshape(16, 24, HEAD)
-    out_pieces, small_pieces, down_1, down_2, by_y, by_z, normed_grad, row_stats, output = finish(
-        out_half,
-        small,
+    down_1, down_2, by_y, by_z, _, _, output, out_piece, small_piece, token_grad, late = finish(
         down_1,
         down_2,
         [
@@ -1483,40 +1540,38 @@
             hidden,
             flat_pick,
             out_rows.reshape(EXPERTS * ROOM, 512),
+            out_part,
+            out_other,
+            small_part,
+            small_other,
+            middle_grad,
+            tokens,
+            inverse_attention[:, None],
+            jnp.broadcast_to(attention_norm_gain[None], (8, 512)),
         ],
     )
-    normed_grad = jnp.sum(normed_grad.astype(F32), axis=0)
-    row_stats = jnp.sum(row_stats, axis=0)
-    mean_attention = row_stats[:4].reshape(512) / WIDTH
-    unit_attention = token_float * inverse_attention[:, None]
-    token_grad = middle_grad + inverse_attention[:, None] * (
-        normed_grad * attention_norm_gain - unit_attention * mean_attention[:, None]
-    )
-    attention_gain_part = jnp.sum(normed_grad * unit_attention, axis=0)
-
-    out_piece = jnp.sum(out_pieces.astype(F32), axis=0).astype(BF)
     out_total, small_total, late, up_2, qkv_total = collect_sums(
-        by_y,
-        by_z,
-        out_piece,
-        jnp.sum(small_pieces, axis=0),
-        jnp.concatenate([attention_gain_part.reshape(4, HEAD), row_stats[4:]], axis=0),
-        up_2,
+        by_y, by_z, out_piece, small_piece, late, up_2
     )
     small_total = small_total.reshape(384, HEAD)
     late = jnp.sum(late, axis=0)
-    grad_gate_up, grad_down, grad_qkv = pack_grads(
-        up_1, up_2, down_1, down_2, qkv_total.reshape(512, 1536)
+    grad_gate_up, grad_down, grad_qkv, grad_out = pack_grads(
+        up_1,
+        up_2,
+        down_1,
+        down_2,
+        qkv_total.reshape(512, 1536),
+        out_total.reshape(512, 512),
     )
     return (
         output,
-        token_grad.astype(BF),
+        token_grad,
         late[:4].reshape(512),
         small_total[256:260].reshape(512),
         grad_qkv,
         late[4],
         late[5],
-        out_total.astype(F32).reshape(512, 512),
+        grad_out,
         small_total[:256].reshape(EXPERTS, 512).T,
         grad_gate_up,
         grad_down,

time: 515 us -> 506 us (0.983)
  other arithmetic: 26.8 us -> 14.9 us
    reduce_sum x5 -> x0, other arithmetic: 5.68 us -> none  [the longest x1 2.02 us: shards(): out_piece = jnp.sum(out_pieces.astype(F32), axis=0).astype(BF)]
  transfers between devices with their start and end apart: 6 -> 6, of which waited for: 0 -> 0; matrix products, arithmetic and copies ran while one was open for 4% -> 4% of each run, Pallas kernels for 17% -> 18%
where the time goes in v5:
time: 506 us; the launch traced here: 498 us
  Pallas kernels  429 us (85%)
  matrix products  21.8 us (4%)
  starting transfers between devices  18.2 us (4%)
  other arithmetic  14.9 us (3%)
  local copies, waits for them, and re-layouts  12.4 us (2%)
    pallas_call x8, Pallas kernels, exchange(): pl.pallas_call(kernel, out_shape=list(outputs) + list(work_out), in_specs...  418 us
    ppermute x4, starting transfers between devices, shards(): sibling = lambda w: lax.ppermute(w, 'dp', PAIR)  12.9 us
    dot_general x4, matrix products, dot(): return jnp.dot(left, right, preferred_element_type=F32)  12.5 us
    pallas_call x1, Pallas kernels, pack_grads(): pl.pallas_call(pack_kernel, grid=(steps,), out_shape=[shape((2, WIDTH, 2,...  11.5 us
  transfers between devices with their start and end apart: 6, of which 0 were waited for; matrix products, arithmetic and copies ran while one was open for 4% of the time, Pallas kernels for 18%

profile of v5, /device:TPU:1, one launch (start us, length us, event | category | flops | bytes accessed | tf_op | source)
XLA Modules:
  0.0 497.7 jit_solution(9627469555139380959)
XLA Ops:
  2.4 2.8 copy.50
  5.2 54.5 %shard_map.212 = (bf16[512,2048]{1,0:T(8,128)(2,1)}, bf16[4,512,1536]{2,1,0:T(8,128)(2,1)}, s32[4,4,128]{2,1,0:T(4,128)}, f32[4,4,128]{2,1,0:T(4,128)}, bf16[4,4...) custom-call(bf16[512,512]{1,0:T(8,128)(2,1)} %refs_14_.1, ...), custom_call_target="tpu_custom_call" | custom-call | bytes 105000000 | tf_op jit(solution)/shard_map/pallas_call | solution.py:182
  59.7 3.0 collective-permute-start
  62.7 2.4 collective-permute-start.1
  65.1 2.1 fusion.5
  68.4 7.0 %convolution_convert_fusion.3.refs_0_ = bf16[512,1536]{1,0:T(8,128)(2,1)S(1)} fusion(bf16[512,2048]{1,0:T(8,128)(2,1)S(1)} %fusion.7.refs_2_, bf16[2048,1536]{1,0:T(8,128)(2,1)} %bitcast.71), kind=kOutput, calls=%fused_computation.18 | convolution fusion | flops 3222011904 | bytes 9961472 | tf_op jit(solution)/shard_map/dot_general | solution.py:1335
  75.4 21.9 %shard_map.213.refs_1_.refs_4_ = bf16[2048,384]{1,0:T(8,128)(2,1)S(1)} custom-call(bf16[512,1536]{1,0:T(8,128)(2,1)S(1)} %convolution_convert_fusion.3.refs_0_), custom_call_target="tpu_custom_call" | custom-call | bytes 105000000 | tf_op jit(solution)/shard_map/pallas_call | solution.py:182
  98.5 1.3 copy.41.refs_2_
  100.1 2.9 fusion.27
  104.8 65.9 %shard_map.214 = (bf16[16,40,2048]{2,1,0:T(8,128)(2,1)}, bf16[2048,128]{1,0:T(8,128)(2,1)}, bf16[2048,128]{1,0:T(8,128)(2,1)}, f32[2048,1]{1,0:T(8,128)}, f32[20...) custom-call(bf16[64,40,512]{2,1,0:T(8,128)(2,1)} %get-tuple-element.62.refs_0_, ...), custom_call_target="tpu_custom_call" | custom-call | bytes 105000000 | tf_op jit(solution)/shard_map/pallas_call | solution.py:182
  170.7 2.9 multiply_reduce_fusion.1
  174.5 11.9 %shard_map.215 = f32[4,72,512]{2,1,0:T(8,128)S(1)} custom-call(f32[72,512]{1,0:T(8,128)S(1)} %maximum_maximum_fusion.1.refs_0_), custom_call_target="tpu_custom_call" | custom-call | bytes 105000000 | tf_op jit(solution)/shard_map/pallas_call | solution.py:182
  187.9 11.5 %collective-permute-start.5 = (bf16[256,2048]{1,0:T(8,128)(2,1)}, bf16[256,2048]{1,0:T(8,128)(2,1)}, u32[]{:S(2)}, u32[]{:S(2)}) collective-permute-start(bf16[256,2048]{1,0:T(8,128)(2,1)} %get-tuple-element.77.refs_6_), channel_id=1, source_target_pairs={{0,16},{16,0},{32,48},{48,32},{64,80},{80,64},{96,112},{112,96},{1... | collective-permute-start | bytes 3145736 | tf_op jit(solution)/shard_map/ppermute | solution.py:1434
  200.5 1.6 convolution_convert_fusion
  202.1 1.7 pad_add_fusion.refs_0_
  203.9 104.6 %shard_map.216 = (bf16[64,40,512]{2,1,0:T(8,128)(2,1)}, bf16[64,40,512]{2,1,0:T(8,128)(2,1)}, bf16[16,40,2048]{2,1,0:T(8,128)(2,1)}, bf16[2048,512]{1,0:T(8,128)...) custom-call(bf16[64,40,512]{2,1,0:T(8,128)(2,1)} %pad_add_fusion.refs_0_, ...), custom_call_target="tpu_custom_call" | custom-call | bytes 105000000 | tf_op jit(solution)/shard_map/pallas_call | solution.py:182
  312.3 2.3 multiply_reduce_fusion
  314.6 2.6 convolution_convert_fusion.1.refs_3_
  317.2 2.6 convolution_convert_fusion.2
  320.7 55.3 %shard_map.217 = (bf16[16,64,512]{2,1,0:T(8,128)(2,1)}, f32[384,128]{1,0:T(8,128)}, bf16[2048,512]{1,0:T(8,128)(2,1)}, bf16[512,1536]{1,0:T(8,128)(2,1)}, f32[8,128]{1,0:T(8,128)}) custom-call(bf16[16,128,512]{2,1,0:T(8,128)(2,1)} %bitcast.69, f32[384,128]{1,0:T(8,128)} %maximum_maximum_fusion.refs_1_.refs_11_, bf16[2048,512]{1,0:T(8,128)(2,1)} %get-tuple-element.82.refs_2_, ...), custom_call_target="tpu_custom_call" | custom-call | bytes 105000000 | tf_op jit(solution)/shard_map/pallas_call | solution.py:182
  376.6 62.3 %shard_map.218 = (bf16[256,2048]{1,0:T(8,128)(2,1)}, bf16[256,2048]{1,0:T(8,128)(2,1)}, bf16[4,32,1536]{2,1,0:T(8,128)(2,1)}, bf16[4,128,384]{2,1,0:T(8,128)(2,1...) custom-call(bf16[256,2048]{1,0:T(8,128)(2,1)} %get-tuple-element.79., ...), custom_call_target="tpu_custom_call" | custom-call | bytes 105000000 | tf_op jit(solution)/shard_map/pallas_call | solution.py:182
  439.0 41.1 %shard_map.219 = (bf16[4,2,64,512]{3,2,1,0:T(8,128)(2,1)}, f32[16,24,128]{2,1,0:T(8,128)}, f32[32,8,128]{2,1,0:T(8,128)}, bf16[2048,512]{1,0:T(8,128)(2,1)}, bf16[2,2,4,32,1536]{4,3,2,1,0:T(8,128)(2,1)}) custom-call(bf16[64,512]{1,0:T(8,128)(2,1)} %get-tuple-element.95.refs_0_, f32[24,128]{1,0:T(8,128)} %get-tuple-element.96.refs_1_, ...), custom_call_target="tpu_custom_call" | custom-call | bytes 105000000 | tf_op jit(solution)/shard_map/pallas_call | solution.py:182
  482.0 1.3 slice_bitcast_fusion
  484.4 11.5 %shard_map.220 = (f32[2,2048,2,256]{3,2,1,0:T(2,128)}, f32[2,256,2048]{2,1,0:T(8,128)}, f32[512,4,384]{2,1,0:T(4,128)}, f32[512,512]{1,0:T(8,128)}) custom-call(bf16[2048,512]{1,0:T(8,128)(2,1)} %get-tuple-element.103.up_1, bf16[2048,512]{1,0:T(8,128)(2,1)} %get-tuple-element.104.up_2, bf16[256,2048]{1,0:T(8,128)(2,1)} %get-tuple-element.105.down_1, ...), custom_call_target="tpu_custom_call" | custom-call | tf_op jit(solution)/shard_map/pallas_call | solution.py:1312
  (101 shorter events, 19.3 us)
Async XLA Ops:
  0.6 173.0 %copy-start = (bf16[512,64]{0,1:T(8,128)(2,1)S(1)}, bf16[512,64]{0,1:T(8,128)(2,1)}, u32[]{:S(2)}) copy-start(bf16[512,64]{0,1:T(8,128)(2,1)} %param.22) | copy-start | bytes 196612
  59.7 7.5 %copy-start.4 = (bf16[512,2048]{1,0:T(8,128)(2,1)S(1)}, bf16[512,2048]{1,0:T(8,128)(2,1)}, u32[]{:S(2)}) copy-start(bf16[512,2048]{1,0:T(8,128)(2,1)} %get-tuple-element.63) | copy-start | bytes 6291460
  59.7 111.0 %collective-permute-start = (bf16[2048,512]{1,0:T(8,128)(2,1)}, bf16[2048,512]{1,0:T(8,128)(2,1)}, u32[]{:S(2)}, u32[]{:S(2)}) collective-permute-start(bf16[2048,512]{1,0:T(8,128)(2,1)} %get-tuple-element.68), channel_id=1, source_target_pairs={{0,16},{4,0},{8,20},{12,4},{16,24},{20,8},{24,28},{28,12},{32,48},... | collective-permute-start | bytes 6291464 | tf_op jit(solution)/shard_map/ppermute | solution.py:1380
  62.7 108.0 %collective-permute-start.1 = (bf16[2048,512]{1,0:T(8,128)(2,1)}, bf16[2048,512]{1,0:T(8,128)(2,1)}, u32[]{:S(2)}, u32[]{:S(2)}) collective-permute-start(bf16[2048,512]{1,0:T(8,128)(2,1)} %get-tuple-element.69), channel_id=1, source_target_pairs={{0,4},{4,20},{8,0},{12,16},{16,12},{20,28},{24,8},{28,24},{32,36},... | collective-permute-start | bytes 6291464 | tf_op jit(solution)/shard_map/ppermute | solution.py:1380
  68.4 7.0 %copy-start.5 = (bf16[512,2048]{1,0:T(8,128)(2,1)}, bf16[512,2048]{1,0:T(8,128)(2,1)S(1)}, u32[]{:S(2)}) copy-start(bf16[512,2048]{1,0:T(8,128)(2,1)S(1)} %fusion.7.refs_2_) | copy-start | bytes 6291460
  75.4 23.1 %copy-start.15 = (s32[4,4,128]{2,1,0:T(4,128)S(1)}, s32[4,4,128]{2,1,0:T(4,128)}, u32[]{:S(2)}) copy-start(s32[4,4,128]{2,1,0:T(4,128)} %get-tuple-element.66) | copy-start | bytes 24580
  75.4 24.7 %copy-start.6 = (f32[64,512]{1,0:T(8,128)S(1)}, f32[64,512]{1,0:T(8,128)}, u32[]{:S(2)}) copy-start(f32[64,512]{1,0:T(8,128)} %convolution_select_fusion.refs_7_) | copy-start | bytes 393220
  98.5 5.6 %copy-start.17 = (f32[128]{0:T(128)S(1)}, f32[128]{0:T(128)}, u32[]{:S(2)}) copy-start(f32[128]{0:T(128)} %param.20) | copy-start | bytes 1540
  98.5 5.6 %copy-start.18 = (f32[128]{0:T(128)S(1)}, f32[128]{0:T(128)}, u32[]{:S(2)}) copy-start(f32[128]{0:T(128)} %param.19) | copy-start | bytes 1540
  104.8 65.9 %copy-start.7 = (bf16[512,512]{1,0:T(8,128)(2,1)S(1)}, bf16[512,512]{1,0:T(8,128)(2,1)}, u32[]{:S(2)}) copy-start(bf16[512,512]{1,0:T(8,128)(2,1)} %refs_14_.1) | copy-start | bytes 1572868
  104.8 65.9 %copy-start.19 = (bf16[4,4,128,512]{3,2,1,0:T(8,128)(2,1)S(1)}, bf16[4,4,128,512]{3,2,1,0:T(8,128)(2,1)}, u32[]{:S(2)}) copy-start(bf16[4,4,128,512]{3,2,1,0:T(8,128)(2,1)} %get-tuple-element.73) | copy-start | bytes 6291460
  170.7 3.0 copy-start.13
  173.7 138.6 %copy-start.3 = (f32[512,512]{1,0:T(8,128)}, f32[512,512]{1,0:T(8,128)S(1)}, u32[]{:S(2)}) copy-start(f32[512,512]{1,0:T(8,128)S(1)} %get-tuple-element.132.refs_6_) | copy-start | bytes 3145732
  173.7 26.8 %copy-start.8 = (pred[2560,512]{1,0:T(32,128)(4,1)S(1)}, pred[2560,512]{1,0:T(32,128)(4,1)}, u32[]{:S(2)}) copy-start(pred[2560,512]{1,0:T(32,128)(4,1)} %get-tuple-element.124) | copy-start | bytes 3932164
  186.5 17.4 %collective-permute-start.2 = (bf16[2048,512]{1,0:T(8,128)(2,1)}, bf16[2048,512]{1,0:T(8,128)(2,1)}, u32[]{:S(2)}, u32[]{:S(2)}) collective-permute-start(bf16[2048,512]{1,0:T(8,128)(2,1)} %collective-permute-done.refs_1_), channel_id=1, source_target_pairs={{0,16},{16,0},{32,48},{48,32},{64,80},{80,64},{96,112},{112,96},{1... | collective-permute-start | bytes 6291464 | tf_op jit(solution)/shard_map/ppermute | solution.py:1434
  187.3 16.6 %collective-permute-start.3 = (bf16[2048,512]{1,0:T(8,128)(2,1)}, bf16[2048,512]{1,0:T(8,128)(2,1)}, u32[]{:S(2)}, u32[]{:S(2)}) collective-permute-start(bf16[2048,512]{1,0:T(8,128)(2,1)} %collective-permute-done.1.refs_2_), channel_id=1, source_target_pairs={{0,16},{16,0},{32,48},{48,32},{64,80},{80,64},{96,112},{112,96},{1... | collective-permute-start | bytes 6291464 | tf_op jit(solution)/shard_map/ppermute | solution.py:1434
  187.4 16.5 %collective-permute-start.4 = (bf16[256,2048]{1,0:T(8,128)(2,1)}, bf16[256,2048]{1,0:T(8,128)(2,1)}, u32[]{:S(2)}, u32[]{:S(2)}) collective-permute-start(bf16[256,2048]{1,0:T(8,128)(2,1)} %get-tuple-element.76.refs_5_), channel_id=1, source_target_pairs={{0,16},{16,0},{32,48},{48,32},{64,80},{80,64},{96,112},{112,96},{1... | collective-permute-start | bytes 3145736 | tf_op jit(solution)/shard_map/ppermute | solution.py:1434
  187.9 16.0 %collective-permute-start.5 = (bf16[256,2048]{1,0:T(8,128)(2,1)}, bf16[256,2048]{1,0:T(8,128)(2,1)}, u32[]{:S(2)}, u32[]{:S(2)}) collective-permute-start(bf16[256,2048]{1,0:T(8,128)(2,1)} %get-tuple-element.77.refs_6_), channel_id=1, source_target_pairs={{0,16},{16,0},{32,48},{48,32},{64,80},{80,64},{96,112},{112,96},{1... | collective-permute-start | bytes 3145736 | tf_op jit(solution)/shard_map/ppermute | solution.py:1434
  308.5 3.8 copy-start.10
  314.6 2.6 copy-start.9
  320.7 55.3 %copy-start.14 = (f32[512]{0:T(512)S(1)}, f32[512]{0:T(512)}, u32[]{:S(2)}) copy-start(f32[512]{0:T(512)} %param.16) | copy-start | bytes 6148
  484.4 11.5 %copy-start.12 = (bf16[512,512]{1,0:T(8,128)(2,1)S(1)}, bf16[512,512]{1,0:T(8,128)(2,1)}, u32[]{:S(2)}) copy-start(bf16[512,512]{1,0:T(8,128)(2,1)} %get-tuple-element.146) | copy-start | bytes 1572868
  484.4 12.3 %copy-start.11 = (bf16[512,512]{1,0:T(8,128)(2,1)S(1)}, bf16[512,512]{1,0:T(8,128)(2,1)}, u32[]{:S(2)}) copy-start(bf16[512,512]{1,0:T(8,128)(2,1)} %get-tuple-element.147) | copy-start | bytes 1572868
  484.4 13.1 %copy-start.1 = (bf16[512,64]{0,1:T(8,128)(2,1)S(1)}, bf16[512,64]{0,1:T(8,128)(2,1)}, u32[]{:S(2)}) copy-start(bf16[512,64]{0,1:T(8,128)(2,1)} %param.22) | copy-start | bytes 196612
  (4 other events, 8.5 us)

commit v6 on v5

--- a/solution.py
+++ b/solution.py
@@ -778,7 +778,7 @@
 
 def attend_kernel(
     links,
-    ready,
+    numbers,
     qkv_ref,
     position_ref,
     frequency_ref,
@@ -809,6 +809,7 @@
         return carry
 
     lax.fori_loop(0, SEQ // BLOCK, prepare, 0)
+    to_cols, beside, passed = numbers
     row, col = lax.axis_index("row"), lax.axis_index("col")
     for ahead in (1, 3, 2, 0):
         first = lax.rem(col + ahead, 4) * 512
@@ -832,17 +833,26 @@
             return carry
 
         lax.fori_loop(0, 512 // BLOCK, block, 0)
-        for number in ready[ahead]:
+        if ahead:
+            links.send(to_cols[ahead])
+    gathered[:, rows((row * 4 + col) * HEAD, HEAD)] = out_ref[rows(col * 512, 512), :]
+    for ahead in (0, 1, 3, 2):
+        if ahead:
+            links.arrive(to_cols[ahead])
+        for number in beside[ahead]:
             links.send(number)
-    gathered[:, rows((row * 4 + col) * HEAD, HEAD)] = out_ref[rows(col * 512, 512), :]
+    for ahead in (0, 1, 3, 2):
+        for number, onward in zip(beside[ahead], passed[ahead]):
+            links.arrive(number)
+            links.send(onward)
 
 
 def attend(qkv, position, frequency, gains, blocks):
     take, put = expert_views()
     sends = [(offset, 0, take, 0, put) for offset in CUBE]
-    ready = {ahead: [] for ahead in range(4)}
-    for offset in PLANE:
-        ready[offset[3]].append(len(sends))
+    to_cols, beside, passed = {}, {}, {}
+    for offset in COLS:
+        to_cols[offset[3]] = len(sends)
         sends.append(
             (
                 offset,
@@ -852,13 +862,27 @@
                 lambda o, me, p: o.at[:, rows((me[2] * 4 + me[3]) * HEAD, HEAD)],
             )
         )
+    sides = ((0, 0, 1, 0), (0, 0, 3, 0))
+    head_of = lambda row, me, ahead: rows((row * 4 + (me[3] + 4 - ahead) % 4) * HEAD, HEAD)
+    for ahead in range(4):
+        beside[ahead], passed[ahead] = [], []
+        for offset in sides:
+            view = lambda ref, me, p, ahead=ahead: ref.at[:, head_of(me[2], me, ahead)]
+            beside[ahead].append(len(sends))
+            sends.append((offset, ("made", 5), view, ("made", 5), view))
+        for index, offset in enumerate(sides):
+            view = lambda ref, me, p, ahead=ahead, index=index, d=offset[2]: ref.at[
+                pl.ds(index * 256, 256), head_of((me[2] + 4 - d) % 4, me, ahead)
+            ]
+            passed[ahead].append(len(sends))
+            sends.append((offset, ("made", 5), view, ("made", 5), view))
     return exchange(
         [blocks],
         [shape((16, ROOM, WIDTH))],
         sends,
         [(0, lambda s, me: take(s, me, me), 0, lambda o, me: put(o, me, me), (ROOM, 512))],
         6,
-        work=lambda links, *refs: attend_kernel(links, ready, *refs),
+        work=lambda links, *refs: attend_kernel(links, (to_cols, beside, passed), *refs),
         work_in=[qkv, position, frequency, gains],
         work_out=[
             shape((SEQ, HEAD)),

time: 506 us -> 495 us (0.978)
  Pallas kernels: 429 us -> 419 us
    pallas_call x8, Pallas kernels: 418 us -> 407 us  [exchange(): pl.pallas_call(kernel, out_shape=list(outputs) + list(work_out), in_specs...]
  transfers between devices with their start and end apart: 6 -> 6, of which waited for: 0 -> 0; matrix products, arithmetic and copies ran while one was open for 4% -> 4% of each run, Pallas kernels for 18% -> 17%
where the time goes in v6:
time: 495 us; the launch traced here: 488 us
  Pallas kernels  419 us (85%)
  matrix products  21.8 us (4%)
  starting transfers between devices  18.4 us (4%)
  other arithmetic  14.9 us (3%)
  local copies, waits for them, and re-layouts  12.4 us (3%)
    pallas_call x8, Pallas kernels, exchange(): pl.pallas_call(kernel, out_shape=list(outputs) + list(work_out), in_specs...  407 us
    ppermute x4, starting transfers between devices, shards(): sibling = lambda w: lax.ppermute(w, 'dp', PAIR)  13 us
    dot_general x4, matrix products, dot(): return jnp.dot(left, right, preferred_element_type=F32)  12.5 us
    pallas_call x1, Pallas kernels, pack_grads(): pl.pallas_call(pack_kernel, grid=(steps,), out_shape=[shape((2, WIDTH, 2,...  11.5 us
  transfers between devices with their start and end apart: 6, of which 0 were waited for; matrix products, arithmetic and copies ran while one was open for 4% of the time, Pallas kernels for 17%

profile of v6, /device:TPU:1, one launch (start us, length us, event | category | flops | bytes accessed | tf_op | source)
XLA Modules:
  0.0 487.7 jit_solution(1679094592505938866)
XLA Ops:
  2.4 2.8 copy.50
  5.2 54.5 %shard_map.212 = (bf16[512,2048]{1,0:T(8,128)(2,1)}, bf16[4,512,1536]{2,1,0:T(8,128)(2,1)}, s32[4,4,128]{2,1,0:T(4,128)}, f32[4,4,128]{2,1,0:T(4,128)}, bf16[4,4...) custom-call(bf16[512,512]{1,0:T(8,128)(2,1)} %refs_14_.1, ...), custom_call_target="tpu_custom_call" | custom-call | bytes 105000000 | tf_op jit(solution)/shard_map/pallas_call | solution.py:182
  59.7 3.0 collective-permute-start
  62.7 2.4 collective-permute-start.1
  65.1 2.1 fusion.5
  68.4 7.0 %convolution_convert_fusion.3.refs_0_ = bf16[512,1536]{1,0:T(8,128)(2,1)S(1)} fusion(bf16[512,2048]{1,0:T(8,128)(2,1)S(1)} %fusion.7.refs_2_, bf16[2048,1536]{1,0:T(8,128)(2,1)} %bitcast.71), kind=kOutput, calls=%fused_computation.18 | convolution fusion | flops 3222011904 | bytes 9961472 | tf_op jit(solution)/shard_map/dot_general | solution.py:1359
  75.4 21.9 %shard_map.213.refs_1_.refs_4_ = bf16[2048,384]{1,0:T(8,128)(2,1)S(1)} custom-call(bf16[512,1536]{1,0:T(8,128)(2,1)S(1)} %convolution_convert_fusion.3.refs_0_), custom_call_target="tpu_custom_call" | custom-call | bytes 105000000 | tf_op jit(solution)/shard_map/pallas_call | solution.py:182
  98.5 1.3 copy.41.refs_2_
  100.1 2.9 fusion.27
  104.8 60.7 %shard_map.214 = (bf16[16,40,2048]{2,1,0:T(8,128)(2,1)}, bf16[2048,128]{1,0:T(8,128)(2,1)}, bf16[2048,128]{1,0:T(8,128)(2,1)}, f32[2048,1]{1,0:T(8,128)}, f32[20...) custom-call(bf16[64,40,512]{2,1,0:T(8,128)(2,1)} %get-tuple-element.62.refs_0_, ...), custom_call_target="tpu_custom_call" | custom-call | bytes 105000000 | tf_op jit(solution)/shard_map/pallas_call | solution.py:182
  165.5 2.9 multiply_reduce_fusion.1
  169.3 10.0 %shard_map.215 = f32[4,72,512]{2,1,0:T(8,128)S(1)} custom-call(f32[72,512]{1,0:T(8,128)S(1)} %maximum_maximum_fusion.1.refs_0_), custom_call_target="tpu_custom_call" | custom-call | bytes 105000000 | tf_op jit(solution)/shard_map/pallas_call | solution.py:182
  180.9 11.5 %collective-permute-start.5 = (bf16[256,2048]{1,0:T(8,128)(2,1)}, bf16[256,2048]{1,0:T(8,128)(2,1)}, u32[]{:S(2)}, u32[]{:S(2)}) collective-permute-start(bf16[256,2048]{1,0:T(8,128)(2,1)} %get-tuple-element.77.refs_6_), channel_id=1, source_target_pairs={{0,16},{16,0},{32,48},{48,32},{64,80},{80,64},{96,112},{112,96},{1... | collective-permute-start | bytes 3145736 | tf_op jit(solution)/shard_map/ppermute | solution.py:1458
  193.5 1.6 convolution_convert_fusion
  195.1 1.7 pad_add_fusion.refs_0_
  196.8 102.3 %shard_map.216 = (bf16[64,40,512]{2,1,0:T(8,128)(2,1)}, bf16[64,40,512]{2,1,0:T(8,128)(2,1)}, bf16[16,40,2048]{2,1,0:T(8,128)(2,1)}, bf16[2048,512]{1,0:T(8,128)...) custom-call(bf16[64,40,512]{2,1,0:T(8,128)(2,1)} %pad_add_fusion.refs_0_, ...), custom_call_target="tpu_custom_call" | custom-call | bytes 105000000 | tf_op jit(solution)/shard_map/pallas_call | solution.py:182
  303.0 2.3 multiply_reduce_fusion
  305.3 2.6 convolution_convert_fusion.1.refs_3_
  307.9 2.6 convolution_convert_fusion.2
  311.3 55.7 %shard_map.217 = (bf16[16,64,512]{2,1,0:T(8,128)(2,1)}, f32[384,128]{1,0:T(8,128)}, bf16[2048,512]{1,0:T(8,128)(2,1)}, bf16[512,1536]{1,0:T(8,128)(2,1)}, f32[8,128]{1,0:T(8,128)}) custom-call(bf16[16,128,512]{2,1,0:T(8,128)(2,1)} %bitcast.69, f32[384,128]{1,0:T(8,128)} %maximum_maximum_fusion.refs_1_.refs_11_, bf16[2048,512]{1,0:T(8,128)(2,1)} %get-tuple-element.82.refs_2_, ...), custom_call_target="tpu_custom_call" | custom-call | bytes 105000000 | tf_op jit(solution)/shard_map/pallas_call | solution.py:182
  367.6 59.6 %shard_map.218 = (bf16[256,2048]{1,0:T(8,128)(2,1)}, bf16[256,2048]{1,0:T(8,128)(2,1)}, bf16[4,32,1536]{2,1,0:T(8,128)(2,1)}, bf16[4,128,384]{2,1,0:T(8,128)(2,1...) custom-call(bf16[256,2048]{1,0:T(8,128)(2,1)} %get-tuple-element.79., ...), custom_call_target="tpu_custom_call" | custom-call | bytes 105000000 | tf_op jit(solution)/shard_map/pallas_call | solution.py:182
  427.3 42.8 %shard_map.219 = (bf16[4,2,64,512]{3,2,1,0:T(8,128)(2,1)}, f32[16,24,128]{2,1,0:T(8,128)}, f32[32,8,128]{2,1,0:T(8,128)}, bf16[2048,512]{1,0:T(8,128)(2,1)}, bf16[2,2,4,32,1536]{4,3,2,1,0:T(8,128)(2,1)}) custom-call(bf16[64,512]{1,0:T(8,128)(2,1)} %get-tuple-element.95.refs_0_, f32[24,128]{1,0:T(8,128)} %get-tuple-element.96.refs_1_, ...), custom_call_target="tpu_custom_call" | custom-call | bytes 105000000 | tf_op jit(solution)/shard_map/pallas_call | solution.py:182
  472.0 1.3 slice_bitcast_fusion
  474.4 11.5 %shard_map.220 = (f32[2,2048,2,256]{3,2,1,0:T(2,128)}, f32[2,256,2048]{2,1,0:T(8,128)}, f32[512,4,384]{2,1,0:T(4,128)}, f32[512,512]{1,0:T(8,128)}) custom-call(bf16[2048,512]{1,0:T(8,128)(2,1)} %get-tuple-element.103.up_1, bf16[2048,512]{1,0:T(8,128)(2,1)} %get-tuple-element.104.up_2, bf16[256,2048]{1,0:T(8,128)(2,1)} %get-tuple-element.105.down_1, ...), custom_call_target="tpu_custom_call" | custom-call | tf_op jit(solution)/shard_map/pallas_call | solution.py:1336
  (101 shorter events, 19.4 us)
Async XLA Ops:
  0.6 167.8 %copy-start = (bf16[512,64]{0,1:T(8,128)(2,1)S(1)}, bf16[512,64]{0,1:T(8,128)(2,1)}, u32[]{:S(2)}) copy-start(bf16[512,64]{0,1:T(8,128)(2,1)} %param.22) | copy-start | bytes 196612
  59.7 7.5 %copy-start.4 = (bf16[512,2048]{1,0:T(8,128)(2,1)S(1)}, bf16[512,2048]{1,0:T(8,128)(2,1)}, u32[]{:S(2)}) copy-start(bf16[512,2048]{1,0:T(8,128)(2,1)} %get-tuple-element.63) | copy-start | bytes 6291460
  59.7 105.8 %collective-permute-start = (bf16[2048,512]{1,0:T(8,128)(2,1)}, bf16[2048,512]{1,0:T(8,128)(2,1)}, u32[]{:S(2)}, u32[]{:S(2)}) collective-permute-start(bf16[2048,512]{1,0:T(8,128)(2,1)} %get-tuple-element.68), channel_id=1, source_target_pairs={{0,16},{4,0},{8,20},{12,4},{16,24},{20,8},{24,28},{28,12},{32,48},... | collective-permute-start | bytes 6291464 | tf_op jit(solution)/shard_map/ppermute | solution.py:1404
  62.7 102.8 %collective-permute-start.1 = (bf16[2048,512]{1,0:T(8,128)(2,1)}, bf16[2048,512]{1,0:T(8,128)(2,1)}, u32[]{:S(2)}, u32[]{:S(2)}) collective-permute-start(bf16[2048,512]{1,0:T(8,128)(2,1)} %get-tuple-element.69), channel_id=1, source_target_pairs={{0,4},{4,20},{8,0},{12,16},{16,12},{20,28},{24,8},{28,24},{32,36},... | collective-permute-start | bytes 6291464 | tf_op jit(solution)/shard_map/ppermute | solution.py:1404
  68.4 7.0 %copy-start.5 = (bf16[512,2048]{1,0:T(8,128)(2,1)}, bf16[512,2048]{1,0:T(8,128)(2,1)S(1)}, u32[]{:S(2)}) copy-start(bf16[512,2048]{1,0:T(8,128)(2,1)S(1)} %fusion.7.refs_2_) | copy-start | bytes 6291460
  75.4 23.1 %copy-start.15 = (s32[4,4,128]{2,1,0:T(4,128)S(1)}, s32[4,4,128]{2,1,0:T(4,128)}, u32[]{:S(2)}) copy-start(s32[4,4,128]{2,1,0:T(4,128)} %get-tuple-element.66) | copy-start | bytes 24580
  75.4 24.7 %copy-start.6 = (f32[64,512]{1,0:T(8,128)S(1)}, f32[64,512]{1,0:T(8,128)}, u32[]{:S(2)}) copy-start(f32[64,512]{1,0:T(8,128)} %convolution_select_fusion.refs_7_) | copy-start | bytes 393220
  98.5 5.6 %copy-start.17 = (f32[128]{0:T(128)S(1)}, f32[128]{0:T(128)}, u32[]{:S(2)}) copy-start(f32[128]{0:T(128)} %param.20) | copy-start | bytes 1540
  98.5 5.6 %copy-start.18 = (f32[128]{0:T(128)S(1)}, f32[128]{0:T(128)}, u32[]{:S(2)}) copy-start(f32[128]{0:T(128)} %param.19) | copy-start | bytes 1540
  104.8 60.7 %copy-start.7 = (bf16[512,512]{1,0:T(8,128)(2,1)S(1)}, bf16[512,512]{1,0:T(8,128)(2,1)}, u32[]{:S(2)}) copy-start(bf16[512,512]{1,0:T(8,128)(2,1)} %refs_14_.1) | copy-start | bytes 1572868
  104.8 60.7 %copy-start.19 = (bf16[4,4,128,512]{3,2,1,0:T(8,128)(2,1)S(1)}, bf16[4,4,128,512]{3,2,1,0:T(8,128)(2,1)}, u32[]{:S(2)}) copy-start(bf16[4,4,128,512]{3,2,1,0:T(8,128)(2,1)} %get-tuple-element.73) | copy-start | bytes 6291460
  165.5 3.0 copy-start.13
  168.5 134.5 %copy-start.3 = (f32[512,512]{1,0:T(8,128)}, f32[512,512]{1,0:T(8,128)S(1)}, u32[]{:S(2)}) copy-start(f32[512,512]{1,0:T(8,128)S(1)} %get-tuple-element.132.refs_6_) | copy-start | bytes 3145732
  168.5 25.0 %copy-start.8 = (pred[2560,512]{1,0:T(32,128)(4,1)S(1)}, pred[2560,512]{1,0:T(32,128)(4,1)}, u32[]{:S(2)}) copy-start(pred[2560,512]{1,0:T(32,128)(4,1)} %get-tuple-element.124) | copy-start | bytes 3932164
  179.4 17.5 %collective-permute-start.2 = (bf16[2048,512]{1,0:T(8,128)(2,1)}, bf16[2048,512]{1,0:T(8,128)(2,1)}, u32[]{:S(2)}, u32[]{:S(2)}) collective-permute-start(bf16[2048,512]{1,0:T(8,128)(2,1)} %collective-permute-done.refs_1_), channel_id=1, source_target_pairs={{0,16},{16,0},{32,48},{48,32},{64,80},{80,64},{96,112},{112,96},{1... | collective-permute-start | bytes 6291464 | tf_op jit(solution)/shard_map/ppermute | solution.py:1458
  180.3 16.6 %collective-permute-start.3 = (bf16[2048,512]{1,0:T(8,128)(2,1)}, bf16[2048,512]{1,0:T(8,128)(2,1)}, u32[]{:S(2)}, u32[]{:S(2)}) collective-permute-start(bf16[2048,512]{1,0:T(8,128)(2,1)} %collective-permute-done.1.refs_2_), channel_id=1, source_target_pairs={{0,16},{16,0},{32,48},{48,32},{64,80},{80,64},{96,112},{112,96},{1... | collective-permute-start | bytes 6291464 | tf_op jit(solution)/shard_map/ppermute | solution.py:1458
  180.4 16.4 %collective-permute-start.4 = (bf16[256,2048]{1,0:T(8,128)(2,1)}, bf16[256,2048]{1,0:T(8,128)(2,1)}, u32[]{:S(2)}, u32[]{:S(2)}) collective-permute-start(bf16[256,2048]{1,0:T(8,128)(2,1)} %get-tuple-element.76.refs_5_), channel_id=1, source_target_pairs={{0,16},{16,0},{32,48},{48,32},{64,80},{80,64},{96,112},{112,96},{1... | collective-permute-start | bytes 3145736 | tf_op jit(solution)/shard_map/ppermute | solution.py:1458
  180.9 16.0 %collective-permute-start.5 = (bf16[256,2048]{1,0:T(8,128)(2,1)}, bf16[256,2048]{1,0:T(8,128)(2,1)}, u32[]{:S(2)}, u32[]{:S(2)}) collective-permute-start(bf16[256,2048]{1,0:T(8,128)(2,1)} %get-tuple-element.77.refs_6_), channel_id=1, source_target_pairs={{0,16},{16,0},{32,48},{48,32},{64,80},{80,64},{96,112},{112,96},{1... | collective-permute-start | bytes 3145736 | tf_op jit(solution)/shard_map/ppermute | solution.py:1458
  299.1 3.8 copy-start.10
  305.3 2.6 copy-start.9
  311.3 55.7 %copy-start.14 = (f32[512]{0:T(512)S(1)}, f32[512]{0:T(512)}, u32[]{:S(2)}) copy-start(f32[512]{0:T(512)} %param.16) | copy-start | bytes 6148
  474.4 11.5 %copy-start.12 = (bf16[512,512]{1,0:T(8,128)(2,1)S(1)}, bf16[512,512]{1,0:T(8,128)(2,1)}, u32[]{:S(2)}) copy-start(bf16[512,512]{1,0:T(8,128)(2,1)} %get-tuple-element.146) | copy-start | bytes 1572868
  474.4 12.3 %copy-start.11 = (bf16[512,512]{1,0:T(8,128)(2,1)S(1)}, bf16[512,512]{1,0:T(8,128)(2,1)}, u32[]{:S(2)}) copy-start(bf16[512,512]{1,0:T(8,128)(2,1)} %get-tuple-element.147) | copy-start | bytes 1572868
  474.4 13.1 %copy-start.1 = (bf16[512,64]{0,1:T(8,128)(2,1)S(1)}, bf16[512,64]{0,1:T(8,128)(2,1)}, u32[]{:S(2)}) copy-start(bf16[512,64]{0,1:T(8,128)(2,1)} %param.22) | copy-start | bytes 196612
  (4 other events, 8.5 us)

commit v7 on v6

--- a/solution.py
+++ b/solution.py
@@ -699,11 +699,11 @@
         lambda o, me, p: o.at[me[0], me[2]],
         ("work", 1),
     )
+    sends.add([OTHER_BACK], whole, 3, whole, 3)
     out_sent = sends.add(LINES, whole, 0, put_out, 0)
     sends.add([SIBLING], whole, 0, put_out, 0)
     sends.add(SOURCES, whole, 1, put_small, 1)
     sends.add(OTHERS, whole, 2, put_late, 2)
-    sends.add([OTHER_BACK], whole, 3, whole, 3)
     later = len(sends)
     qkv_sent = sends.add(LINES, whole, ("made", 0), put_qkv, ("scratch", 2))
     sends.add([SIBLING], whole, ("made", 0), put_qkv, ("scratch", 2))

time: 495 us -> 495 us (level)
  no operation moved by 1% of the time
where the time goes in v7:
time: 495 us; the launch traced here: 488 us
  Pallas kernels  419 us (85%)
  matrix products  21.8 us (4%)
  starting transfers between devices  18.4 us (4%)
  other arithmetic  14.9 us (3%)
  local copies, waits for them, and re-layouts  12.4 us (3%)
    pallas_call x8, Pallas kernels, exchange(): pl.pallas_call(kernel, out_shape=list(outputs) + list(work_out), in_specs...  408 us
    ppermute x4, starting transfers between devices, shards(): sibling = lambda w: lax.ppermute(w, 'dp', PAIR)  13 us
    dot_general x4, matrix products, dot(): return jnp.dot(left, right, preferred_element_type=F32)  12.5 us
    pallas_call x1, Pallas kernels, pack_grads(): pl.pallas_call(pack_kernel, grid=(steps,), out_shape=[shape((2, WIDTH, 2,...  11.5 us
  transfers between devices with their start and end apart: 6, of which 0 were waited for; matrix products, arithmetic and copies ran while one was open for 4% of the time, Pallas kernels for 17%

profile of v7, /device:TPU:1, one launch (start us, length us, event | category | flops | bytes accessed | tf_op | source)
XLA Modules:
  0.0 487.7 jit_solution(7349820367914169169)
XLA Ops:
  2.4 2.8 copy.50
  5.2 54.5 %shard_map.212 = (bf16[512,2048]{1,0:T(8,128)(2,1)}, bf16[4,512,1536]{2,1,0:T(8,128)(2,1)}, s32[4,4,128]{2,1,0:T(4,128)}, f32[4,4,128]{2,1,0:T(4,128)}, bf16[4,4...) custom-call(bf16[512,512]{1,0:T(8,128)(2,1)} %refs_14_.1, ...), custom_call_target="tpu_custom_call" | custom-call | bytes 105000000 | tf_op jit(solution)/shard_map/pallas_call | solution.py:182
  59.7 3.0 collective-permute-start
  62.7 2.4 collective-permute-start.1
  65.1 2.1 fusion.5
  68.4 7.0 %convolution_convert_fusion.3.refs_0_ = bf16[512,1536]{1,0:T(8,128)(2,1)S(1)} fusion(bf16[512,2048]{1,0:T(8,128)(2,1)S(1)} %fusion.7.refs_2_, bf16[2048,1536]{1,0:T(8,128)(2,1)} %bitcast.71), kind=kOutput, calls=%fused_computation.18 | convolution fusion | flops 3222011904 | bytes 9961472 | tf_op jit(solution)/shard_map/dot_general | solution.py:1359
  75.4 21.9 %shard_map.213.refs_1_.refs_4_ = bf16[2048,384]{1,0:T(8,128)(2,1)S(1)} custom-call(bf16[512,1536]{1,0:T(8,128)(2,1)S(1)} %convolution_convert_fusion.3.refs_0_), custom_call_target="tpu_custom_call" | custom-call | bytes 105000000 | tf_op jit(solution)/shard_map/pallas_call | solution.py:182
  98.5 1.3 copy.41.refs_2_
  100.1 2.9 fusion.27
  104.8 60.7 %shard_map.214 = (bf16[16,40,2048]{2,1,0:T(8,128)(2,1)}, bf16[2048,128]{1,0:T(8,128)(2,1)}, bf16[2048,128]{1,0:T(8,128)(2,1)}, f32[2048,1]{1,0:T(8,128)}, f32[20...) custom-call(bf16[64,40,512]{2,1,0:T(8,128)(2,1)} %get-tuple-element.62.refs_0_, ...), custom_call_target="tpu_custom_call" | custom-call | bytes 105000000 | tf_op jit(solution)/shard_map/pallas_call | solution.py:182
  165.5 2.9 multiply_reduce_fusion.1
  169.3 10.0 %shard_map.215 = f32[4,72,512]{2,1,0:T(8,128)S(1)} custom-call(f32[72,512]{1,0:T(8,128)S(1)} %maximum_maximum_fusion.1.refs_0_), custom_call_target="tpu_custom_call" | custom-call | bytes 105000000 | tf_op jit(solution)/shard_map/pallas_call | solution.py:182
  180.9 11.5 %collective-permute-start.5 = (bf16[256,2048]{1,0:T(8,128)(2,1)}, bf16[256,2048]{1,0:T(8,128)(2,1)}, u32[]{:S(2)}, u32[]{:S(2)}) collective-permute-start(bf16[256,2048]{1,0:T(8,128)(2,1)} %get-tuple-element.77.refs_6_), channel_id=1, source_target_pairs={{0,16},{16,0},{32,48},{48,32},{64,80},{80,64},{96,112},{112,96},{1... | collective-permute-start | bytes 3145736 | tf_op jit(solution)/shard_map/ppermute | solution.py:1458
  193.5 1.6 convolution_convert_fusion
  195.1 1.7 pad_add_fusion.refs_0_
  196.8 102.3 %shard_map.216 = (bf16[64,40,512]{2,1,0:T(8,128)(2,1)}, bf16[64,40,512]{2,1,0:T(8,128)(2,1)}, bf16[16,40,2048]{2,1,0:T(8,128)(2,1)}, bf16[2048,512]{1,0:T(8,128)...) custom-call(bf16[64,40,512]{2,1,0:T(8,128)(2,1)} %pad_add_fusion.refs_0_, ...), custom_call_target="tpu_custom_call" | custom-call | bytes 105000000 | tf_op jit(solution)/shard_map/pallas_call | solution.py:182
  303.0 2.3 multiply_reduce_fusion
  305.3 2.6 convolution_convert_fusion.1.refs_3_
  307.9 2.6 convolution_convert_fusion.2
  311.3 55.7 %shard_map.217 = (bf16[16,64,512]{2,1,0:T(8,128)(2,1)}, f32[384,128]{1,0:T(8,128)}, bf16[2048,512]{1,0:T(8,128)(2,1)}, bf16[512,1536]{1,0:T(8,128)(2,1)}, f32[8,128]{1,0:T(8,128)}) custom-call(bf16[16,128,512]{2,1,0:T(8,128)(2,1)} %bitcast.69, f32[384,128]{1,0:T(8,128)} %maximum_maximum_fusion.refs_1_.refs_11_, bf16[2048,512]{1,0:T(8,128)(2,1)} %get-tuple-element.82.refs_2_, ...), custom_call_target="tpu_custom_call" | custom-call | bytes 105000000 | tf_op jit(solution)/shard_map/pallas_call | solution.py:182
  367.6 59.6 %shard_map.218 = (bf16[256,2048]{1,0:T(8,128)(2,1)}, bf16[256,2048]{1,0:T(8,128)(2,1)}, bf16[4,32,1536]{2,1,0:T(8,128)(2,1)}, bf16[4,128,384]{2,1,0:T(8,128)(2,1...) custom-call(bf16[256,2048]{1,0:T(8,128)(2,1)} %get-tuple-element.79., ...), custom_call_target="tpu_custom_call" | custom-call | bytes 105000000 | tf_op jit(solution)/shard_map/pallas_call | solution.py:182
  427.3 42.9 %shard_map.219 = (bf16[4,2,64,512]{3,2,1,0:T(8,128)(2,1)}, f32[16,24,128]{2,1,0:T(8,128)}, f32[32,8,128]{2,1,0:T(8,128)}, bf16[2048,512]{1,0:T(8,128)(2,1)}, bf16[2,2,4,32,1536]{4,3,2,1,0:T(8,128)(2,1)}) custom-call(bf16[64,512]{1,0:T(8,128)(2,1)} %get-tuple-element.95.refs_0_, f32[24,128]{1,0:T(8,128)} %get-tuple-element.96.refs_1_, ...), custom_call_target="tpu_custom_call" | custom-call | bytes 105000000 | tf_op jit(solution)/shard_map/pallas_call | solution.py:182
  472.0 1.3 slice_bitcast_fusion
  474.5 11.5 %shard_map.220 = (f32[2,2048,2,256]{3,2,1,0:T(2,128)}, f32[2,256,2048]{2,1,0:T(8,128)}, f32[512,4,384]{2,1,0:T(4,128)}, f32[512,512]{1,0:T(8,128)}) custom-call(bf16[2048,512]{1,0:T(8,128)(2,1)} %get-tuple-element.103.up_1, bf16[2048,512]{1,0:T(8,128)(2,1)} %get-tuple-element.104.up_2, bf16[256,2048]{1,0:T(8,128)(2,1)} %get-tuple-element.105.down_1, ...), custom_call_target="tpu_custom_call" | custom-call | tf_op jit(solution)/shard_map/pallas_call | solution.py:1336
  (101 shorter events, 19.4 us)
Async XLA Ops:
  0.6 167.8 %copy-start = (bf16[512,64]{0,1:T(8,128)(2,1)S(1)}, bf16[512,64]{0,1:T(8,128)(2,1)}, u32[]{:S(2)}) copy-start(bf16[512,64]{0,1:T(8,128)(2,1)} %param.22) | copy-start | bytes 196612
  59.7 7.5 %copy-start.4 = (bf16[512,2048]{1,0:T(8,128)(2,1)S(1)}, bf16[512,2048]{1,0:T(8,128)(2,1)}, u32[]{:S(2)}) copy-start(bf16[512,2048]{1,0:T(8,128)(2,1)} %get-tuple-element.63) | copy-start | bytes 6291460
  59.7 105.8 %collective-permute-start = (bf16[2048,512]{1,0:T(8,128)(2,1)}, bf16[2048,512]{1,0:T(8,128)(2,1)}, u32[]{:S(2)}, u32[]{:S(2)}) collective-permute-start(bf16[2048,512]{1,0:T(8,128)(2,1)} %get-tuple-element.68), channel_id=1, source_target_pairs={{0,16},{4,0},{8,20},{12,4},{16,24},{20,8},{24,28},{28,12},{32,48},... | collective-permute-start | bytes 6291464 | tf_op jit(solution)/shard_map/ppermute | solution.py:1404
  62.7 102.8 %collective-permute-start.1 = (bf16[2048,512]{1,0:T(8,128)(2,1)}, bf16[2048,512]{1,0:T(8,128)(2,1)}, u32[]{:S(2)}, u32[]{:S(2)}) collective-permute-start(bf16[2048,512]{1,0:T(8,128)(2,1)} %get-tuple-element.69), channel_id=1, source_target_pairs={{0,4},{4,20},{8,0},{12,16},{16,12},{20,28},{24,8},{28,24},{32,36},... | collective-permute-start | bytes 6291464 | tf_op jit(solution)/shard_map/ppermute | solution.py:1404
  68.4 7.0 %copy-start.5 = (bf16[512,2048]{1,0:T(8,128)(2,1)}, bf16[512,2048]{1,0:T(8,128)(2,1)S(1)}, u32[]{:S(2)}) copy-start(bf16[512,2048]{1,0:T(8,128)(2,1)S(1)} %fusion.7.refs_2_) | copy-start | bytes 6291460
  75.4 23.1 %copy-start.15 = (s32[4,4,128]{2,1,0:T(4,128)S(1)}, s32[4,4,128]{2,1,0:T(4,128)}, u32[]{:S(2)}) copy-start(s32[4,4,128]{2,1,0:T(4,128)} %get-tuple-element.66) | copy-start | bytes 24580
  75.4 24.7 %copy-start.6 = (f32[64,512]{1,0:T(8,128)S(1)}, f32[64,512]{1,0:T(8,128)}, u32[]{:S(2)}) copy-start(f32[64,512]{1,0:T(8,128)} %convolution_select_fusion.refs_7_) | copy-start | bytes 393220
  98.5 5.6 %copy-start.17 = (f32[128]{0:T(128)S(1)}, f32[128]{0:T(128)}, u32[]{:S(2)}) copy-start(f32[128]{0:T(128)} %param.20) | copy-start | bytes 1540
  98.5 5.6 %copy-start.18 = (f32[128]{0:T(128)S(1)}, f32[128]{0:T(128)}, u32[]{:S(2)}) copy-start(f32[128]{0:T(128)} %param.19) | copy-start | bytes 1540
  104.8 60.7 %copy-start.7 = (bf16[512,512]{1,0:T(8,128)(2,1)S(1)}, bf16[512,512]{1,0:T(8,128)(2,1)}, u32[]{:S(2)}) copy-start(bf16[512,512]{1,0:T(8,128)(2,1)} %refs_14_.1) | copy-start | bytes 1572868
  104.8 60.7 %copy-start.19 = (bf16[4,4,128,512]{3,2,1,0:T(8,128)(2,1)S(1)}, bf16[4,4,128,512]{3,2,1,0:T(8,128)(2,1)}, u32[]{:S(2)}) copy-start(bf16[4,4,128,512]{3,2,1,0:T(8,128)(2,1)} %get-tuple-element.73) | copy-start | bytes 6291460
  165.5 3.0 copy-start.13
  168.5 134.5 %copy-start.3 = (f32[512,512]{1,0:T(8,128)}, f32[512,512]{1,0:T(8,128)S(1)}, u32[]{:S(2)}) copy-start(f32[512,512]{1,0:T(8,128)S(1)} %get-tuple-element.132.refs_6_) | copy-start | bytes 3145732
  168.5 25.0 %copy-start.8 = (pred[2560,512]{1,0:T(32,128)(4,1)S(1)}, pred[2560,512]{1,0:T(32,128)(4,1)}, u32[]{:S(2)}) copy-start(pred[2560,512]{1,0:T(32,128)(4,1)} %get-tuple-element.124) | copy-start | bytes 3932164
  179.4 17.5 %collective-permute-start.2 = (bf16[2048,512]{1,0:T(8,128)(2,1)}, bf16[2048,512]{1,0:T(8,128)(2,1)}, u32[]{:S(2)}, u32[]{:S(2)}) collective-permute-start(bf16[2048,512]{1,0:T(8,128)(2,1)} %collective-permute-done.refs_1_), channel_id=1, source_target_pairs={{0,16},{16,0},{32,48},{48,32},{64,80},{80,64},{96,112},{112,96},{1... | collective-permute-start | bytes 6291464 | tf_op jit(solution)/shard_map/ppermute | solution.py:1458
  180.3 16.6 %collective-permute-start.3 = (bf16[2048,512]{1,0:T(8,128)(2,1)}, bf16[2048,512]{1,0:T(8,128)(2,1)}, u32[]{:S(2)}, u32[]{:S(2)}) collective-permute-start(bf16[2048,512]{1,0:T(8,128)(2,1)} %collective-permute-done.1.refs_2_), channel_id=1, source_target_pairs={{0,16},{16,0},{32,48},{48,32},{64,80},{80,64},{96,112},{112,96},{1... | collective-permute-start | bytes 6291464 | tf_op jit(solution)/shard_map/ppermute | solution.py:1458
  180.4 16.4 %collective-permute-start.4 = (bf16[256,2048]{1,0:T(8,128)(2,1)}, bf16[256,2048]{1,0:T(8,128)(2,1)}, u32[]{:S(2)}, u32[]{:S(2)}) collective-permute-start(bf16[256,2048]{1,0:T(8,128)(2,1)} %get-tuple-element.76.refs_5_), channel_id=1, source_target_pairs={{0,16},{16,0},{32,48},{48,32},{64,80},{80,64},{96,112},{112,96},{1... | collective-permute-start | bytes 3145736 | tf_op jit(solution)/shard_map/ppermute | solution.py:1458
  180.9 16.0 %collective-permute-start.5 = (bf16[256,2048]{1,0:T(8,128)(2,1)}, bf16[256,2048]{1,0:T(8,128)(2,1)}, u32[]{:S(2)}, u32[]{:S(2)}) collective-permute-start(bf16[256,2048]{1,0:T(8,128)(2,1)} %get-tuple-element.77.refs_6_), channel_id=1, source_target_pairs={{0,16},{16,0},{32,48},{48,32},{64,80},{80,64},{96,112},{112,96},{1... | collective-permute-start | bytes 3145736 | tf_op jit(solution)/shard_map/ppermute | solution.py:1458
  299.1 3.8 copy-start.10
  305.3 2.6 copy-start.9
  311.3 55.7 %copy-start.14 = (f32[512]{0:T(512)S(1)}, f32[512]{0:T(512)}, u32[]{:S(2)}) copy-start(f32[512]{0:T(512)} %param.16) | copy-start | bytes 6148
  474.5 11.5 %copy-start.12 = (bf16[512,512]{1,0:T(8,128)(2,1)S(1)}, bf16[512,512]{1,0:T(8,128)(2,1)}, u32[]{:S(2)}) copy-start(bf16[512,512]{1,0:T(8,128)(2,1)} %get-tuple-element.146) | copy-start | bytes 1572868
  474.5 12.3 %copy-start.11 = (bf16[512,512]{1,0:T(8,128)(2,1)S(1)}, bf16[512,512]{1,0:T(8,128)(2,1)}, u32[]{:S(2)}) copy-start(bf16[512,512]{1,0:T(8,128)(2,1)} %get-tuple-element.147) | copy-start | bytes 1572868
  474.5 13.1 %copy-start.1 = (bf16[512,64]{0,1:T(8,128)(2,1)S(1)}, bf16[512,64]{0,1:T(8,128)(2,1)}, u32[]{:S(2)}) copy-start(bf16[512,64]{0,1:T(8,128)(2,1)} %param.22) | copy-start | bytes 196612
  (4 other events, 8.5 us)
